TPU v7x, 512 devices: a whole 4x4x16 slice. The times are simulated.
512 devices in a mesh: pool: 128 (over x, z, core), tp: 4 (over y).
Axes of the slice: x: 4, y: 4, z: 16, core: 2. Of those that a mesh axis runs over, the one named last changes fastest.
Arguments:
- queries: bfloat16 [1024, 16, 8192], P('pool', None, 'tp'), may hold values from -96 to 96
- self_key: bfloat16 [1024, 16, 1024], P('pool', None, 'tp'), may hold values from -4 to 4
- self_value: bfloat16 [1024, 16, 1024], P('pool', None, 'tp'), may hold values from -6 to 6
- passage_key: bfloat16 [512, 16, 1024], P('pool', None, 'tp'), may hold values from -6 to 6
- passage_value: bfloat16 [512, 16, 1024], P('pool', None, 'tp'), may hold values from -6 to 6
- out_grad: bfloat16 [1024, 16, 8192], P('pool', None, 'tp'), may hold values from -6 to 6
- block_ids: int32 [1024, 16], P('pool'), may hold values from 0 to 511, as said below
- block_valid: int32 [1024, 16], P('pool'), may hold values 0 or 1
- passage_slot: int32 [512], P(('pool', 'tp')), may hold values from 0 to 511, as said below
Outputs:
- query_grad: bfloat16 [1024, 16, 8192], P('pool', None, 'tp')
- self_key_grad: bfloat16 [1024, 16, 1024], P('pool', None, 'tp')
- self_value_grad: bfloat16 [1024, 16, 1024], P('pool', None, 'tp')
- passage_key_grad: bfloat16 [512, 16, 1024], P('pool', None, 'tp')
- passage_value_grad: bfloat16 [512, 16, 1024], P('pool', None, 'tp')
Inputs may be any that keep to these rules, and one draw needn't show every extreme that they name: passage_slot is a permutation; the slots of one owner are the 4 consecutive ones that the pool index holds. `block_ids`: of the 128 entries of one pool index's lists, at most 2 name passages whose slots lie on one owner, and exactly 2 do for some owner.
All inputs are finite; a program needn't handle non-finite values. No bound on the sum of `block_valid` on one device may be relied on, other than what follows from the above.
Results may differ from a plain program's by a relative error of at most 0.04.
Values may be sent and summed in bfloat16 or wider, within the bound.
No kernel may reach another device: no remote copies, remote signals or barrier semaphores. Data moves between devices by JAX's collectives and lax.ppermute only.
A program may use at most 128 MiB of HBM per device.

v0:
```python
import jax
import jax.numpy as jnp
from jax import lax
from jax.sharding import PartitionSpec as P

HD = 128


def backward(q, keys, values, dout, allowed):
    qlen = q.shape[0]
    span = keys.shape[0]
    kvh = keys.shape[1] // HD
    group = q.shape[1] // (kvh * HD)
    scale = HD ** (-0.5)
    qg = q.reshape(qlen, kvh, group, HD)
    kg = keys.reshape(span, kvh, HD)
    vg = values.reshape(span, kvh, HD)
    dg = dout.reshape(qlen, kvh, group, HD)
    scores = jnp.einsum("lkgd,skd->kgls", qg, kg, preferred_element_type=jnp.float32) * scale
    scores = jnp.where(allowed, scores, -1e30)
    top = jnp.max(scores, axis=-1, keepdims=True)
    weights = jnp.where(allowed, jnp.exp(scores - top), 0.0)
    probs = weights / jnp.sum(weights, axis=-1, keepdims=True)
    probs_low = probs.astype(jnp.bfloat16)
    out_low = jnp.einsum(
        "kgls,skd->lkgd", probs_low, vg, preferred_element_type=jnp.float32
    ).astype(jnp.bfloat16)
    delta = jnp.einsum("lkgd,lkgd->kgl", dg, out_low, preferred_element_type=jnp.float32)
    dprob = jnp.einsum("lkgd,skd->kgls", dg, vg, preferred_element_type=jnp.float32)
    dscore = (probs * (dprob - delta[..., None])).astype(jnp.bfloat16)
    query_grad = (
        (jnp.einsum("kgls,skd->lkgd", dscore, kg, preferred_element_type=jnp.float32) * scale)
        .astype(jnp.bfloat16)
        .reshape(qlen, -1)
    )
    key_part = (
        jnp.einsum("kgls,lkgd->skd", dscore, qg, preferred_element_type=jnp.float32) * scale
    ).reshape(span, -1)
    value_part = jnp.einsum(
        "kgls,lkgd->skd", probs_low, dg, preferred_element_type=jnp.float32
    ).reshape(span, -1)
    return (query_grad, key_part, value_part)


def per_device(
    queries,
    self_key,
    self_value,
    passage_key,
    passage_value,
    out_grad,
    block_ids,
    block_valid,
    passage_slot,
):
    npool = lax.axis_size("pool")
    pdev, plen, feat = passage_key.shape
    qpd, qlen = (queries.shape[0], queries.shape[1])
    nblock = block_ids.shape[1]
    count = qpd * nblock
    width = nblock * plen
    slot_map = lax.all_gather(passage_slot, ("pool", "tp"), axis=0, tiled=True)
    every = jnp.arange(slot_map.shape[0], dtype=jnp.int32)
    flat_ids = block_ids.reshape(count)
    slots = jnp.sum(jnp.where(flat_ids[:, None] == every[None, :], slot_map[None, :], 0), axis=1)
    capacity = max(2, 2 * count // npool)
    owner = slots // pdev
    local = slots % pdev
    order = jnp.arange(count, dtype=jnp.int32)
    rank = jnp.sum((owner[:, None] == owner[None, :]) & (order[:, None] > order[None, :]), axis=1)
    target = owner * capacity + rank
    positions = jnp.arange(npool * capacity, dtype=jnp.int32)
    send_local = jnp.sum(
        jnp.where(target[:, None] == positions[None, :], local[:, None] + 1, 0), axis=0
    )
    wanted = lax.all_to_all(send_local, "pool", split_axis=0, concat_axis=0, tiled=True) - 1
    stored = jnp.stack([passage_key, passage_value], axis=1)
    reply = jnp.take(stored, jnp.maximum(wanted, 0), axis=0)
    arrived = lax.all_to_all(reply, "pool", split_axis=0, concat_axis=0, tiled=True)
    fetched = jnp.take(arrived, target, axis=0)
    fetched = fetched.reshape(qpd, nblock, 2, plen, feat)
    causal = jnp.arange(qlen)[None, :] <= jnp.arange(qlen)[:, None]

    def one_query(item):
        q, own_key, own_value, dout, blocks, valid = item
        keys = jnp.concatenate([blocks[:, 0].reshape(width, feat), own_key], axis=0)
        values = jnp.concatenate([blocks[:, 1].reshape(width, feat), own_value], axis=0)
        passage_ok = jnp.broadcast_to((valid > 0)[:, None], (nblock, plen)).reshape(1, width)
        allowed = jnp.concatenate([jnp.broadcast_to(passage_ok, (qlen, width)), causal], axis=1)
        query_grad, key_part, value_part = backward(q, keys, values, dout, allowed)
        partial_value = jnp.stack(
            [
                key_part[:width].reshape(nblock, plen, feat),
                value_part[:width].reshape(nblock, plen, feat),
            ],
            axis=1,
        ).astype(jnp.bfloat16)
        return (
            query_grad,
            key_part[width:].astype(jnp.bfloat16),
            value_part[width:].astype(jnp.bfloat16),
            partial_value,
        )

    query_grad, self_key_grad, self_value_grad, partial_value = lax.map(
        one_query, (queries, self_key, self_value, out_grad, fetched, block_valid)
    )
    partial_value = partial_value.reshape(count, 2 * plen * feat)
    owned = jnp.arange(pdev, dtype=jnp.int32)
    outgoing = (
        jnp.zeros((npool * capacity, 2 * plen * feat), jnp.bfloat16).at[target].set(partial_value)
    )
    returned = lax.all_to_all(outgoing, "pool", split_axis=0, concat_axis=0, tiled=True)
    picks = (wanted[None, :] == owned[:, None]).astype(jnp.bfloat16)
    summed = jnp.dot(picks, returned, preferred_element_type=jnp.float32)
    summed = summed.reshape(pdev, 2, plen, feat).astype(jnp.bfloat16)
    return (query_grad, self_key_grad, self_value_grad, summed[:, 0], summed[:, 1])


def solution(mesh):
    placed = (
        P("pool", None, "tp"),
        P("pool", None, "tp"),
        P("pool", None, "tp"),
        P("pool", None, "tp"),
        P("pool", None, "tp"),
        P("pool", None, "tp"),
        P("pool", None),
        P("pool", None),
        P(("pool", "tp")),
    )
    return jax.shard_map(
        per_device,
        mesh=mesh,
        in_specs=placed,
        out_specs=(
            P("pool", None, "tp"),
            P("pool", None, "tp"),
            P("pool", None, "tp"),
            P("pool", None, "tp"),
            P("pool", None, "tp"),
        ),
        check_vma=False,
    )
```

profile of v0, /device:TPU:1, one launch (start us, length us, event | category | flops | bytes accessed | tf_op | source)
XLA Modules:
  0.0 642.2 jit_solution(18174596237309663180)
XLA Ops:
  1.4 111.0 %all-reduce = s32[512]{0:T(512)S(1)} all-reduce(s32[512]{0:T(512)S(1)} %dynamic-update-slice), channel_id=1, replica_groups=mesh['pool'=128,'tp'=4] {'pool','tp'}, use_global_device_ids=true, to_apply=%add | all-reduce | flops 512 | bytes 4096
  114.5 10.3 %all-to-all-start = ((s32[128,2,1]{1,2,0:T(1,128)}), s32[128,2,1]{1,2,0:T(1,128)S(1)}, u32[]{:S(2)}, u32[]{:S(2)}) async-start(s32[128,2,1]{1,2,0:T(1,128)} %bitcast.2), calls=%async_computation | async-start | bytes 131072 | tf_op jit(solution)/shard_map/all_to_all | solution.py:76
  125.5 14.2 %all-to-all-done = s32[128,2,1]{1,2,0:T(1,128)S(1)} async-done(((s32[128,2,1]{1,2,0:T(1,128)}), s32[128,2,1]{1,2,0:T(1,128)S(1)}, u32[]{:S(2)}, u32[]{:S(2)}) %all-to-all-start) | async-done | bytes 1056 | tf_op jit(solution)/shard_map/all_to_all | solution.py:76
  140.4 2.8 gather_fusion
  143.2 4.0 broadcast_select_fusion
  147.3 7.7 %all-to-all-start.1 = ((bf16[256,2,16,256]{3,2,1,0:T(8,128)(2,1)}), bf16[256,2,16,256]{3,2,1,0:T(8,128)(2,1)}, u32[]{:S(2)}, u32[]{:S(2)}) async-start(bf16[256,2,16,256]{3,2,1,0:T(8,128)(2,1)} %broadcast_select_fusion), calls=%async_computation.1 | async-start | bytes 8388608 | tf_op jit(solution)/shard_map/all_to_all | solution.py:79
  155.2 185.2 %all-to-all-done.1 = bf16[256,2,16,256]{3,2,1,0:T(8,128)(2,1)} async-done(((bf16[256,2,16,256]{3,2,1,0:T(8,128)(2,1)}), bf16[256,2,16,256]{3,2,1,0:T(8,128)(2,1)}, u32[]{:S(2)}, u32[]{:S(2)}) %all-to-all-start.1) | async-done | bytes 4194336 | tf_op jit(solution)/shard_map/all_to_all | solution.py:79
  340.3 2.9 gather_fusion.1
  343.2 1.6 broadcast_select_fusion.1
  344.8 64.6 %while.17 = (s32[]{:T(128)}, bf16[8,16,2048]{2,1,0:T(8,128)(2,1)S(1)}, bf16[8,16,256]{2,1,0:T(8,128)(2,1)}, bf16[8,16,256]{2,1,0:T(8,128)(2,1)}, bf16[8,16,2,16,...) while((s32[]{:T(128)}, ...), condition=%wide.region_6.7_spmd.clone, body=%wide.region_3.6_spmd.clone.sunk | while | flops 109408800 | bytes 8521486 | solution.py:105
  344.8 0.9 dynamic-slice_bitcast_fusion.3
  346.5 1.0 copy_bitcast_fusion.2
  352.9 0.9 dynamic-slice_bitcast_fusion.3
  354.6 1.0 copy_bitcast_fusion.2
  361.0 0.9 dynamic-slice_bitcast_fusion.3
  362.6 1.0 copy_bitcast_fusion.2
  369.1 0.9 dynamic-slice_bitcast_fusion.3
  370.7 1.0 copy_bitcast_fusion.2
  377.1 0.9 dynamic-slice_bitcast_fusion.3
  378.8 1.0 copy_bitcast_fusion.2
  385.2 0.9 dynamic-slice_bitcast_fusion.3
  386.9 1.0 copy_bitcast_fusion.2
  393.3 0.9 dynamic-slice_bitcast_fusion.3
  394.9 1.0 copy_bitcast_fusion.2
  403.0 1.0 copy_bitcast_fusion.2
  409.4 3.1 reshape.286
  412.5 6.0 scatter_custom_fusion
  418.5 7.6 %all_to_all.20 = bf16[128,2,8192]{2,1,0:T(2,128)(2,1)} reshape(bf16[256,8192]{1,0:T(8,128)(2,1)} %scatter_custom_fusion) | data formatting | bytes 8388608 | tf_op jit(solution)/shard_map/all_to_all | solution.py:113
  426.1 197.8 %all_to_all.26 = bf16[128,2,8192]{2,1,0:T(2,128)(2,1)} all-to-all(bf16[128,2,8192]{2,1,0:T(2,128)(2,1)} %all_to_all.20), channel_id=1, replica_groups=mesh['pool'=128,'tp'=4] {'pool'}, dimensions={0} | all-to-all | bytes 8388608 | tf_op jit(solution)/shard_map/all_to_all | solution.py:113
  623.9 7.2 %all_to_all.22 = bf16[256,8192]{1,0:T(8,128)(2,1)} reshape(bf16[128,2,8192]{2,1,0:T(2,128)(2,1)} %all_to_all.26) | data formatting | bytes 8388608 | tf_op jit(solution)/shard_map/all_to_all | solution.py:113
  631.1 6.4 copy.85
  637.5 3.4 convolution_convert_fusion.1
  (382 shorter events, 54.1 us)
Async XLA Ops:
  114.5 25.3 %all-to-all-start = ((s32[128,2,1]{1,2,0:T(1,128)}), s32[128,2,1]{1,2,0:T(1,128)S(1)}, u32[]{:S(2)}, u32[]{:S(2)}) async-start(s32[128,2,1]{1,2,0:T(1,128)} %bitcast.2), calls=%async_computation | async-start | bytes 131072 | tf_op jit(solution)/shard_map/all_to_all | solution.py:76
  147.3 193.1 %all-to-all-start.1 = ((bf16[256,2,16,256]{3,2,1,0:T(8,128)(2,1)}), bf16[256,2,16,256]{3,2,1,0:T(8,128)(2,1)}, u32[]{:S(2)}, u32[]{:S(2)}) async-start(bf16[256,2,16,256]{3,2,1,0:T(8,128)(2,1)} %broadcast_select_fusion), calls=%async_computation.1 | async-start | bytes 8388608 | tf_op jit(solution)/shard_map/all_to_all | solution.py:79
  409.4 9.0 %copy-start = (bf16[8,16,2048]{2,1,0:T(8,128)(2,1)}, bf16[8,16,2048]{2,1,0:T(8,128)(2,1)S(1)}, u32[]{:S(2)}) copy-start(bf16[8,16,2048]{2,1,0:T(8,128)(2,1)S(1)} %get-tuple-element.151) | copy-start | bytes 1572868
where the time goes:
time: 647 us; the launch traced here: 642 us
  blocking collectives  309 us (48%)
  waiting for transfers between devices  199 us (31%)
  local copies, waits for them, and re-layouts  77.2 us (12%)
  other arithmetic  20 us (3%)
  starting transfers between devices  18 us (3%)
  matrix products  15.7 us (2%)
    all_to_all x1, blocking collectives, per_device(): lax.all_to_all(outgoing, 'pool', split_axis=0, concat_axis=0, tiled=True)  198 us
    all_to_all x1, waiting for transfers between devices, per_device(): lax.all_to_all(reply, 'pool', split_axis=0, concat_axis=0, tiled=True)  185 us
    unnamed x1, blocking collectives  111 us
    all_to_all x2, local copies, waits for them, and re-layouts, per_device(): lax.all_to_all(outgoing, 'pool', split_axis=0, concat_axis=0, tiled=True)  14.8 us
    all_to_all x1, waiting for transfers between devices, per_device(): lax.all_to_all(send_local, 'pool', split_axis=0, concat_axis=0, tiled=True)  14.2 us
  transfers between devices with their start and end apart: 2, of which 2 were waited for; matrix products, arithmetic and copies ran while one was open for 0% of the time, Pallas kernels for 0%

commit v1 on v0

v1 whole, which is shorter than its diff:
```python
import jax
import jax.numpy as jnp
from jax import lax
from jax.experimental import pallas as pl
from jax.experimental.pallas import tpu as pltpu
from jax.sharding import Mesh
from jax.sharding import PartitionSpec as P

HD = 128
GROUP = 8
QLEN = 16
LP = 16
NB = 16
QPD = 8
P_DEV = 4
CHIP_P = 2 * P_DEV
XS, ZH, ZL = 4, 4, 4
ZS = ZH * ZL
TILES = 2 * CHIP_P
ROWS = TILES + 1
COLUMN = ZS * ROWS
GCOLUMN = ZS * TILES
SCALE = HD ** (-0.5)
SPAN = NB * LP
WIDE = 2 * GROUP * HD + 2 * HD
BF = jnp.bfloat16
F32 = jnp.float32


def ring(n, d):
    return [(i, (i + d) % n) for i in range(n)]


def dot(a, b, ca, cb):
    return lax.dot_general(a, b, (((ca,), (cb,)), ((), ())), preferred_element_type=F32)


def attention_kernel(
    where_ref,
    gwhere_ref,
    valid_ref,
    s0,
    s1,
    s2a,
    s2b,
    s3,
    mine,
    other,
    g0,
    g1,
    g2a,
    g2b,
    g3,
    dq_mine,
    dq_other,
    self_mine,
    self_other,
    store,
    grads,
    sem_in,
    sem_out,
):
    half = COLUMN // 2
    loads = [
        pltpu.make_async_copy(src, store.at[pl.ds(start, size)], sem_in.at[i])
        for i, (src, start, size) in enumerate(
            [
                (s0, 0, COLUMN),
                (s1, COLUMN, COLUMN),
                (s2a, 2 * COLUMN, half),
                (s2b, 2 * COLUMN + half, half),
                (s3, 3 * COLUMN, COLUMN),
            ]
        )
    ]
    for copy in loads:
        copy.start()

    def clear(i, carry):
        grads[pl.ds(i * 16, 16)] = jnp.zeros((16, LP, HD), BF)
        return carry

    lax.fori_loop(0, XS * GCOLUMN // 16, clear, 0)
    for copy in loads:
        copy.wait()

    u = lax.broadcasted_iota(jnp.int32, (QLEN, GROUP * QLEN), 0)
    t = lax.broadcasted_iota(jnp.int32, (QLEN, GROUP * QLEN), 1) % QLEN
    causal = jnp.where(u <= t, 0.0, -1e30).astype(F32)

    def stacked(ref, b, start):
        return jnp.concatenate(
            [ref[b, :, start + g * HD : start + (g + 1) * HD] for g in range(GROUP)], axis=0
        )

    def one(b, base, pack, dq_out, self_out):
        row = (base + b) * NB
        at = [where_ref[row + j] for j in range(NB)]
        q = stacked(pack, b, 0)
        do = stacked(pack, b, GROUP * HD)
        own = 2 * GROUP * HD
        keys = jnp.concatenate([store[i] for i in at] + [pack[b, :, own : own + HD]], axis=0)
        values = jnp.concatenate(
            [store[i + 1] for i in at] + [pack[b, :, own + HD : own + 2 * HD]], axis=0
        )
        bias = jnp.concatenate(
            [
                jnp.full((LP, GROUP * QLEN), jnp.where(valid_ref[row + j] > 0, 0.0, -1e30), F32)
                for j in range(NB)
            ]
            + [causal],
            axis=0,
        )
        scores = dot(keys, q, 1, 1) * SCALE + bias
        top = jnp.max(scores, axis=0, keepdims=True)
        weights = jnp.exp(scores - top)
        probs = weights * (1.0 / jnp.sum(weights, axis=0, keepdims=True))
        low = probs.astype(BF)
        dprob = dot(values, do, 1, 1)
        delta = jnp.sum(probs * dprob, axis=0, keepdims=True)
        dscore = (probs * (dprob - delta)).astype(BF)
        dq = (dot(dscore, keys, 0, 0) * SCALE).astype(BF)
        for g in range(GROUP):
            dq_out[b, :, g * HD : (g + 1) * HD] = dq[g * QLEN : (g + 1) * QLEN]
        dk = (dot(dscore, q, 1, 0) * SCALE).astype(BF)
        dv = dot(low, do, 1, 0).astype(BF)
        self_out[b, :, :HD] = dk[SPAN:]
        self_out[b, :, HD:] = dv[SPAN:]
        for j in range(NB):
            to = gwhere_ref[row + j]
            for k, part in enumerate((dk, dv)):
                grads[to + k] = (
                    grads[to + k].astype(F32) + part[j * LP : (j + 1) * LP].astype(F32)
                ).astype(BF)

    def step(b, carry):
        one(b, 0, mine, dq_mine, self_mine)
        one(b, QPD, other, dq_other, self_other)
        return carry

    lax.fori_loop(0, QPD, step, 0)
    ghalf = GCOLUMN // 2
    stores = [
        pltpu.make_async_copy(grads.at[pl.ds(start, size)], dst, sem_out.at[i])
        for i, (dst, start, size) in enumerate(
            [
                (g2a, 2 * GCOLUMN, ghalf),
                (g2b, 2 * GCOLUMN + ghalf, ghalf),
                (g1, GCOLUMN, GCOLUMN),
                (g3, 3 * GCOLUMN, GCOLUMN),
                (g0, 0, GCOLUMN),
            ]
        )
    ]
    for copy in stores:
        copy.start()
    for copy in stores:
        copy.wait()


def attention(where, gwhere, valid, s0, s1, s2a, s2b, s3, mine, other):
    smem = pl.BlockSpec(memory_space=pltpu.SMEM)
    vmem = pl.BlockSpec(memory_space=pltpu.VMEM)
    hbm = pl.BlockSpec(memory_space=pl.ANY)

    def tiles(n):
        return jax.ShapeDtypeStruct((n, LP, HD), BF)

    query = jax.ShapeDtypeStruct((QPD, QLEN, GROUP * HD), BF)
    own = jax.ShapeDtypeStruct((QPD, QLEN, 2 * HD), BF)
    return pl.pallas_call(
        attention_kernel,
        out_shape=(
            tiles(GCOLUMN),
            tiles(GCOLUMN),
            tiles(GCOLUMN // 2),
            tiles(GCOLUMN // 2),
            tiles(GCOLUMN),
            query,
            query,
            own,
            own,
        ),
        in_specs=[smem] * 3 + [hbm] * 5 + [vmem] * 2,
        out_specs=(hbm,) * 5 + (vmem,) * 4,
        scratch_shapes=[
            pltpu.VMEM((XS * COLUMN, LP, HD), BF),
            pltpu.VMEM((XS * GCOLUMN, LP, HD), BF),
            pltpu.SemaphoreType.DMA((5,)),
            pltpu.SemaphoreType.DMA((5,)),
        ],
        compiler_params=pltpu.CompilerParams(vmem_limit_bytes=40 * 2**20),
        cost_estimate=pl.CostEstimate(
            flops=16 * 5 * 2 * 272 * 128 * 128, bytes_accessed=12 * 2**20, transcendentals=16 * 272 * 128
        ),
    )(where, gwhere, valid, s0, s1, s2a, s2b, s3, mine, other)


def total(*parts):
    out = parts[0].astype(F32)
    for part in parts[1:]:
        out = out + part.astype(F32)
    return out.astype(BF)


def per_device(
    queries,
    self_key,
    self_value,
    passage_key,
    passage_value,
    out_grad,
    block_ids,
    block_valid,
    passage_slot,
):
    core = lax.axis_index("core")
    my_x = lax.axis_index("x")
    swap = ring(2, 1)
    feat = GROUP * HD

    def head(array, c, width):
        return lax.dynamic_slice_in_dim(array, c * width, width, axis=array.ndim - 1)

    def passages(c):
        return jnp.stack([head(passage_key, c, HD), head(passage_value, c, HD)], axis=1)

    def by_core(mine_part, other_part, axis):
        first = jnp.where(core == 0, mine_part, other_part)
        second = jnp.where(core == 0, other_part, mine_part)
        return jnp.concatenate([first, second], axis=axis)

    chip_slots = lax.all_to_all(
        jnp.broadcast_to(passage_slot, (8,)), ("core", "tp"), split_axis=0, concat_axis=0, tiled=True
    )
    kv_other = lax.ppermute(passages(1 - core), "core", swap)
    kv_chip = by_core(passages(core), kv_other, 0).reshape(TILES, LP, HD)
    coded = jnp.concatenate([chip_slots // 16, chip_slots % 16]).astype(BF)
    code_tile = jnp.pad(coded.reshape(1, 1, 16), ((0, 0), (0, LP - 1), (0, HD - 16)))
    payload = jnp.concatenate([kv_chip, code_tile], axis=0)

    def pack(c):
        return jnp.concatenate(
            [
                head(queries, c, feat),
                head(out_grad, c, feat),
                head(self_key, c, HD),
                head(self_value, c, HD),
            ],
            axis=2,
        )

    mine = pack(core)
    other = lax.ppermute(pack(1 - core), "core", swap)
    lists = jnp.stack([block_ids, block_valid])
    lists_other = lax.ppermute(lists, "core", swap)

    far = lax.all_to_all(
        jnp.broadcast_to(payload[None], (ZH, ROWS, LP, HD)), "zh", split_axis=0, concat_axis=0, tiled=True
    )
    near = lax.all_to_all(
        jnp.broadcast_to(far[None], (ZL, ZH, ROWS, LP, HD)), "zl", split_axis=0, concat_axis=0, tiled=True
    )
    s0 = near.reshape(COLUMN, LP, HD)
    half = COLUMN // 2
    s1 = lax.ppermute(s0, "x", ring(XS, -1))
    s3 = lax.ppermute(s0, "x", ring(XS, 1))
    s2a = lax.ppermute(s1[:half], "x", ring(XS, -1))
    s2b = lax.ppermute(s3[half:], "x", ring(XS, 1))

    def place(number):
        pool = number // P_DEV
        x = pool // (2 * ZS)
        z = pool // 2 % ZS
        dx = (x - my_x) % XS
        return dx * ZS + z % ZL * ZH + z // ZL, pool % 2 * P_DEV + number % P_DEV

    codes = jnp.concatenate(
        [s.reshape(-1, ROWS, LP, HD)[:, TILES, 0, :16] for s in (s0, s1, s2a, s2b, s3)], axis=0
    ).astype(jnp.int32)
    slot_of = (codes[:, :CHIP_P] * 16 + codes[:, CHIP_P:]).reshape(-1)
    ids = jnp.concatenate([block_ids, lists_other[0]]).reshape(-1)
    valid = jnp.concatenate([block_valid, lists_other[1]]).reshape(-1)
    chip, inner = place(ids)
    id_at = chip * CHIP_P + inner
    every = jnp.arange(slot_of.shape[0], dtype=jnp.int32)
    slots = jnp.sum(jnp.where(id_at[:, None] == every[None, :], slot_of[None, :], 0), axis=1)
    chip, inner = place(slots)
    where = chip * ROWS + 2 * inner
    gwhere = chip * TILES + 2 * inner

    g0, g1, g2a, g2b, g3, dq_mine, dq_other, self_mine, self_other = attention(
        where, gwhere, valid, s0, s1, s2a, s2b, s3, mine, other
    )

    ghalf = GCOLUMN // 2
    via_a = lax.ppermute(g2a, "x", ring(XS, 1))
    via_b = lax.ppermute(g2b, "x", ring(XS, -1))
    up = jnp.concatenate([total(g1[:ghalf], via_a), g1[ghalf:]], axis=0)
    down = jnp.concatenate([g3[:ghalf], total(g3[ghalf:], via_b)], axis=0)
    from_below = lax.ppermute(up, "x", ring(XS, 1))
    from_above = lax.ppermute(down, "x", ring(XS, -1))
    column = total(g0, from_below, from_above).reshape(ZL, ZH, TILES, LP, HD)
    near_parts = lax.all_to_all(column, "zl", split_axis=0, concat_axis=0, tiled=True)
    near_sum = total(*[near_parts[i] for i in range(ZL)])
    far_parts = lax.all_to_all(near_sum, "zh", split_axis=0, concat_axis=0, tiled=True)
    chip_sum = total(*[far_parts[i] for i in range(ZH)]).reshape(2, P_DEV, 2, LP, HD)
    kept = lax.dynamic_index_in_dim(chip_sum, core, 0, keepdims=False)
    given = lax.dynamic_index_in_dim(chip_sum, 1 - core, 0, keepdims=False)
    taken = lax.ppermute(given, "core", swap)
    grad = by_core(kept, taken, 3)

    dq_taken = lax.ppermute(dq_other, "core", swap)
    self_taken = lax.ppermute(self_other, "core", swap)
    query_grad = by_core(dq_mine, dq_taken, 2)
    self_key_grad = by_core(self_mine[:, :, :HD], self_taken[:, :, :HD], 2)
    self_value_grad = by_core(self_mine[:, :, HD:], self_taken[:, :, HD:], 2)
    return (query_grad, self_key_grad, self_value_grad, grad[:, 0], grad[:, 1])


def solution(mesh):
    fine = Mesh(mesh.devices.reshape(XS, ZH, ZL, 2, 4), ("x", "zh", "zl", "core", "tp"))
    pool = ("x", "zh", "zl", "core")
    rows = P(pool, None, "tp")
    return jax.shard_map(
        per_device,
        mesh=fine,
        in_specs=(rows,) * 6 + (P(pool, None), P(pool, None), P(pool + ("tp",))),
        out_specs=(rows,) * 5,
        check_vma=False,
    )
```

time: 647 us -> 236 us (0.36)
  blocking collectives: 309 us -> 89.5 us
  waiting for transfers between devices: 199 us -> 51 us
  local copies, waits for them, and re-layouts: 77.2 us -> 8.19 us
  starting transfers between devices: 18 us -> 65.3 us
  matrix products: 15.7 us -> 0 us
  other arithmetic: 20 us -> 7.01 us
  Pallas kernels: 0 us -> 12 us
    all_to_all x2, waiting for transfers between devices: 199 us -> 7.62 us  [the longest x1 5.95 us: per_device(): lax.all_to_all(near_sum, 'zh', split_axis=0, concat_axis=0, tiled=True)]
    unnamed x1 -> x0, blocking collectives: 111 us -> none
    all_to_all x1 -> x3, blocking collectives: 198 us -> 89.5 us  [the longest x1 35.3 us: per_device(): lax.all_to_all(jnp.broadcast_to(far[None], (ZL, ZH, ROWS, LP, HD)), 'zl',...]
    ppermute x0 -> x14, starting transfers between devices: none -> 51.7 us  [the longest x1 8.57 us: per_device(): taken = lax.ppermute(given, 'core', swap)]
    ppermute x0 -> x14, waiting for transfers between devices: none -> 43.4 us  [the longest x1 15 us: per_device(): from_above = lax.ppermute(down, 'x', ring(XS, -1))]
    all_to_all x3 -> x0, local copies, waits for them, and re-layouts: 15.6 us -> none  [the longest x2 14.8 us: per_device(): lax.all_to_all(outgoing, 'pool', split_axis=0, concat_axis=0, tiled=True)]
    dot_general x41 -> x0, matrix products: 12.6 us -> none  [the longest x1 3.37 us: per_device(): summed = jnp.dot(picks, returned, preferred_element_type=jnp.float32)]
    pallas_call x0 -> x1, Pallas kernels: none -> 12 us  [attention(): pl.pallas_call(attention_kernel, out_shape=(tiles(GCOLUMN), tiles(GCOLUMN...]
  transfers between devices with their start and end apart: 2 -> 16, of which waited for: 2 -> 9; matrix products, arithmetic and copies ran while one was open for 0% -> 5% of each run, Pallas kernels for 0% -> 0%
where the time goes in v1:
time: 236 us; the launch traced here: 235 us
  blocking collectives  89.5 us (38%)
  starting transfers between devices  65.3 us (28%)
  waiting for transfers between devices  51 us (22%)
  Pallas kernels  12 us (5%)
  local copies, waits for them, and re-layouts  8.19 us (3%)
  other arithmetic  7.01 us (3%)
    all_to_all x1, blocking collectives, per_device(): lax.all_to_all(jnp.broadcast_to(far[None], (ZL, ZH, ROWS, LP, HD)), 'zl',...  35.3 us
    all_to_all x1, blocking collectives, per_device(): lax.all_to_all(column, 'zl', split_axis=0, concat_axis=0, tiled=True)  29.4 us
    all_to_all x1, blocking collectives, per_device(): lax.all_to_all(jnp.broadcast_to(payload[None], (ZH, ROWS, LP, HD)), 'zh',...  24.9 us
    ppermute x1, waiting for transfers between devices, per_device(): from_above = lax.ppermute(down, 'x', ring(XS, -1))  15 us
    pallas_call x1, Pallas kernels, attention(): pl.pallas_call(attention_kernel, out_shape=(tiles(GCOLUMN), tiles(GCOLUMN...  12 us
    ppermute x1, waiting for transfers between devices, per_device(): s3 = lax.ppermute(s0, 'x', ring(XS, 1))  10.6 us
    all_to_all x1, starting transfers between devices, per_device(): lax.all_to_all(jnp.broadcast_to(passage_slot, (8,)), ('core', 'tp'), spli...  10.1 us
    ppermute x1, starting transfers between devices, per_device(): taken = lax.ppermute(given, 'core', swap)  8.57 us
  transfers between devices with their start and end apart: 16, of which 9 were waited for; matrix products, arithmetic and copies ran while one was open for 5% of the time, Pallas kernels for 0%

profile of v1, /device:TPU:1, one launch (start us, length us, event | category | flops | bytes accessed | tf_op | source)
XLA Modules:
  0.0 234.7 jit_solution(18433710869807032986)
XLA Ops:
  1.9 10.1 %all-to-all-start = ((s32[8,1,1]{2,1,0:T(1,128)}), s32[8,1,1]{2,1,0:T(1,128)S(1)}, u32[]{:S(2)}, u32[]{:S(2)}) async-start(s32[8,1,1]{2,1,0:T(1,128)} %broadcast_in_dim.36), calls=%async_computation | async-start | bytes 8192 | tf_op jit(solution)/shard_map/all_to_all | solution.py:233
  12.8 2.0 collective-permute-start.1
  14.8 1.7 all-to-all-done
  16.9 24.9 %all_to_all.29 = bf16[4,17,16,128]{3,2,1,0:T(8,128)(2,1)S(1)} all-to-all(bf16[4,17,16,128]{3,2,1,0:T(8,128)(2,1)S(1)} %broadcast_in_dim.37), channel_id=1, replica_groups=mesh['x'=4,'zh'=4,'zl'=4,'core'=2,'tp'=4] {'zh'}, dimensions={0} | all-to-all | bytes 557056 | tf_op jit(solution)/shard_map/all_to_all | solution.py:258
  42.0 35.3 %all_to_all.30 = bf16[4,4,17,16,128]{4,3,2,1,0:T(8,128)(2,1)S(1)} all-to-all(bf16[4,4,17,16,128]{4,3,2,1,0:T(8,128)(2,1)S(1)} %broadcast_in_dim.38), channel_id=1, replica_groups=mesh['x'=4,'zh'=4,'zl'=4,'core'=2,'tp'=4] {'zl'}, dimensions={0} | all-to-all | bytes 2228224 | tf_op jit(solution)/shard_map/all_to_all | solution.py:261
  77.2 3.1 %collective-permute-start.4 = (bf16[272,16,128]{2,1,0:T(8,128)(2,1)S(1)}, bf16[272,16,128]{2,1,0:T(8,128)(2,1)S(1)}, u32[]{:S(2)}, u32[]{:S(2)}) collective-permute-start(bf16[272,16,128]{2,1,0:T(8,128)(2,1)S(1)} %bitcast.48), channel_id=1, source_target_pairs={{0,128},{128,256},{256,384},{384,0},{1,129},{129,257},{257,385},{3... | collective-permute-start | bytes 3342344 | tf_op jit(solution)/shard_map/ppermute | solution.py:267
  80.3 3.4 %collective-permute-start.2 = (bf16[272,16,128]{2,1,0:T(8,128)(2,1)S(1)}, bf16[272,16,128]{2,1,0:T(8,128)(2,1)S(1)}, u32[]{:S(2)}, u32[]{:S(2)}) collective-permute-start(bf16[272,16,128]{2,1,0:T(8,128)(2,1)S(1)} %bitcast.49), channel_id=1, source_target_pairs={{0,384},{128,0},{256,128},{384,256},{1,385},{129,1},{257,129},{385... | collective-permute-start | bytes 3342344 | tf_op jit(solution)/shard_map/ppermute | solution.py:266
  83.8 4.7 %collective-permute-start = (s32[2,8,16]{2,1,0:T(8,128)S(1)}, s32[2,8,16]{2,1,0:T(8,128)S(1)}, u32[]{:S(2)}, u32[]{:S(2)}) collective-permute-start(s32[2,8,16]{2,1,0:T(8,128)S(1)} %pad_add_fusion), channel_id=1, source_target_pairs={{0,4},{4,0},{1,5},{5,1},{2,6},{6,2},{3,7},{7,3},{8,12},{12,8},{9,1... | collective-permute-start | bytes 3080 | tf_op jit(solution)/shard_map/ppermute | solution.py:256
  88.5 1.3 constant_dynamic-slice_fusion.2
  90.7 1.9 collective-permute-start.6
  93.5 10.6 %collective-permute-done.4.s3 = bf16[272,16,128]{2,1,0:T(8,128)(2,1)S(1)} collective-permute-done((bf16[272,16,128]{2,1,0:T(8,128)(2,1)S(1)}, bf16[272,16,128]{2,1,0:T(8,128)(2,1)S(1)}, u32[]{:S(2)}, u32[]{:S(2)}) %collective-permute-start.4) | collective-permute-done | bytes 1114144 | tf_op jit(solution)/shard_map/ppermute | solution.py:267
  104.1 0.9 slice.121
  105.0 1.9 collective-permute-start.5
  107.0 0.9 slice.119
  107.9 4.6 %collective-permute-start.3 = (bf16[136,16,128]{2,1,0:T(8,128)(2,1)}, bf16[136,16,128]{2,1,0:T(8,128)(2,1)}, u32[]{:S(2)}, u32[]{:S(2)}) collective-permute-start(bf16[136,16,128]{2,1,0:T(8,128)(2,1)} %slice.119), channel_id=1, source_target_pairs={{0,384},{128,0},{256,128},{384,256},{1,385},{129,1},{257,129},{385... | collective-permute-start | bytes 1671176 | tf_op jit(solution)/shard_map/ppermute | solution.py:268
  113.0 6.4 %collective-permute-done.5.s2b = bf16[136,16,128]{2,1,0:T(8,128)(2,1)} collective-permute-done((bf16[136,16,128]{2,1,0:T(8,128)(2,1)}, bf16[136,16,128]{2,1,0:T(8,128)(2,1)}, u32[]{:S(2)}, u32[]{:S(2)}) %collective-permute-start.5) | collective-permute-done | bytes 557088 | tf_op jit(solution)/shard_map/ppermute | solution.py:269
  120.2 1.0 collective-permute-done.3.s2a
  122.6 1.1 copy-done
  123.6 12.0 %shard_map.128 = (bf16[256,16,128]{2,1,0:T(8,128)(2,1)S(1)}, bf16[256,16,128]{2,1,0:T(8,128)(2,1)S(1)}, bf16[128,16,128]{2,1,0:T(8,128)(2,1)S(1)}, bf16[128,16,1...) custom-call(s32[256]{0:T(256)S(1)} %multiply_add_fusion.1.where_ref,, ...), custom_call_target="tpu_custom_call" | custom-call | flops 713031680 | bytes 12582912 | tf_op jit(solution)/shard_map/pallas_call | solution.py:171
  135.7 5.3 %collective-permute-start.11 = (bf16[128,16,128]{2,1,0:T(8,128)(2,1)S(1)}, bf16[128,16,128]{2,1,0:T(8,128)(2,1)S(1)}, u32[]{:S(2)}, u32[]{:S(2)}) collective-permute-start(bf16[128,16,128]{2,1,0:T(8,128)(2,1)S(1)} %get-tuple-element.22), channel_id=1, source_target_pairs={{0,384},{128,0},{256,128},{384,256},{1,385},{129,1},{257,129},{385... | collective-permute-start | bytes 1572872 | tf_op jit(solution)/shard_map/ppermute | solution.py:298
  141.0 1.9 collective-permute-start.9
  143.0 4.8 %collective-permute-done.11 = bf16[128,16,128]{2,1,0:T(8,128)(2,1)S(1)} collective-permute-done((bf16[128,16,128]{2,1,0:T(8,128)(2,1)S(1)}, bf16[128,16,128]{2,1,0:T(8,128)(2,1)S(1)}, u32[]{:S(2)}, u32[]{:S(2)}) %collective-permute-start.11) | collective-permute-done | bytes 524320 | tf_op jit(solution)/shard_map/ppermute | solution.py:298
  148.1 5.3 %collective-permute-start.12 = (bf16[256,16,128]{2,1,0:T(8,128)(2,1)S(1)}, bf16[256,16,128]{2,1,0:T(8,128)(2,1)S(1)}, u32[]{:S(2)}, u32[]{:S(2)}) collective-permute-start(bf16[256,16,128]{2,1,0:T(8,128)(2,1)S(1)} %pad_maximum_fusion.1), channel_id=1, source_target_pairs={{0,384},{128,0},{256,128},{384,256},{1,385},{129,1},{257,129},{385... | collective-permute-start | bytes 3145736 | tf_op jit(solution)/shard_map/ppermute | solution.py:302
  153.7 1.9 collective-permute-start.10
  155.6 15.0 %collective-permute-done.12 = bf16[256,16,128]{2,1,0:T(8,128)(2,1)S(1)} collective-permute-done((bf16[256,16,128]{2,1,0:T(8,128)(2,1)S(1)}, bf16[256,16,128]{2,1,0:T(8,128)(2,1)S(1)}, u32[]{:S(2)}, u32[]{:S(2)}) %collective-permute-start.12) | collective-permute-done | bytes 1048608 | tf_op jit(solution)/shard_map/ppermute | solution.py:302
  170.6 5.3 %collective-permute-done.10 = bf16[256,16,128]{2,1,0:T(8,128)(2,1)S(1)} collective-permute-done((bf16[256,16,128]{2,1,0:T(8,128)(2,1)S(1)}, bf16[256,16,128]{2,1,0:T(8,128)(2,1)S(1)}, u32[]{:S(2)}, u32[]{:S(2)}) %collective-permute-start.10) | collective-permute-done | bytes 1048608 | tf_op jit(solution)/shard_map/ppermute | solution.py:301
  176.3 29.4 %all_to_all.31 = bf16[4,4,16,16,128]{4,3,2,1,0:T(8,128)(2,1)S(1)} all-to-all(bf16[4,4,16,16,128]{4,3,2,1,0:T(8,128)(2,1)S(1)} %bitcast.54), channel_id=1, replica_groups=mesh['x'=4,'zh'=4,'zl'=4,'core'=2,'tp'=4] {'zl'}, dimensions={0} | all-to-all | bytes 2097152 | tf_op jit(solution)/shard_map/all_to_all | solution.py:304
  206.6 3.4 %all-to-all-start.4 = ((bf16[4,16,16,128]{3,2,1,0:T(8,128)(2,1)}), bf16[4,16,16,128]{3,2,1,0:T(8,128)(2,1)S(1)}, u32[]{:S(2)}, u32[]{:S(2)}) async-start(bf16[4,16,16,128]{3,2,1,0:T(8,128)(2,1)} %fusion), calls=%async_computation.4 | async-start | bytes 524288 | tf_op jit(solution)/shard_map/all_to_all | solution.py:306
  210.0 5.2 %collective-permute-start.8 = (bf16[8,16,256]{2,1,0:T(8,128)(2,1)S(1)}, bf16[8,16,256]{2,1,0:T(8,128)(2,1)S(1)}, u32[]{:S(2)}, u32[]{:S(2)}) collective-permute-start(bf16[8,16,256]{2,1,0:T(8,128)(2,1)S(1)} %get-tuple-element.17), channel_id=1, source_target_pairs={{0,4},{4,0},{1,5},{5,1},{2,6},{6,2},{3,7},{7,3},{8,12},{12,8},{9,1... | collective-permute-start | bytes 196616 | tf_op jit(solution)/shard_map/ppermute | solution.py:314
  215.2 1.9 collective-permute-start.7
  218.7 6.0 %all-to-all-done.4 = bf16[4,16,16,128]{3,2,1,0:T(8,128)(2,1)S(1)} async-done(((bf16[4,16,16,128]{3,2,1,0:T(8,128)(2,1)}), bf16[4,16,16,128]{3,2,1,0:T(8,128)(2,1)S(1)}, u32[]{:S(2)}, u32[]{:S(2)}) %all-to-all-start.4) | async-done | bytes 262176 | tf_op jit(solution)/shard_map/all_to_all | solution.py:306
  224.7 8.6 %collective-permute-start.13 = (bf16[4,2,16,128]{3,2,1,0:T(8,128)(2,1)S(1)}, bf16[4,2,16,128]{3,2,1,0:T(8,128)(2,1)S(1)}, u32[]{:S(2)}, u32[]{:S(2)}) collective-permute-start(bf16[4,2,16,128]{3,2,1,0:T(8,128)(2,1)S(1)} %dynamic-slice_bitcast_fusion), channel_id=1, source_target_pairs={{0,4},{4,0},{1,5},{5,1},{2,6},{6,2},{3,7},{7,3},{8,12},{12,8},{9,1... | collective-permute-start | bytes 98312 | tf_op jit(solution)/shard_map/ppermute | solution.py:310
  (81 shorter events, 11.3 us)
Async XLA Ops:
  1.9 14.6 %all-to-all-start = ((s32[8,1,1]{2,1,0:T(1,128)}), s32[8,1,1]{2,1,0:T(1,128)S(1)}, u32[]{:S(2)}, u32[]{:S(2)}) async-start(s32[8,1,1]{2,1,0:T(1,128)} %broadcast_in_dim.36), calls=%async_computation | async-start | bytes 8192 | tf_op jit(solution)/shard_map/all_to_all | solution.py:233
  12.8 4.0 %collective-permute-start.1 = (bf16[4,2,16,128]{3,2,1,0:T(8,128)(2,1)S(1)}, bf16[4,2,16,128]{3,2,1,0:T(8,128)(2,1)S(1)}, u32[]{:S(2)}, u32[]{:S(2)}) collective-permute-start(bf16[4,2,16,128]{3,2,1,0:T(8,128)(2,1)S(1)} %pad_maximum_fusion.11), channel_id=1, source_target_pairs={{0,4},{4,0},{1,5},{5,1},{2,6},{6,2},{3,7},{7,3},{8,12},{12,8},{9,1... | collective-permute-start | bytes 98312 | tf_op jit(solution)/shard_map/ppermute | solution.py:236
  41.9 41.8 %copy-start.7 = (s32[8,16]{1,0:T(8,128)S(1)}, s32[8,16]{1,0:T(8,128)}, u32[]{:S(2)}) copy-start(s32[8,16]{1,0:T(8,128)} %param.16) | copy-start | bytes 1540
  41.9 41.8 %copy-start.8 = (s32[8,16]{1,0:T(8,128)S(1)}, s32[8,16]{1,0:T(8,128)}, u32[]{:S(2)}) copy-start(s32[8,16]{1,0:T(8,128)} %param.15) | copy-start | bytes 1540
  41.9 46.5 %copy-start.5 = (bf16[8,16,256]{2,1,0:T(8,128)(2,1)S(1)}, bf16[8,16,256]{2,1,0:T(8,128)(2,1)}, u32[]{:S(2)}) copy-start(bf16[8,16,256]{2,1,0:T(8,128)(2,1)} %param.11) | copy-start | bytes 196612
  41.9 46.5 %copy-start.6 = (bf16[8,16,256]{2,1,0:T(8,128)(2,1)S(1)}, bf16[8,16,256]{2,1,0:T(8,128)(2,1)}, u32[]{:S(2)}) copy-start(bf16[8,16,256]{2,1,0:T(8,128)(2,1)} %param.10) | copy-start | bytes 196612
  77.2 26.9 %collective-permute-start.4 = (bf16[272,16,128]{2,1,0:T(8,128)(2,1)S(1)}, bf16[272,16,128]{2,1,0:T(8,128)(2,1)S(1)}, u32[]{:S(2)}, u32[]{:S(2)}) collective-permute-start(bf16[272,16,128]{2,1,0:T(8,128)(2,1)S(1)} %bitcast.48), channel_id=1, source_target_pairs={{0,128},{128,256},{256,384},{384,0},{1,129},{129,257},{257,385},{3... | collective-permute-start | bytes 3342344 | tf_op jit(solution)/shard_map/ppermute | solution.py:267
  80.3 26.6 %collective-permute-start.2 = (bf16[272,16,128]{2,1,0:T(8,128)(2,1)S(1)}, bf16[272,16,128]{2,1,0:T(8,128)(2,1)S(1)}, u32[]{:S(2)}, u32[]{:S(2)}) collective-permute-start(bf16[272,16,128]{2,1,0:T(8,128)(2,1)S(1)} %bitcast.49), channel_id=1, source_target_pairs={{0,384},{128,0},{256,128},{384,256},{1,385},{129,1},{257,129},{385... | collective-permute-start | bytes 3342344 | tf_op jit(solution)/shard_map/ppermute | solution.py:266
  83.8 28.7 %collective-permute-start = (s32[2,8,16]{2,1,0:T(8,128)S(1)}, s32[2,8,16]{2,1,0:T(8,128)S(1)}, u32[]{:S(2)}, u32[]{:S(2)}) collective-permute-start(s32[2,8,16]{2,1,0:T(8,128)S(1)} %pad_add_fusion), channel_id=1, source_target_pairs={{0,4},{4,0},{1,5},{5,1},{2,6},{6,2},{3,7},{7,3},{8,12},{12,8},{9,1... | collective-permute-start | bytes 3080 | tf_op jit(solution)/shard_map/ppermute | solution.py:256
  90.7 31.9 %collective-permute-start.6 = (bf16[8,16,2304]{2,1,0:T(8,128)(2,1)}, bf16[8,16,2304]{2,1,0:T(8,128)(2,1)}, u32[]{:S(2)}, u32[]{:S(2)}) collective-permute-start(bf16[8,16,2304]{2,1,0:T(8,128)(2,1)} %pad_maximum_fusion.3), channel_id=1, source_target_pairs={{0,4},{4,0},{1,5},{5,1},{2,6},{6,2},{3,7},{7,3},{8,12},{12,8},{9,1... | collective-permute-start | bytes 1769480 | tf_op jit(solution)/shard_map/ppermute | solution.py:254
  105.0 14.4 %collective-permute-start.5 = (bf16[136,16,128]{2,1,0:T(8,128)(2,1)}, bf16[136,16,128]{2,1,0:T(8,128)(2,1)}, u32[]{:S(2)}, u32[]{:S(2)}) collective-permute-start(bf16[136,16,128]{2,1,0:T(8,128)(2,1)} %slice.121), channel_id=1, source_target_pairs={{0,128},{128,256},{256,384},{384,0},{1,129},{129,257},{257,385},{3... | collective-permute-start | bytes 1671176 | tf_op jit(solution)/shard_map/ppermute | solution.py:269
  107.9 13.3 %collective-permute-start.3 = (bf16[136,16,128]{2,1,0:T(8,128)(2,1)}, bf16[136,16,128]{2,1,0:T(8,128)(2,1)}, u32[]{:S(2)}, u32[]{:S(2)}) collective-permute-start(bf16[136,16,128]{2,1,0:T(8,128)(2,1)} %slice.119), channel_id=1, source_target_pairs={{0,384},{128,0},{256,128},{384,256},{1,385},{129,1},{257,129},{385... | collective-permute-start | bytes 1671176 | tf_op jit(solution)/shard_map/ppermute | solution.py:268
  122.6 1.1 copy-start
  135.7 12.3 %copy-start.1 = (bf16[8,16,1024]{2,1,0:T(8,128)(2,1)}, bf16[8,16,1024]{2,1,0:T(8,128)(2,1)S(1)}, u32[]{:S(2)}) copy-start(bf16[8,16,1024]{2,1,0:T(8,128)(2,1)S(1)} %get-tuple-element.14) | copy-start | bytes 786436
  135.7 12.3 %copy-start.3 = (bf16[8,16,1024]{2,1,0:T(8,128)(2,1)}, bf16[8,16,1024]{2,1,0:T(8,128)(2,1)S(1)}, u32[]{:S(2)}) copy-start(bf16[8,16,1024]{2,1,0:T(8,128)(2,1)S(1)} %get-tuple-element.15) | copy-start | bytes 786436
  135.7 12.2 %collective-permute-start.11 = (bf16[128,16,128]{2,1,0:T(8,128)(2,1)S(1)}, bf16[128,16,128]{2,1,0:T(8,128)(2,1)S(1)}, u32[]{:S(2)}, u32[]{:S(2)}) collective-permute-start(bf16[128,16,128]{2,1,0:T(8,128)(2,1)S(1)} %get-tuple-element.22), channel_id=1, source_target_pairs={{0,384},{128,0},{256,128},{384,256},{1,385},{129,1},{257,129},{385... | collective-permute-start | bytes 1572872 | tf_op jit(solution)/shard_map/ppermute | solution.py:298
  141.0 12.4 %collective-permute-start.9 = (bf16[128,16,128]{2,1,0:T(8,128)(2,1)S(1)}, bf16[128,16,128]{2,1,0:T(8,128)(2,1)S(1)}, u32[]{:S(2)}, u32[]{:S(2)}) collective-permute-start(bf16[128,16,128]{2,1,0:T(8,128)(2,1)S(1)} %get-tuple-element.20), channel_id=1, source_target_pairs={{0,128},{128,256},{256,384},{384,0},{1,129},{129,257},{257,385},{3... | collective-permute-start | bytes 1572872 | tf_op jit(solution)/shard_map/ppermute | solution.py:297
  148.1 22.5 %collective-permute-start.12 = (bf16[256,16,128]{2,1,0:T(8,128)(2,1)S(1)}, bf16[256,16,128]{2,1,0:T(8,128)(2,1)S(1)}, u32[]{:S(2)}, u32[]{:S(2)}) collective-permute-start(bf16[256,16,128]{2,1,0:T(8,128)(2,1)S(1)} %pad_maximum_fusion.1), channel_id=1, source_target_pairs={{0,384},{128,0},{256,128},{384,256},{1,385},{129,1},{257,129},{385... | collective-permute-start | bytes 3145736 | tf_op jit(solution)/shard_map/ppermute | solution.py:302
  153.7 22.2 %collective-permute-start.10 = (bf16[256,16,128]{2,1,0:T(8,128)(2,1)S(1)}, bf16[256,16,128]{2,1,0:T(8,128)(2,1)S(1)}, u32[]{:S(2)}, u32[]{:S(2)}) collective-permute-start(bf16[256,16,128]{2,1,0:T(8,128)(2,1)S(1)} %pad_maximum_fusion), channel_id=1, source_target_pairs={{0,128},{128,256},{256,384},{384,0},{1,129},{129,257},{257,385},{3... | collective-permute-start | bytes 3145736 | tf_op jit(solution)/shard_map/ppermute | solution.py:301
  205.7 9.5 %copy-start.4 = (bf16[8,16,1024]{2,1,0:T(8,128)(2,1)S(1)}, bf16[8,16,1024]{2,1,0:T(8,128)(2,1)}, u32[]{:S(2)}) copy-start(bf16[8,16,1024]{2,1,0:T(8,128)(2,1)} %copy-done.3) | copy-start | bytes 786436
  205.7 12.9 %copy-start.2 = (bf16[8,16,1024]{2,1,0:T(8,128)(2,1)S(1)}, bf16[8,16,1024]{2,1,0:T(8,128)(2,1)}, u32[]{:S(2)}) copy-start(bf16[8,16,1024]{2,1,0:T(8,128)(2,1)} %copy-done.1) | copy-start | bytes 786436
  206.6 18.1 %all-to-all-start.4 = ((bf16[4,16,16,128]{3,2,1,0:T(8,128)(2,1)}), bf16[4,16,16,128]{3,2,1,0:T(8,128)(2,1)S(1)}, u32[]{:S(2)}, u32[]{:S(2)}) async-start(bf16[4,16,16,128]{3,2,1,0:T(8,128)(2,1)} %fusion), calls=%async_computation.4 | async-start | bytes 524288 | tf_op jit(solution)/shard_map/all_to_all | solution.py:306
  210.0 7.2 %collective-permute-start.8 = (bf16[8,16,256]{2,1,0:T(8,128)(2,1)S(1)}, bf16[8,16,256]{2,1,0:T(8,128)(2,1)S(1)}, u32[]{:S(2)}, u32[]{:S(2)}) collective-permute-start(bf16[8,16,256]{2,1,0:T(8,128)(2,1)S(1)} %get-tuple-element.17), channel_id=1, source_target_pairs={{0,4},{4,0},{1,5},{5,1},{2,6},{6,2},{3,7},{7,3},{8,12},{12,8},{9,1... | collective-permute-start | bytes 196616 | tf_op jit(solution)/shard_map/ppermute | solution.py:314
  215.2 3.4 %collective-permute-start.7 = (bf16[8,16,1024]{2,1,0:T(8,128)(2,1)S(1)}, bf16[8,16,1024]{2,1,0:T(8,128)(2,1)S(1)}, u32[]{:S(2)}, u32[]{:S(2)}) collective-permute-start(bf16[8,16,1024]{2,1,0:T(8,128)(2,1)S(1)} %copy-done.4), channel_id=1, source_target_pairs={{0,4},{4,0},{1,5},{5,1},{2,6},{6,2},{3,7},{7,3},{8,12},{12,8},{9,1... | collective-permute-start | bytes 786440 | tf_op jit(solution)/shard_map/ppermute | solution.py:313
  224.7 9.4 %collective-permute-start.13 = (bf16[4,2,16,128]{3,2,1,0:T(8,128)(2,1)S(1)}, bf16[4,2,16,128]{3,2,1,0:T(8,128)(2,1)S(1)}, u32[]{:S(2)}, u32[]{:S(2)}) collective-permute-start(bf16[4,2,16,128]{3,2,1,0:T(8,128)(2,1)S(1)} %dynamic-slice_bitcast_fusion), channel_id=1, source_target_pairs={{0,4},{4,0},{1,5},{5,1},{2,6},{6,2},{3,7},{7,3},{8,12},{12,8},{9,1... | collective-permute-start | bytes 98312 | tf_op jit(solution)/shard_map/ppermute | solution.py:310

commit v2 on v1

v2 whole, which is shorter than its diff:
```python
import jax
import jax.numpy as jnp
from jax import lax
from jax.experimental import pallas as pl
from jax.experimental.pallas import tpu as pltpu
from jax.sharding import Mesh
from jax.sharding import PartitionSpec as P

HD = 128
GROUP = 8
QLEN = 16
LP = 16
NB = 16
QPD = 8
P_DEV = 4
XS, ZH, ZL, TP = 4, 4, 4, 4
ZS = ZH * ZL
TILES = 2 * P_DEV
CLASS = XS * ZH * 2 * TILES
SCALE = HD ** (-0.5)
SPAN = NB * LP
WIDE = 2 * GROUP * HD + 2 * HD
BF = jnp.bfloat16
F32 = jnp.float32


def ring(n, d):
    return [(i, (i + d) % n) for i in range(n)]


def dot(a, b, ca, cb):
    return lax.dot_general(a, b, (((ca,), (cb,)), ((), ())), preferred_element_type=F32)


def attention_kernel(
    where_ref,
    valid_ref,
    s0,
    s1,
    s2a,
    s2b,
    s3,
    mine,
    other,
    g0,
    g1,
    g2a,
    g2b,
    g3,
    dq_mine,
    dq_other,
    self_mine,
    self_other,
    store,
    grads,
    sem_in,
    sem_out,
):
    half = CLASS // 2
    loads = [
        pltpu.make_async_copy(src, store.at[pl.ds(start, size)], sem_in.at[i])
        for i, (src, start, size) in enumerate(
            [
                (s0, 0, CLASS),
                (s1, CLASS, CLASS),
                (s2a, 2 * CLASS, half),
                (s2b, 2 * CLASS + half, half),
                (s3, 3 * CLASS, CLASS),
            ]
        )
    ]
    for copy in loads:
        copy.start()

    def clear(i, carry):
        grads[pl.ds(i * 16, 16)] = jnp.zeros((16, LP, HD), BF)
        return carry

    lax.fori_loop(0, ZL * CLASS // 16, clear, 0)
    for copy in loads:
        copy.wait()

    u = lax.broadcasted_iota(jnp.int32, (QLEN, GROUP * QLEN), 0)
    t = lax.broadcasted_iota(jnp.int32, (QLEN, GROUP * QLEN), 1) % QLEN
    causal = jnp.where(u <= t, 0.0, -1e30).astype(F32)

    def stacked(ref, b, start):
        return jnp.concatenate(
            [ref[b, :, start + g * HD : start + (g + 1) * HD] for g in range(GROUP)], axis=0
        )

    def one(b, base, pack, dq_out, self_out):
        row = (base + b) * NB
        at = [where_ref[row + j] for j in range(NB)]
        q = stacked(pack, b, 0)
        do = stacked(pack, b, GROUP * HD)
        own = 2 * GROUP * HD
        keys = jnp.concatenate([store[i] for i in at] + [pack[b, :, own : own + HD]], axis=0)
        values = jnp.concatenate(
            [store[i + 1] for i in at] + [pack[b, :, own + HD : own + 2 * HD]], axis=0
        )
        bias = jnp.concatenate(
            [
                jnp.full((LP, GROUP * QLEN), jnp.where(valid_ref[row + j] > 0, 0.0, -1e30), F32)
                for j in range(NB)
            ]
            + [causal],
            axis=0,
        )
        scores = dot(keys, q, 1, 1) * SCALE + bias
        top = jnp.max(scores, axis=0, keepdims=True)
        weights = jnp.exp(scores - top)
        probs = weights * (1.0 / jnp.sum(weights, axis=0, keepdims=True))
        low = probs.astype(BF)
        dprob = dot(values, do, 1, 1)
        delta = jnp.sum(probs * dprob, axis=0, keepdims=True)
        dscore = (probs * (dprob - delta)).astype(BF)
        dq = (dot(dscore, keys, 0, 0) * SCALE).astype(BF)
        for g in range(GROUP):
            dq_out[b, :, g * HD : (g + 1) * HD] = dq[g * QLEN : (g + 1) * QLEN]
        dk = (dot(dscore, q, 1, 0) * SCALE).astype(BF)
        dv = dot(low, do, 1, 0).astype(BF)
        self_out[b, :, :HD] = dk[SPAN:]
        self_out[b, :, HD:] = dv[SPAN:]
        for j in range(NB):
            for k, part in enumerate((dk, dv)):
                to = at[j] + k
                grads[to] = (
                    grads[to].astype(F32) + part[j * LP : (j + 1) * LP].astype(F32)
                ).astype(BF)

    def step(b, carry):
        one(b, 0, mine, dq_mine, self_mine)
        one(b, QPD, other, dq_other, self_other)
        return carry

    lax.fori_loop(0, QPD, step, 0)
    stores = [
        pltpu.make_async_copy(grads.at[pl.ds(start, size)], dst, sem_out.at[i])
        for i, (dst, start, size) in enumerate(
            [
                (g2a, 2 * CLASS, half),
                (g2b, 2 * CLASS + half, half),
                (g1, CLASS, CLASS),
                (g3, 3 * CLASS, CLASS),
                (g0, 0, CLASS),
            ]
        )
    ]
    for copy in stores:
        copy.start()
    for copy in stores:
        copy.wait()


def attention(where, valid, s0, s1, s2a, s2b, s3, mine, other):
    smem = pl.BlockSpec(memory_space=pltpu.SMEM)
    vmem = pl.BlockSpec(memory_space=pltpu.VMEM)
    hbm = pl.BlockSpec(memory_space=pl.ANY)

    def tiles(n):
        return jax.ShapeDtypeStruct((n, LP, HD), BF)

    query = jax.ShapeDtypeStruct((QPD, QLEN, GROUP * HD), BF)
    own = jax.ShapeDtypeStruct((QPD, QLEN, 2 * HD), BF)
    return pl.pallas_call(
        attention_kernel,
        out_shape=(
            tiles(CLASS),
            tiles(CLASS),
            tiles(CLASS // 2),
            tiles(CLASS // 2),
            tiles(CLASS),
            query,
            query,
            own,
            own,
        ),
        in_specs=[smem] * 2 + [hbm] * 5 + [vmem] * 2,
        out_specs=(hbm,) * 5 + (vmem,) * 4,
        scratch_shapes=[
            pltpu.VMEM((ZL * CLASS, LP, HD), BF),
            pltpu.VMEM((ZL * CLASS, LP, HD), BF),
            pltpu.SemaphoreType.DMA((5,)),
            pltpu.SemaphoreType.DMA((5,)),
        ],
        compiler_params=pltpu.CompilerParams(vmem_limit_bytes=40 * 2**20),
        cost_estimate=pl.CostEstimate(
            flops=16 * 5 * 2 * 272 * 128 * 128, bytes_accessed=12 * 2**20, transcendentals=16 * 272 * 128
        ),
    )(where, valid, s0, s1, s2a, s2b, s3, mine, other)


def total(*parts):
    out = parts[0].astype(F32)
    for part in parts[1:]:
        out = out + part.astype(F32)
    return out.astype(BF)


def per_device(
    queries,
    self_key,
    self_value,
    passage_key,
    passage_value,
    out_grad,
    block_ids,
    block_valid,
    passage_slot,
):
    core = lax.axis_index("core")
    my_zl = lax.axis_index("zl")
    swap = ring(2, 1)
    around = ("zh", "zl")
    feat = GROUP * HD
    half = CLASS // 2

    def head(array, c, width):
        return lax.dynamic_slice_in_dim(array, c * width, width, axis=array.ndim - 1)

    def by_core(mine_part, other_part, axis):
        first = jnp.where(core == 0, mine_part, other_part)
        second = jnp.where(core == 0, other_part, mine_part)
        return jnp.concatenate([first, second], axis=axis)

    code = jnp.concatenate([passage_slot // 16, passage_slot % 16]).astype(BF)
    code_tile = jnp.pad(code.reshape(1, 1, 2), ((0, 0), (0, LP - 1), (0, HD - 2)))

    def passages(c):
        lanes = slice(c * HD, (c + 1) * HD)
        both = jnp.stack([passage_key[:, :, lanes], passage_value[:, :, lanes]], axis=1)
        return jnp.concatenate([both.reshape(TILES, LP, HD), code_tile], axis=0)

    heads = jnp.stack([passages(0), passages(1)])
    far = lax.all_to_all(
        jnp.broadcast_to(heads[None], (ZH, 2, TILES + 1, LP, HD)).reshape(2 * ZH, TILES + 1, LP, HD),
        ("zh", "core"),
        split_axis=0,
        concat_axis=0,
        tiled=True,
    )
    s0 = lax.all_to_all(
        jnp.broadcast_to(far[None, :, :TILES], (XS, 2 * ZH, TILES, LP, HD)),
        "x",
        split_axis=0,
        concat_axis=0,
        tiled=True,
    ).reshape(CLASS, LP, HD)
    s1 = lax.ppermute(s0, around, ring(ZS, -1))
    s3 = lax.ppermute(s0, around, ring(ZS, 1))
    s2a = lax.ppermute(s1[:half], around, ring(ZS, -1))
    s2b = lax.ppermute(s3[half:], around, ring(ZS, 1))

    def pack(c):
        return jnp.concatenate(
            [
                head(queries, c, feat),
                head(out_grad, c, feat),
                head(self_key, c, HD),
                head(self_value, c, HD),
            ],
            axis=2,
        )

    mine = pack(core)
    other = lax.ppermute(pack(1 - core), "core", swap)
    lists = jnp.stack([block_ids, block_valid])
    lists_other = lax.ppermute(lists, "core", swap)

    codes = far[:, TILES, 0, :2].astype(jnp.int32)
    known = codes[:, 0] * 16 + codes[:, 1]
    known, _ = lax.optimization_barrier((known, s0[:1, 0, :1]))
    slot_of = lax.all_to_all(
        jnp.broadcast_to(known[None], (XS * ZL * TP, 2 * ZH)),
        ("x", "zl", "tp"),
        split_axis=0,
        concat_axis=0,
        tiled=True,
    ).reshape(-1)

    def parts(number):
        pool = number // P_DEV
        z = pool // 2 % ZS
        return pool // (2 * ZS), z // ZL, z % ZL, pool % 2, number % P_DEV

    ids = jnp.concatenate([block_ids, lists_other[0]]).reshape(-1)
    valid = jnp.concatenate([block_valid, lists_other[1]]).reshape(-1)
    x, zh, zl, c, inner = parts(ids)
    id_at = (((x * ZL + zl) * TP + inner) * ZH + zh) * 2 + c
    every = jnp.arange(slot_of.shape[0], dtype=jnp.int32)
    slots = jnp.sum(jnp.where(id_at[:, None] == every[None, :], slot_of[None, :], 0), axis=1)
    x, zh, zl, c, inner = parts(slots)
    where = ((((zl - my_zl) % ZL * XS + x) * ZH + zh) * 2 + c) * TILES + 2 * inner

    g0, g1, g2a, g2b, g3, dq_mine, dq_other, self_mine, self_other = attention(
        where, valid, s0, s1, s2a, s2b, s3, mine, other
    )

    via_a = lax.ppermute(g2a, around, ring(ZS, 1))
    via_b = lax.ppermute(g2b, around, ring(ZS, -1))
    up = jnp.concatenate([total(g1[:half], via_a), g1[half:]], axis=0)
    down = jnp.concatenate([g3[:half], total(g3[half:], via_b)], axis=0)
    from_below = lax.ppermute(up, around, ring(ZS, 1))
    from_above = lax.ppermute(down, around, ring(ZS, -1))
    summed = total(g0, from_below, from_above).reshape(XS, 2 * ZH, TILES, LP, HD)
    x_parts = lax.all_to_all(summed, "x", split_axis=0, concat_axis=0, tiled=True)
    x_sum = total(*[x_parts[i] for i in range(XS)])
    far_parts = lax.all_to_all(x_sum, ("zh", "core"), split_axis=0, concat_axis=0, tiled=True)
    far_parts = far_parts.reshape(ZH, 2, P_DEV, 2, LP, HD)
    grad = total(*[far_parts[i] for i in range(ZH)])
    key_grad = jnp.concatenate([grad[0, :, 0], grad[1, :, 0]], axis=2)
    value_grad = jnp.concatenate([grad[0, :, 1], grad[1, :, 1]], axis=2)

    dq_taken = lax.ppermute(dq_other, "core", swap)
    self_taken = lax.ppermute(self_other, "core", swap)
    query_grad = by_core(dq_mine, dq_taken, 2)
    self_key_grad = by_core(self_mine[:, :, :HD], self_taken[:, :, :HD], 2)
    self_value_grad = by_core(self_mine[:, :, HD:], self_taken[:, :, HD:], 2)
    return (query_grad, self_key_grad, self_value_grad, key_grad, value_grad)


def solution(mesh):
    fine = Mesh(mesh.devices.reshape(XS, ZH, ZL, 2, TP), ("x", "zh", "zl", "core", "tp"))
    pool = ("x", "zh", "zl", "core")
    rows = P(pool, None, "tp")
    return jax.shard_map(
        per_device,
        mesh=fine,
        in_specs=(rows,) * 6 + (P(pool, None), P(pool, None), P(pool + ("tp",))),
        out_specs=(rows,) * 5,
        check_vma=False,
    )
```

time: 236 us -> 211 us (0.89)
  blocking collectives: 89.5 us -> 35.8 us
  waiting for transfers between devices: 51 us -> 73.3 us
  starting transfers between devices: 65.3 us -> 68.1 us
  other arithmetic: 7.01 us -> 9.78 us
    all_to_all x3 -> x1, blocking collectives: 89.5 us -> 35.8 us  [per_device(): lax.all_to_all(jnp.broadcast_to(heads[None], (ZH, 2, TILES + 1, LP, HD))....]
    all_to_all x2 -> x4, waiting for transfers between devices: 7.62 us -> 30.8 us  [the longest x1 15.5 us: per_device(): lax.all_to_all(x_sum, ('zh', 'core'), split_axis=0, concat_axis=0, tiled=...]
    all_to_all x2 -> x4, starting transfers between devices: 13.5 us -> 28.1 us  [the longest x1 12.6 us: per_device(): lax.all_to_all(x_sum, ('zh', 'core'), split_axis=0, concat_axis=0, tiled=...]
    ppermute x10 -> x8, starting transfers between devices: 38 us -> 25 us  [the longest x1 6.04 us: per_device(): s3 = lax.ppermute(s0, around, ring(ZS, 1))]
    ppermute x1, starting transfers between devices: 5.21 us -> 8.26 us  [per_device(): self_taken = lax.ppermute(self_other, 'core', swap)]
    ppermute x10 -> x8, waiting for transfers between devices: 43.2 us -> 42.5 us  [the longest x1 16.7 us: per_device(): s3 = lax.ppermute(s0, around, ring(ZS, 1))]
  transfers between devices with their start and end apart: 16 -> 16, of which waited for: 9 -> 7; matrix products, arithmetic and copies ran while one was open for 5% -> 6% of each run, Pallas kernels for 0% -> 0%
where the time goes in v2:
time: 211 us; the launch traced here: 210 us
  waiting for transfers between devices  73.3 us (35%)
  starting transfers between devices  68.1 us (32%)
  blocking collectives  35.8 us (17%)
  Pallas kernels  11.6 us (5%)
  local copies, waits for them, and re-layouts  9.97 us (5%)
  other arithmetic  9.78 us (5%)
    all_to_all x1, blocking collectives, per_device(): lax.all_to_all(jnp.broadcast_to(heads[None], (ZH, 2, TILES + 1, LP, HD))....  35.8 us
    ppermute x1, waiting for transfers between devices, per_device(): s3 = lax.ppermute(s0, around, ring(ZS, 1))  16.7 us
    ppermute x1, waiting for transfers between devices, per_device(): from_above = lax.ppermute(down, around, ring(ZS, -1))  15.8 us
    all_to_all x1, waiting for transfers between devices, per_device(): lax.all_to_all(x_sum, ('zh', 'core'), split_axis=0, concat_axis=0, tiled=...  15.5 us
    all_to_all x1, starting transfers between devices, per_device(): lax.all_to_all(x_sum, ('zh', 'core'), split_axis=0, concat_axis=0, tiled=...  12.6 us
    pallas_call x1, Pallas kernels, attention(): pl.pallas_call(attention_kernel, out_shape=(tiles(CLASS), tiles(CLASS), t...  11.6 us
    all_to_all x1, waiting for transfers between devices, per_device(): lax.all_to_all(jnp.broadcast_to(known[None], (XS * ZL * TP, 2 * ZH)), ('x...  8.94 us
    ppermute x1, starting transfers between devices, per_device(): self_taken = lax.ppermute(self_other, 'core', swap)  8.26 us
  transfers between devices with their start and end apart: 16, of which 7 were waited for; matrix products, arithmetic and copies ran while one was open for 6% of the time, Pallas kernels for 0%

profile of v2, /device:TPU:1, one launch (start us, length us, event | category | flops | bytes accessed | tf_op | source)
XLA Modules:
  0.0 210.2 jit_solution(12076557123182784807)
XLA Ops:
  3.0 35.8 %all_to_all.26 = bf16[8,9,16,128]{3,2,1,0:T(8,128)(2,1)S(1)} all-to-all(bf16[8,9,16,128]{3,2,1,0:T(8,128)(2,1)S(1)} %bitcast.48), channel_id=1, replica_groups=mesh['x'=4,'zh'=4,'zl'=4,'core'=2,'tp'=4] {'zh','core'}, dimensions={0} | all-to-all | bytes 589824 | tf_op jit(solution)/shard_map/all_to_all | solution.py:236
  39.5 1.2 broadcast_in_dim.39
  40.7 4.2 %all-to-all-start.2 = ((bf16[4,8,8,16,128]{4,3,2,1,0:T(8,128)(2,1)}), bf16[4,8,8,16,128]{4,3,2,1,0:T(8,128)(2,1)S(1)}, u32[]{:S(2)}, u32[]{:S(2)}) async-start(bf16[4,8,8,16,128]{4,3,2,1,0:T(8,128)(2,1)} %broadcast_in_dim.39), calls=%async_computation.2 | async-start | bytes 2097152 | tf_op jit(solution)/shard_map/all_to_all | solution.py:243
  45.5 2.9 %collective-permute-start = (s32[2,8,16]{2,1,0:T(8,128)}, s32[2,8,16]{2,1,0:T(8,128)S(1)}, u32[]{:S(2)}, u32[]{:S(2)}) collective-permute-start(s32[2,8,16]{2,1,0:T(8,128)} %pad_add_fusion), channel_id=1, source_target_pairs={{0,4},{4,0},{1,5},{5,1},{2,6},{6,2},{3,7},{7,3},{8,12},{12,8},{9,1... | collective-permute-start | bytes 3080 | tf_op jit(solution)/shard_map/ppermute | solution.py:269
  49.9 0.9 pad_maximum_fusion.3
  50.7 1.9 collective-permute-start.5
  52.6 6.3 %all-to-all-done.2 = bf16[4,8,8,16,128]{4,3,2,1,0:T(8,128)(2,1)S(1)} async-done(((bf16[4,8,8,16,128]{4,3,2,1,0:T(8,128)(2,1)}), bf16[4,8,8,16,128]{4,3,2,1,0:T(8,128)(2,1)S(1)}, u32[]{:S(2)}, u32[]{:S(2)}) %all-to-all-start.2) | async-done | bytes 1048608 | tf_op jit(solution)/shard_map/all_to_all | solution.py:243
  59.0 6.0 %collective-permute-start.3 = (bf16[256,16,128]{2,1,0:T(8,128)(2,1)S(1)}, bf16[256,16,128]{2,1,0:T(8,128)(2,1)S(1)}, u32[]{:S(2)}, u32[]{:S(2)}) collective-permute-start(bf16[256,16,128]{2,1,0:T(8,128)(2,1)S(1)} %bitcast.45), channel_id=1, source_target_pairs={{0,8},{8,16},{16,24},{24,32},{32,40},{40,48},{48,56},{56,64},{64,7... | collective-permute-start | bytes 3145736 | tf_op jit(solution)/shard_map/ppermute | solution.py:251
  65.0 1.9 collective-permute-start.1
  66.9 1.0 pad_maximum_fusion.2.mine
  69.0 16.7 %collective-permute-done.3.s3 = bf16[256,16,128]{2,1,0:T(8,128)(2,1)S(1)} collective-permute-done((bf16[256,16,128]{2,1,0:T(8,128)(2,1)S(1)}, bf16[256,16,128]{2,1,0:T(8,128)(2,1)S(1)}, u32[]{:S(2)}, u32[]{:S(2)}) %collective-permute-start.3) | collective-permute-done | bytes 1048608 | tf_op jit(solution)/shard_map/ppermute | solution.py:251
  85.7 0.8 slice.138
  86.5 3.9 %collective-permute-start.4 = (bf16[128,16,128]{2,1,0:T(8,128)(2,1)}, bf16[128,16,128]{2,1,0:T(8,128)(2,1)}, u32[]{:S(2)}, u32[]{:S(2)}) collective-permute-start(bf16[128,16,128]{2,1,0:T(8,128)(2,1)} %slice.138), channel_id=1, source_target_pairs={{0,8},{8,16},{16,24},{24,32},{32,40},{40,48},{48,56},{56,64},{64,7... | collective-permute-start | bytes 1572872 | tf_op jit(solution)/shard_map/ppermute | solution.py:253
  90.4 1.9 slice.137
  92.3 2.6 %collective-permute-start.2 = (bf16[128,16,128]{2,1,0:T(8,128)(2,1)}, bf16[128,16,128]{2,1,0:T(8,128)(2,1)}, u32[]{:S(2)}, u32[]{:S(2)}) collective-permute-start(bf16[128,16,128]{2,1,0:T(8,128)(2,1)} %slice.137), channel_id=1, source_target_pairs={{0,120},{8,0},{16,8},{24,16},{32,24},{40,32},{48,40},{56,48},{64,5... | collective-permute-start | bytes 1572872 | tf_op jit(solution)/shard_map/ppermute | solution.py:252
  95.6 7.7 %all-to-all-start.1 = ((s32[64,1,8]{2,1,0:T(1,128)}), s32[64,1,8]{2,1,0:T(1,128)S(1)}, u32[]{:S(2)}, u32[]{:S(2)}) async-start(s32[64,1,8]{2,1,0:T(1,128)} %broadcast_in_dim.17), calls=%async_computation.1 | async-start | bytes 65536 | tf_op jit(solution)/shard_map/all_to_all | solution.py:274
  103.3 8.9 %all-to-all-done.1 = s32[64,1,8]{2,1,0:T(1,128)S(1)} async-done(((s32[64,1,8]{2,1,0:T(1,128)}), s32[64,1,8]{2,1,0:T(1,128)S(1)}, u32[]{:S(2)}, u32[]{:S(2)}) %all-to-all-start.1) | async-done | bytes 2080 | tf_op jit(solution)/shard_map/all_to_all | solution.py:274
  113.9 11.6 %shard_map.128 = (bf16[256,16,128]{2,1,0:T(8,128)(2,1)S(1)}, bf16[256,16,128]{2,1,0:T(8,128)(2,1)S(1)}, bf16[128,16,128]{2,1,0:T(8,128)(2,1)S(1)}, bf16[128,16,1...) custom-call(s32[256]{0:T(256)S(1)} %fusion.19.where_ref, ...), custom_call_target="tpu_custom_call" | custom-call | flops 713031680 | bytes 12582912 | tf_op jit(solution)/shard_map/pallas_call | solution.py:166
  125.5 1.9 collective-permute-start.10
  127.4 3.4 %collective-permute-start.8 = (bf16[128,16,128]{2,1,0:T(8,128)(2,1)S(1)}, bf16[128,16,128]{2,1,0:T(8,128)(2,1)S(1)}, u32[]{:S(2)}, u32[]{:S(2)}) collective-permute-start(bf16[128,16,128]{2,1,0:T(8,128)(2,1)S(1)} %get-tuple-element.20), channel_id=1, source_target_pairs={{0,8},{8,16},{16,24},{24,32},{32,40},{40,48},{48,56},{56,64},{64,7... | collective-permute-start | bytes 1572872 | tf_op jit(solution)/shard_map/ppermute | solution.py:300
  130.9 5.4 %collective-permute-done.10 = bf16[128,16,128]{2,1,0:T(8,128)(2,1)S(1)} collective-permute-done((bf16[128,16,128]{2,1,0:T(8,128)(2,1)S(1)}, bf16[128,16,128]{2,1,0:T(8,128)(2,1)S(1)}, u32[]{:S(2)}, u32[]{:S(2)}) %collective-permute-start.10) | collective-permute-done | bytes 524320 | tf_op jit(solution)/shard_map/ppermute | solution.py:301
  136.5 3.4 %collective-permute-start.11 = (bf16[256,16,128]{2,1,0:T(8,128)(2,1)S(1)}, bf16[256,16,128]{2,1,0:T(8,128)(2,1)S(1)}, u32[]{:S(2)}, u32[]{:S(2)}) collective-permute-start(bf16[256,16,128]{2,1,0:T(8,128)(2,1)S(1)} %pad_maximum_fusion.1), channel_id=1, source_target_pairs={{0,120},{8,0},{16,8},{24,16},{32,24},{40,32},{48,40},{56,48},{64,5... | collective-permute-start | bytes 3145736 | tf_op jit(solution)/shard_map/ppermute | solution.py:305
  140.2 1.9 collective-permute-start.9
  142.1 15.8 %collective-permute-done.11 = bf16[256,16,128]{2,1,0:T(8,128)(2,1)S(1)} collective-permute-done((bf16[256,16,128]{2,1,0:T(8,128)(2,1)S(1)}, bf16[256,16,128]{2,1,0:T(8,128)(2,1)S(1)}, u32[]{:S(2)}, u32[]{:S(2)}) %collective-permute-start.11) | collective-permute-done | bytes 1048608 | tf_op jit(solution)/shard_map/ppermute | solution.py:305
  157.9 4.6 %collective-permute-done.9 = bf16[256,16,128]{2,1,0:T(8,128)(2,1)S(1)} collective-permute-done((bf16[256,16,128]{2,1,0:T(8,128)(2,1)S(1)}, bf16[256,16,128]{2,1,0:T(8,128)(2,1)S(1)}, u32[]{:S(2)}, u32[]{:S(2)}) %collective-permute-start.9) | collective-permute-done | bytes 1048608 | tf_op jit(solution)/shard_map/ppermute | solution.py:304
  162.5 1.4 add_convert_fusion
  163.9 3.6 %all-to-all-start.3 = ((bf16[4,8,8,16,128]{4,3,2,1,0:T(8,128)(2,1)}), bf16[4,8,8,16,128]{4,3,2,1,0:T(8,128)(2,1)S(1)}, u32[]{:S(2)}, u32[]{:S(2)}) async-start(bf16[4,8,8,16,128]{4,3,2,1,0:T(8,128)(2,1)} %bitcast.19), calls=%async_computation.3 | async-start | bytes 2097152 | tf_op jit(solution)/shard_map/all_to_all | solution.py:307
  167.6 8.3 %collective-permute-start.7 = (bf16[8,16,256]{2,1,0:T(8,128)(2,1)S(1)}, bf16[8,16,256]{2,1,0:T(8,128)(2,1)S(1)}, u32[]{:S(2)}, u32[]{:S(2)}) collective-permute-start(bf16[8,16,256]{2,1,0:T(8,128)(2,1)S(1)} %copy-done.5), channel_id=1, source_target_pairs={{0,4},{4,0},{1,5},{5,1},{2,6},{6,2},{3,7},{7,3},{8,12},{12,8},{9,1... | collective-permute-start | bytes 196616 | tf_op jit(solution)/shard_map/ppermute | solution.py:316
  175.9 1.9 collective-permute-start.6
  177.8 0.8 fusion
  178.7 12.6 %all-to-all-start.4 = ((bf16[8,8,16,128]{3,2,1,0:T(8,128)(2,1)}), bf16[8,8,16,128]{3,2,1,0:T(8,128)(2,1)S(1)}, u32[]{:S(2)}, u32[]{:S(2)}) async-start(bf16[8,8,16,128]{3,2,1,0:T(8,128)(2,1)} %fusion), calls=%async_computation.4 | async-start | bytes 524288 | tf_op jit(solution)/shard_map/all_to_all | solution.py:309
  193.4 15.5 %all-to-all-done.4 = bf16[8,8,16,128]{3,2,1,0:T(8,128)(2,1)S(1)} async-done(((bf16[8,8,16,128]{3,2,1,0:T(8,128)(2,1)}), bf16[8,8,16,128]{3,2,1,0:T(8,128)(2,1)S(1)}, u32[]{:S(2)}, u32[]{:S(2)}) %all-to-all-start.4) | async-done | bytes 262176 | tf_op jit(solution)/shard_map/all_to_all | solution.py:309
  (77 shorter events, 11.7 us)
Async XLA Ops:
  38.7 0.7 copy-start.6
  40.7 4.2 %copy-start.11 = (s32[8,16]{1,0:T(8,128)S(1)}, s32[8,16]{1,0:T(8,128)}, u32[]{:S(2)}) copy-start(s32[8,16]{1,0:T(8,128)} %param.15) | copy-start | bytes 1540
  40.7 4.2 %copy-start.12 = (s32[8,16]{1,0:T(8,128)S(1)}, s32[8,16]{1,0:T(8,128)}, u32[]{:S(2)}) copy-start(s32[8,16]{1,0:T(8,128)} %param.16) | copy-start | bytes 1540
  40.7 7.7 %copy-start.9 = (bf16[8,16,256]{2,1,0:T(8,128)(2,1)S(1)}, bf16[8,16,256]{2,1,0:T(8,128)(2,1)}, u32[]{:S(2)}) copy-start(bf16[8,16,256]{2,1,0:T(8,128)(2,1)} %param.11) | copy-start | bytes 196612
  40.7 7.7 %copy-start.10 = (bf16[8,16,256]{2,1,0:T(8,128)(2,1)S(1)}, bf16[8,16,256]{2,1,0:T(8,128)(2,1)}, u32[]{:S(2)}) copy-start(bf16[8,16,256]{2,1,0:T(8,128)(2,1)} %param.10) | copy-start | bytes 196612
  40.7 8.4 %copy-start.7 = (bf16[8,16,2048]{2,1,0:T(8,128)(2,1)S(1)}, bf16[8,16,2048]{2,1,0:T(8,128)(2,1)}, u32[]{:S(2)}) copy-start(bf16[8,16,2048]{2,1,0:T(8,128)(2,1)} %param.14) | copy-start | bytes 1572868
  40.7 8.4 %copy-start.8 = (bf16[8,16,2048]{2,1,0:T(8,128)(2,1)S(1)}, bf16[8,16,2048]{2,1,0:T(8,128)(2,1)}, u32[]{:S(2)}) copy-start(bf16[8,16,2048]{2,1,0:T(8,128)(2,1)} %param.9) | copy-start | bytes 1572868
  40.7 18.3 %all-to-all-start.2 = ((bf16[4,8,8,16,128]{4,3,2,1,0:T(8,128)(2,1)}), bf16[4,8,8,16,128]{4,3,2,1,0:T(8,128)(2,1)S(1)}, u32[]{:S(2)}, u32[]{:S(2)}) async-start(bf16[4,8,8,16,128]{4,3,2,1,0:T(8,128)(2,1)} %broadcast_in_dim.39), calls=%async_computation.2 | async-start | bytes 2097152 | tf_op jit(solution)/shard_map/all_to_all | solution.py:243
  45.5 22.5 %collective-permute-start = (s32[2,8,16]{2,1,0:T(8,128)}, s32[2,8,16]{2,1,0:T(8,128)S(1)}, u32[]{:S(2)}, u32[]{:S(2)}) collective-permute-start(s32[2,8,16]{2,1,0:T(8,128)} %pad_add_fusion), channel_id=1, source_target_pairs={{0,4},{4,0},{1,5},{5,1},{2,6},{6,2},{3,7},{7,3},{8,12},{12,8},{9,1... | collective-permute-start | bytes 3080 | tf_op jit(solution)/shard_map/ppermute | solution.py:269
  50.7 63.1 %collective-permute-start.5 = (bf16[8,16,2304]{2,1,0:T(8,128)(2,1)}, bf16[8,16,2304]{2,1,0:T(8,128)(2,1)S(1)}, u32[]{:S(2)}, u32[]{:S(2)}) collective-permute-start(bf16[8,16,2304]{2,1,0:T(8,128)(2,1)} %pad_maximum_fusion.3), channel_id=1, source_target_pairs={{0,4},{4,0},{1,5},{5,1},{2,6},{6,2},{3,7},{7,3},{8,12},{12,8},{9,1... | collective-permute-start | bytes 1769480 | tf_op jit(solution)/shard_map/ppermute | solution.py:267
  59.0 26.7 %collective-permute-start.3 = (bf16[256,16,128]{2,1,0:T(8,128)(2,1)S(1)}, bf16[256,16,128]{2,1,0:T(8,128)(2,1)S(1)}, u32[]{:S(2)}, u32[]{:S(2)}) collective-permute-start(bf16[256,16,128]{2,1,0:T(8,128)(2,1)S(1)} %bitcast.45), channel_id=1, source_target_pairs={{0,8},{8,16},{16,24},{24,32},{32,40},{40,48},{48,56},{56,64},{64,7... | collective-permute-start | bytes 3145736 | tf_op jit(solution)/shard_map/ppermute | solution.py:251
  65.0 25.4 %collective-permute-start.1 = (bf16[256,16,128]{2,1,0:T(8,128)(2,1)S(1)}, bf16[256,16,128]{2,1,0:T(8,128)(2,1)}, u32[]{:S(2)}, u32[]{:S(2)}) collective-permute-start(bf16[256,16,128]{2,1,0:T(8,128)(2,1)S(1)} %bitcast.46), channel_id=1, source_target_pairs={{0,120},{8,0},{16,8},{24,16},{32,24},{40,32},{48,40},{56,48},{64,5... | collective-permute-start | bytes 3145736 | tf_op jit(solution)/shard_map/ppermute | solution.py:250
  86.5 27.3 %collective-permute-start.4 = (bf16[128,16,128]{2,1,0:T(8,128)(2,1)}, bf16[128,16,128]{2,1,0:T(8,128)(2,1)}, u32[]{:S(2)}, u32[]{:S(2)}) collective-permute-start(bf16[128,16,128]{2,1,0:T(8,128)(2,1)} %slice.138), channel_id=1, source_target_pairs={{0,8},{8,16},{16,24},{24,32},{32,40},{40,48},{48,56},{56,64},{64,7... | collective-permute-start | bytes 1572872 | tf_op jit(solution)/shard_map/ppermute | solution.py:253
  92.3 21.6 %collective-permute-start.2 = (bf16[128,16,128]{2,1,0:T(8,128)(2,1)}, bf16[128,16,128]{2,1,0:T(8,128)(2,1)}, u32[]{:S(2)}, u32[]{:S(2)}) collective-permute-start(bf16[128,16,128]{2,1,0:T(8,128)(2,1)} %slice.137), channel_id=1, source_target_pairs={{0,120},{8,0},{16,8},{24,16},{32,24},{40,32},{48,40},{56,48},{64,5... | collective-permute-start | bytes 1572872 | tf_op jit(solution)/shard_map/ppermute | solution.py:252
  95.6 16.7 %all-to-all-start.1 = ((s32[64,1,8]{2,1,0:T(1,128)}), s32[64,1,8]{2,1,0:T(1,128)S(1)}, u32[]{:S(2)}, u32[]{:S(2)}) async-start(s32[64,1,8]{2,1,0:T(1,128)} %broadcast_in_dim.17), calls=%async_computation.1 | async-start | bytes 65536 | tf_op jit(solution)/shard_map/all_to_all | solution.py:274
  125.5 5.4 %copy-start = (bf16[8,16,256]{2,1,0:T(8,128)(2,1)}, bf16[8,16,256]{2,1,0:T(8,128)(2,1)S(1)}, u32[]{:S(2)}) copy-start(bf16[8,16,256]{2,1,0:T(8,128)(2,1)S(1)} %get-tuple-element.16) | copy-start | bytes 196612
  125.5 5.4 %copy-start.2 = (bf16[8,16,1024]{2,1,0:T(8,128)(2,1)}, bf16[8,16,1024]{2,1,0:T(8,128)(2,1)S(1)}, u32[]{:S(2)}) copy-start(bf16[8,16,1024]{2,1,0:T(8,128)(2,1)S(1)} %get-tuple-element.15) | copy-start | bytes 786436
  125.5 5.4 %copy-start.4 = (bf16[8,16,256]{2,1,0:T(8,128)(2,1)}, bf16[8,16,256]{2,1,0:T(8,128)(2,1)S(1)}, u32[]{:S(2)}) copy-start(bf16[8,16,256]{2,1,0:T(8,128)(2,1)S(1)} %get-tuple-element.17) | copy-start | bytes 196612
  125.5 10.8 %collective-permute-start.10 = (bf16[128,16,128]{2,1,0:T(8,128)(2,1)S(1)}, bf16[128,16,128]{2,1,0:T(8,128)(2,1)S(1)}, u32[]{:S(2)}, u32[]{:S(2)}) collective-permute-start(bf16[128,16,128]{2,1,0:T(8,128)(2,1)S(1)} %get-tuple-element.22), channel_id=1, source_target_pairs={{0,120},{8,0},{16,8},{24,16},{32,24},{40,32},{48,40},{56,48},{64,5... | collective-permute-start | bytes 1572872 | tf_op jit(solution)/shard_map/ppermute | solution.py:301
  127.4 12.5 %collective-permute-start.8 = (bf16[128,16,128]{2,1,0:T(8,128)(2,1)S(1)}, bf16[128,16,128]{2,1,0:T(8,128)(2,1)S(1)}, u32[]{:S(2)}, u32[]{:S(2)}) collective-permute-start(bf16[128,16,128]{2,1,0:T(8,128)(2,1)S(1)} %get-tuple-element.20), channel_id=1, source_target_pairs={{0,8},{8,16},{16,24},{24,32},{32,40},{40,48},{48,56},{56,64},{64,7... | collective-permute-start | bytes 1572872 | tf_op jit(solution)/shard_map/ppermute | solution.py:300
  136.5 21.4 %collective-permute-start.11 = (bf16[256,16,128]{2,1,0:T(8,128)(2,1)S(1)}, bf16[256,16,128]{2,1,0:T(8,128)(2,1)S(1)}, u32[]{:S(2)}, u32[]{:S(2)}) collective-permute-start(bf16[256,16,128]{2,1,0:T(8,128)(2,1)S(1)} %pad_maximum_fusion.1), channel_id=1, source_target_pairs={{0,120},{8,0},{16,8},{24,16},{32,24},{40,32},{48,40},{56,48},{64,5... | collective-permute-start | bytes 3145736 | tf_op jit(solution)/shard_map/ppermute | solution.py:305
  140.2 22.3 %collective-permute-start.9 = (bf16[256,16,128]{2,1,0:T(8,128)(2,1)S(1)}, bf16[256,16,128]{2,1,0:T(8,128)(2,1)S(1)}, u32[]{:S(2)}, u32[]{:S(2)}) collective-permute-start(bf16[256,16,128]{2,1,0:T(8,128)(2,1)S(1)} %pad_maximum_fusion), channel_id=1, source_target_pairs={{0,8},{8,16},{16,24},{24,32},{32,40},{40,48},{48,56},{56,64},{64,7... | collective-permute-start | bytes 3145736 | tf_op jit(solution)/shard_map/ppermute | solution.py:304
  163.9 3.7 %copy-start.5 = (bf16[8,16,256]{2,1,0:T(8,128)(2,1)S(1)}, bf16[8,16,256]{2,1,0:T(8,128)(2,1)}, u32[]{:S(2)}) copy-start(bf16[8,16,256]{2,1,0:T(8,128)(2,1)} %copy-done.4) | copy-start | bytes 196612
  163.9 12.0 %copy-start.3 = (bf16[8,16,1024]{2,1,0:T(8,128)(2,1)S(1)}, bf16[8,16,1024]{2,1,0:T(8,128)(2,1)}, u32[]{:S(2)}) copy-start(bf16[8,16,1024]{2,1,0:T(8,128)(2,1)} %copy-done.2) | copy-start | bytes 786436
  163.9 13.9 %all-to-all-start.3 = ((bf16[4,8,8,16,128]{4,3,2,1,0:T(8,128)(2,1)}), bf16[4,8,8,16,128]{4,3,2,1,0:T(8,128)(2,1)S(1)}, u32[]{:S(2)}, u32[]{:S(2)}) async-start(bf16[4,8,8,16,128]{4,3,2,1,0:T(8,128)(2,1)} %bitcast.19), calls=%async_computation.3 | async-start | bytes 2097152 | tf_op jit(solution)/shard_map/all_to_all | solution.py:307
  167.6 23.7 %copy-start.1 = (bf16[8,16,256]{2,1,0:T(8,128)(2,1)S(1)}, bf16[8,16,256]{2,1,0:T(8,128)(2,1)}, u32[]{:S(2)}) copy-start(bf16[8,16,256]{2,1,0:T(8,128)(2,1)} %copy-done) | copy-start | bytes 196612
  167.6 23.6 %collective-permute-start.7 = (bf16[8,16,256]{2,1,0:T(8,128)(2,1)S(1)}, bf16[8,16,256]{2,1,0:T(8,128)(2,1)S(1)}, u32[]{:S(2)}, u32[]{:S(2)}) collective-permute-start(bf16[8,16,256]{2,1,0:T(8,128)(2,1)S(1)} %copy-done.5), channel_id=1, source_target_pairs={{0,4},{4,0},{1,5},{5,1},{2,6},{6,2},{3,7},{7,3},{8,12},{12,8},{9,1... | collective-permute-start | bytes 196616 | tf_op jit(solution)/shard_map/ppermute | solution.py:316
  175.9 16.7 %collective-permute-start.6 = (bf16[8,16,1024]{2,1,0:T(8,128)(2,1)S(1)}, bf16[8,16,1024]{2,1,0:T(8,128)(2,1)S(1)}, u32[]{:S(2)}, u32[]{:S(2)}) collective-permute-start(bf16[8,16,1024]{2,1,0:T(8,128)(2,1)S(1)} %copy-done.3), channel_id=1, source_target_pairs={{0,4},{4,0},{1,5},{5,1},{2,6},{6,2},{3,7},{7,3},{8,12},{12,8},{9,1... | collective-permute-start | bytes 786440 | tf_op jit(solution)/shard_map/ppermute | solution.py:315
  178.7 30.3 %all-to-all-start.4 = ((bf16[8,8,16,128]{3,2,1,0:T(8,128)(2,1)}), bf16[8,8,16,128]{3,2,1,0:T(8,128)(2,1)S(1)}, u32[]{:S(2)}, u32[]{:S(2)}) async-start(bf16[8,8,16,128]{3,2,1,0:T(8,128)(2,1)} %fusion), calls=%async_computation.4 | async-start | bytes 524288 | tf_op jit(solution)/shard_map/all_to_all | solution.py:309

commit v3 on v2

--- a/solution.py
+++ b/solution.py
@@ -16,10 +16,10 @@
 XS, ZH, ZL, TP = 4, 4, 4, 4
 ZS = ZH * ZL
 TILES = 2 * P_DEV
-CLASS = XS * ZH * 2 * TILES
+HALF = XS * ZH * TILES
+PARTS = 2 * ZL
 SCALE = HD ** (-0.5)
 SPAN = NB * LP
-WIDE = 2 * GROUP * HD + 2 * HD
 BF = jnp.bfloat16
 F32 = jnp.float32
 
@@ -35,39 +35,15 @@
 def attention_kernel(
     where_ref,
     valid_ref,
-    s0,
-    s1,
-    s2a,
-    s2b,
-    s3,
-    mine,
-    other,
-    g0,
-    g1,
-    g2a,
-    g2b,
-    g3,
-    dq_mine,
-    dq_other,
-    self_mine,
-    self_other,
-    store,
-    grads,
-    sem_in,
-    sem_out,
+    *refs,
 ):
-    half = CLASS // 2
+    stored, (mine, other) = refs[:PARTS], refs[PARTS : PARTS + 2]
+    outs = refs[PARTS + 2 : 2 * PARTS + 2]
+    dq_mine, dq_other, self_mine, self_other = refs[2 * PARTS + 2 : 2 * PARTS + 6]
+    store, grads, sem_in, sem_out = refs[2 * PARTS + 6 :]
     loads = [
-        pltpu.make_async_copy(src, store.at[pl.ds(start, size)], sem_in.at[i])
-        for i, (src, start, size) in enumerate(
-            [
-                (s0, 0, CLASS),
-                (s1, CLASS, CLASS),
-                (s2a, 2 * CLASS, half),
-                (s2b, 2 * CLASS + half, half),
-                (s3, 3 * CLASS, CLASS),
-            ]
-        )
+        pltpu.make_async_copy(src, store.at[pl.ds(i * HALF, HALF)], sem_in.at[i])
+        for i, src in enumerate(stored)
     ]
     for copy in loads:
         copy.start()
@@ -76,7 +52,7 @@
         grads[pl.ds(i * 16, 16)] = jnp.zeros((16, LP, HD), BF)
         return carry
 
-    lax.fori_loop(0, ZL * CLASS // 16, clear, 0)
+    lax.fori_loop(0, PARTS * HALF // 16, clear, 0)
     for copy in loads:
         copy.wait()
 
@@ -136,16 +112,8 @@
 
     lax.fori_loop(0, QPD, step, 0)
     stores = [
-        pltpu.make_async_copy(grads.at[pl.ds(start, size)], dst, sem_out.at[i])
-        for i, (dst, start, size) in enumerate(
-            [
-                (g2a, 2 * CLASS, half),
-                (g2b, 2 * CLASS + half, half),
-                (g1, CLASS, CLASS),
-                (g3, 3 * CLASS, CLASS),
-                (g0, 0, CLASS),
-            ]
-        )
+        pltpu.make_async_copy(grads.at[pl.ds(i * HALF, HALF)], dst, sem_out.at[i])
+        for i, dst in enumerate(outs)
     ]
     for copy in stores:
         copy.start()
@@ -153,42 +121,29 @@
         copy.wait()
 
 
-def attention(where, valid, s0, s1, s2a, s2b, s3, mine, other):
+def attention(where, valid, stored, mine, other):
     smem = pl.BlockSpec(memory_space=pltpu.SMEM)
     vmem = pl.BlockSpec(memory_space=pltpu.VMEM)
     hbm = pl.BlockSpec(memory_space=pl.ANY)
-
-    def tiles(n):
-        return jax.ShapeDtypeStruct((n, LP, HD), BF)
-
+    tiles = jax.ShapeDtypeStruct((HALF, LP, HD), BF)
     query = jax.ShapeDtypeStruct((QPD, QLEN, GROUP * HD), BF)
     own = jax.ShapeDtypeStruct((QPD, QLEN, 2 * HD), BF)
     return pl.pallas_call(
         attention_kernel,
-        out_shape=(
-            tiles(CLASS),
-            tiles(CLASS),
-            tiles(CLASS // 2),
-            tiles(CLASS // 2),
-            tiles(CLASS),
-            query,
-            query,
-            own,
-            own,
-        ),
-        in_specs=[smem] * 2 + [hbm] * 5 + [vmem] * 2,
-        out_specs=(hbm,) * 5 + (vmem,) * 4,
+        out_shape=(tiles,) * PARTS + (query, query, own, own),
+        in_specs=[smem] * 2 + [hbm] * PARTS + [vmem] * 2,
+        out_specs=(hbm,) * PARTS + (vmem,) * 4,
         scratch_shapes=[
-            pltpu.VMEM((ZL * CLASS, LP, HD), BF),
-            pltpu.VMEM((ZL * CLASS, LP, HD), BF),
-            pltpu.SemaphoreType.DMA((5,)),
-            pltpu.SemaphoreType.DMA((5,)),
+            pltpu.VMEM((PARTS * HALF, LP, HD), BF),
+            pltpu.VMEM((PARTS * HALF, LP, HD), BF),
+            pltpu.SemaphoreType.DMA((PARTS,)),
+            pltpu.SemaphoreType.DMA((PARTS,)),
         ],
         compiler_params=pltpu.CompilerParams(vmem_limit_bytes=40 * 2**20),
         cost_estimate=pl.CostEstimate(
             flops=16 * 5 * 2 * 272 * 128 * 128, bytes_accessed=12 * 2**20, transcendentals=16 * 272 * 128
         ),
-    )(where, valid, s0, s1, s2a, s2b, s3, mine, other)
+    )(where, valid, *stored, mine, other)
 
 
 def total(*parts):
@@ -214,7 +169,6 @@
     swap = ring(2, 1)
     around = ("zh", "zl")
     feat = GROUP * HD
-    half = CLASS // 2
 
     def head(array, c, width):
         return lax.dynamic_slice_in_dim(array, c * width, width, axis=array.ndim - 1)
@@ -240,17 +194,26 @@
         concat_axis=0,
         tiled=True,
     )
-    s0 = lax.all_to_all(
-        jnp.broadcast_to(far[None, :, :TILES], (XS, 2 * ZH, TILES, LP, HD)),
-        "x",
-        split_axis=0,
-        concat_axis=0,
-        tiled=True,
-    ).reshape(CLASS, LP, HD)
-    s1 = lax.ppermute(s0, around, ring(ZS, -1))
-    s3 = lax.ppermute(s0, around, ring(ZS, 1))
-    s2a = lax.ppermute(s1[:half], around, ring(ZS, -1))
-    s2b = lax.ppermute(s3[half:], around, ring(ZS, 1))
+    far_halves = far.reshape(2, ZH, TILES + 1, LP, HD)
+
+    def along_x(h):
+        return lax.all_to_all(
+            jnp.broadcast_to(far_halves[h][None, :, :TILES], (XS, ZH, TILES, LP, HD)),
+            "x",
+            split_axis=0,
+            concat_axis=0,
+            tiled=True,
+        ).reshape(HALF, LP, HD)
+
+    def up(part):
+        return lax.ppermute(part, around, ring(ZS, 1))
+
+    def down(part):
+        return lax.ppermute(part, around, ring(ZS, -1))
+
+    s0a, s0b = along_x(0), along_x(1)
+    s1a, s3a = down(s0a), up(s0a)
+    s3b, s1b = up(s0b), down(s0b)
 
     def pack(c):
         return jnp.concatenate(
@@ -270,7 +233,7 @@
 
     codes = far[:, TILES, 0, :2].astype(jnp.int32)
     known = codes[:, 0] * 16 + codes[:, 1]
-    known, _ = lax.optimization_barrier((known, s0[:1, 0, :1]))
+    known, _ = lax.optimization_barrier((known, s0a[:1, 0, :1]))
     slot_of = lax.all_to_all(
         jnp.broadcast_to(known[None], (XS * ZL * TP, 2 * ZH)),
         ("x", "zl", "tp"),
@@ -278,6 +241,8 @@
         concat_axis=0,
         tiled=True,
     ).reshape(-1)
+    s1a, slot_of = lax.optimization_barrier((s1a, slot_of))
+    s2a, s2b = down(s1a), up(s3b)
 
     def parts(number):
         pool = number // P_DEV
@@ -291,19 +256,26 @@
     every = jnp.arange(slot_of.shape[0], dtype=jnp.int32)
     slots = jnp.sum(jnp.where(id_at[:, None] == every[None, :], slot_of[None, :], 0), axis=1)
     x, zh, zl, c, inner = parts(slots)
-    where = ((((zl - my_zl) % ZL * XS + x) * ZH + zh) * 2 + c) * TILES + 2 * inner
-
-    g0, g1, g2a, g2b, g3, dq_mine, dq_other, self_mine, self_other = attention(
-        where, valid, s0, s1, s2a, s2b, s3, mine, other
+    part = (zl - my_zl) % ZL * 2 + zh // 2
+    where = (((part * XS + x) * 2 + zh % 2) * 2 + c) * TILES + 2 * inner
+
+    *grads, dq_mine, dq_other, self_mine, self_other = attention(
+        where, valid, (s0a, s0b, s1a, s1b, s2a, s2b, s3a, s3b), mine, other
     )
-
-    via_a = lax.ppermute(g2a, around, ring(ZS, 1))
-    via_b = lax.ppermute(g2b, around, ring(ZS, -1))
-    up = jnp.concatenate([total(g1[:half], via_a), g1[half:]], axis=0)
-    down = jnp.concatenate([g3[:half], total(g3[half:], via_b)], axis=0)
-    from_below = lax.ppermute(up, around, ring(ZS, 1))
-    from_above = lax.ppermute(down, around, ring(ZS, -1))
-    summed = total(g0, from_below, from_above).reshape(XS, 2 * ZH, TILES, LP, HD)
+    g0a, g0b, g1a, g1b, g2a, g2b, g3a, g3b = grads
+
+    via_a, via_b = up(g2a), down(g2b)
+    from_below_b, from_above_a = up(g1b), down(g3a)
+    from_below_a = up(total(g1a, via_a))
+    from_above_b = down(total(g3b, via_b))
+    halves = (XS, ZH, TILES, LP, HD)
+    summed = jnp.concatenate(
+        [
+            total(g0a, from_above_a, from_below_a).reshape(halves),
+            total(g0b, from_below_b, from_above_b).reshape(halves),
+        ],
+        axis=1,
+    )
     x_parts = lax.all_to_all(summed, "x", split_axis=0, concat_axis=0, tiled=True)
     x_sum = total(*[x_parts[i] for i in range(XS)])
     far_parts = lax.all_to_all(x_sum, ("zh", "core"), split_axis=0, concat_axis=0, tiled=True)
@@ -312,6 +284,7 @@
     key_grad = jnp.concatenate([grad[0, :, 0], grad[1, :, 0]], axis=2)
     value_grad = jnp.concatenate([grad[0, :, 1], grad[1, :, 1]], axis=2)
 
+    dq_other, self_other, _ = lax.optimization_barrier((dq_other, self_other, from_below_b[:1, 0, :1]))
     dq_taken = lax.ppermute(dq_other, "core", swap)
     self_taken = lax.ppermute(self_other, "core", swap)
     query_grad = by_core(dq_mine, dq_taken, 2)

time: 211 us -> 208 us (0.986)
  the two profiles are of different devices: /device:TPU:1 before, /device:TPU:32 now
where the time goes in v3:
time: 208 us; the launch traced here: 207 us
  waiting for transfers between devices  91.6 us (44%)
  starting transfers between devices  88.8 us (43%)
  Pallas kernels  10.9 us (5%)
  other arithmetic  8.16 us (4%)
  local copies, waits for them, and re-layouts  5.73 us (3%)
    ppermute x6, starting transfers between devices, down(): return lax.ppermute(part, around, ring(ZS, -1))  20.7 us
    ppermute x6, waiting for transfers between devices, down(): return lax.ppermute(part, around, ring(ZS, -1))  20.6 us
    all_to_all x1, waiting for transfers between devices, per_device(): lax.all_to_all(jnp.broadcast_to(heads[None], (ZH, 2, TILES + 1, LP, HD))....  20.2 us
    ppermute x6, starting transfers between devices, up(): return lax.ppermute(part, around, ring(ZS, 1))  19.7 us
    all_to_all x1, waiting for transfers between devices, per_device(): lax.all_to_all(x_sum, ('zh', 'core'), split_axis=0, concat_axis=0, tiled=...  19.6 us
    all_to_all x1, starting transfers between devices, per_device(): lax.all_to_all(jnp.broadcast_to(heads[None], (ZH, 2, TILES + 1, LP, HD))....  14.2 us
    all_to_all x2, waiting for transfers between devices, along_x(): lax.all_to_all(jnp.broadcast_to(far_halves[h][None, :, :TILES], (XS, ZH,...  12.7 us
    pallas_call x1, Pallas kernels, attention(): pl.pallas_call(attention_kernel, out_shape=(tiles,) * PARTS + (query, que...  10.9 us
  transfers between devices with their start and end apart: 22, of which 12 were waited for; matrix products, arithmetic and copies ran while one was open for 4% of the time, Pallas kernels for 0%

profile of v3, /device:TPU:32, one launch (start us, length us, event | category | flops | bytes accessed | tf_op | source)
XLA Modules:
  0.0 207.2 jit_solution(11733878097770661509)
XLA Ops:
  3.8 14.2 %all-to-all-start = ((bf16[8,9,16,128]{3,2,1,0:T(8,128)(2,1)}), bf16[8,9,16,128]{3,2,1,0:T(8,128)(2,1)S(1)}, u32[]{:S(2)}, u32[]{:S(2)}) async-start(bf16[8,9,16,128]{3,2,1,0:T(8,128)(2,1)} %bitcast.13), calls=%async_computation | async-start | bytes 589824 | tf_op jit(solution)/shard_map/all_to_all | solution.py:190
  18.0 2.4 %collective-permute-start = (s32[2,8,16]{2,1,0:T(8,128)S(1)}, s32[2,8,16]{2,1,0:T(8,128)S(1)}, u32[]{:S(2)}, u32[]{:S(2)}) collective-permute-start(s32[2,8,16]{2,1,0:T(8,128)S(1)} %pad_add_fusion), channel_id=1, source_target_pairs={{0,4},{4,0},{1,5},{5,1},{2,6},{6,2},{3,7},{7,3},{8,12},{12,8},{9,1... | collective-permute-start | bytes 3080 | tf_op jit(solution)/shard_map/ppermute | solution.py:232
  20.6 20.2 %all-to-all-done = bf16[8,9,16,128]{3,2,1,0:T(8,128)(2,1)S(1)} async-done(((bf16[8,9,16,128]{3,2,1,0:T(8,128)(2,1)}), bf16[8,9,16,128]{3,2,1,0:T(8,128)(2,1)S(1)}, u32[]{:S(2)}, u32[]{:S(2)}) %all-to-all-start) | async-done | bytes 294944 | tf_op jit(solution)/shard_map/all_to_all | solution.py:190
  41.7 4.3 %all-to-all-start.1 = ((bf16[4,4,8,16,128]{4,3,2,1,0:T(8,128)(2,1)}), bf16[4,4,8,16,128]{4,3,2,1,0:T(8,128)(2,1)S(1)}, u32[]{:S(2)}, u32[]{:S(2)}) async-start(bf16[4,4,8,16,128]{4,3,2,1,0:T(8,128)(2,1)} %broadcast_in_dim.17), calls=%async_computation.1 | async-start | bytes 1048576 | tf_op jit(solution)/shard_map/all_to_all | solution.py:200
  48.8 6.6 %all-to-all-done.1 = bf16[4,4,8,16,128]{4,3,2,1,0:T(8,128)(2,1)S(1)} async-done(((bf16[4,4,8,16,128]{4,3,2,1,0:T(8,128)(2,1)}), bf16[4,4,8,16,128]{4,3,2,1,0:T(8,128)(2,1)S(1)}, u32[]{:S(2)}, u32[]{:S(2)}) %all-to-all-start.1) | async-done | bytes 524320 | tf_op jit(solution)/shard_map/all_to_all | solution.py:200
  56.3 3.5 %all-to-all-start.3 = ((bf16[4,4,8,16,128]{4,3,2,1,0:T(8,128)(2,1)}), bf16[4,4,8,16,128]{4,3,2,1,0:T(8,128)(2,1)S(1)}, u32[]{:S(2)}, u32[]{:S(2)}) async-start(bf16[4,4,8,16,128]{4,3,2,1,0:T(8,128)(2,1)} %broadcast_in_dim.21), calls=%async_computation.3 | async-start | bytes 1048576 | tf_op jit(solution)/shard_map/all_to_all | solution.py:200
  61.9 6.1 %all-to-all-done.3 = bf16[4,4,8,16,128]{4,3,2,1,0:T(8,128)(2,1)S(1)} async-done(((bf16[4,4,8,16,128]{4,3,2,1,0:T(8,128)(2,1)}), bf16[4,4,8,16,128]{4,3,2,1,0:T(8,128)(2,1)S(1)}, u32[]{:S(2)}, u32[]{:S(2)}) %all-to-all-start.3) | async-done | bytes 524320 | tf_op jit(solution)/shard_map/all_to_all | solution.py:200
  68.0 2.9 %collective-permute-start.4 = (bf16[128,16,128]{2,1,0:T(8,128)(2,1)S(1)}, bf16[128,16,128]{2,1,0:T(8,128)(2,1)S(1)}, u32[]{:S(2)}, u32[]{:S(2)}) collective-permute-start(bf16[128,16,128]{2,1,0:T(8,128)(2,1)S(1)} %bitcast.50), channel_id=1, source_target_pairs={{0,8},{8,16},{16,24},{24,32},{32,40},{40,48},{48,56},{56,64},{64,7... | collective-permute-start | bytes 1572872 | tf_op jit(solution)/shard_map/ppermute | solution.py:209
  71.6 7.1 %all-to-all-start.2 = ((s32[64,1,8]{2,1,0:T(1,128)}), s32[64,1,8]{2,1,0:T(1,128)S(1)}, u32[]{:S(2)}, u32[]{:S(2)}) async-start(s32[64,1,8]{2,1,0:T(1,128)} %broadcast_in_dim.18), calls=%async_computation.2 | async-start | bytes 65536 | tf_op jit(solution)/shard_map/all_to_all | solution.py:237
  78.8 8.6 %all-to-all-done.2 = s32[64,1,8]{2,1,0:T(1,128)S(1)} async-done(((s32[64,1,8]{2,1,0:T(1,128)}), s32[64,1,8]{2,1,0:T(1,128)S(1)}, u32[]{:S(2)}, u32[]{:S(2)}) %all-to-all-start.2) | async-done | bytes 2080 | tf_op jit(solution)/shard_map/all_to_all | solution.py:237
  88.8 2.5 %collective-permute-start.6 = (bf16[128,16,128]{2,1,0:T(8,128)(2,1)S(1)}, bf16[128,16,128]{2,1,0:T(8,128)(2,1)S(1)}, u32[]{:S(2)}, u32[]{:S(2)}) collective-permute-start(bf16[128,16,128]{2,1,0:T(8,128)(2,1)S(1)} %bitcast.48), channel_id=1, source_target_pairs={{0,8},{8,16},{16,24},{24,32},{32,40},{40,48},{48,56},{56,64},{64,7... | collective-permute-start | bytes 1572872 | tf_op jit(solution)/shard_map/ppermute | solution.py:209
  91.3 3.4 %collective-permute-start.2 = (bf16[128,16,128]{2,1,0:T(8,128)(2,1)S(1)}, bf16[128,16,128]{2,1,0:T(8,128)(2,1)S(1)}, u32[]{:S(2)}, u32[]{:S(2)}) collective-permute-start(bf16[128,16,128]{2,1,0:T(8,128)(2,1)S(1)} %bitcast.51), channel_id=1, source_target_pairs={{0,120},{8,0},{16,8},{24,16},{32,24},{40,32},{48,40},{56,48},{64,5... | collective-permute-start | bytes 1572872 | tf_op jit(solution)/shard_map/ppermute | solution.py:212
  94.7 4.7 %collective-permute-start.3 = (bf16[128,16,128]{2,1,0:T(8,128)(2,1)S(1)}, bf16[128,16,128]{2,1,0:T(8,128)(2,1)S(1)}, u32[]{:S(2)}, u32[]{:S(2)}) collective-permute-start(bf16[128,16,128]{2,1,0:T(8,128)(2,1)S(1)} %collective-permute-done.1.refs_2_), channel_id=1, source_target_pairs={{0,120},{8,0},{16,8},{24,16},{32,24},{40,32},{48,40},{56,48},{64,5... | collective-permute-start | bytes 1572872 | tf_op jit(solution)/shard_map/ppermute | solution.py:212
  99.4 1.9 collective-permute-start.5
  101.7 5.6 %collective-permute-done.2.refs_3_ = bf16[128,16,128]{2,1,0:T(8,128)(2,1)S(1)} collective-permute-done((bf16[128,16,128]{2,1,0:T(8,128)(2,1)S(1)}, bf16[128,16,128]{2,1,0:T(8,128)(2,1)S(1)}, u32[]{:S(2)}, u32[]{:S(2)}) %collective-permute-start.2) | collective-permute-done | bytes 524320 | tf_op jit(solution)/shard_map/ppermute | solution.py:212
  107.3 5.6 %collective-permute-done.3.refs_4_ = bf16[128,16,128]{2,1,0:T(8,128)(2,1)S(1)} collective-permute-done((bf16[128,16,128]{2,1,0:T(8,128)(2,1)S(1)}, bf16[128,16,128]{2,1,0:T(8,128)(2,1)S(1)}, u32[]{:S(2)}, u32[]{:S(2)}) %collective-permute-start.3) | collective-permute-done | bytes 524320 | tf_op jit(solution)/shard_map/ppermute | solution.py:212
  112.9 10.9 %shard_map.128 = (bf16[128,16,128]{2,1,0:T(8,128)(2,1)S(1)}, bf16[128,16,128]{2,1,0:T(8,128)(2,1)S(1)}, bf16[128,16,128]{2,1,0:T(8,128)(2,1)S(1)}, bf16[128,16,1...) custom-call(s32[256]{0:T(256)S(1)} %fusion.19.where_ref, ...), custom_call_target="tpu_custom_call" | custom-call | flops 713031680 | bytes 12582912 | tf_op jit(solution)/shard_map/pallas_call | solution.py:131
  123.9 3.0 %collective-permute-start.11 = (bf16[128,16,128]{2,1,0:T(8,128)(2,1)S(1)}, bf16[128,16,128]{2,1,0:T(8,128)(2,1)S(1)}, u32[]{:S(2)}, u32[]{:S(2)}) collective-permute-start(bf16[128,16,128]{2,1,0:T(8,128)(2,1)S(1)} %get-tuple-element.32), channel_id=1, source_target_pairs={{0,8},{8,16},{16,24},{24,32},{32,40},{40,48},{48,56},{56,64},{64,7... | collective-permute-start | bytes 1572872 | tf_op jit(solution)/shard_map/ppermute | solution.py:209
  126.9 2.9 %collective-permute-start.14 = (bf16[128,16,128]{2,1,0:T(8,128)(2,1)S(1)}, bf16[128,16,128]{2,1,0:T(8,128)(2,1)S(1)}, u32[]{:S(2)}, u32[]{:S(2)}) collective-permute-start(bf16[128,16,128]{2,1,0:T(8,128)(2,1)S(1)} %get-tuple-element.36), channel_id=1, source_target_pairs={{0,120},{8,0},{16,8},{24,16},{32,24},{40,32},{48,40},{56,48},{64,5... | collective-permute-start | bytes 1572872 | tf_op jit(solution)/shard_map/ppermute | solution.py:212
  129.8 5.4 %collective-permute-start.10 = (bf16[128,16,128]{2,1,0:T(8,128)(2,1)S(1)}, bf16[128,16,128]{2,1,0:T(8,128)(2,1)S(1)}, u32[]{:S(2)}, u32[]{:S(2)}) collective-permute-start(bf16[128,16,128]{2,1,0:T(8,128)(2,1)S(1)} %get-tuple-element.30), channel_id=1, source_target_pairs={{0,120},{8,0},{16,8},{24,16},{32,24},{40,32},{48,40},{56,48},{64,5... | collective-permute-start | bytes 1572872 | tf_op jit(solution)/shard_map/ppermute | solution.py:212
  135.7 5.0 %collective-permute-start.12 = (bf16[128,16,128]{2,1,0:T(8,128)(2,1)S(1)}, bf16[128,16,128]{2,1,0:T(8,128)(2,1)S(1)}, u32[]{:S(2)}, u32[]{:S(2)}) collective-permute-start(bf16[128,16,128]{2,1,0:T(8,128)(2,1)S(1)} %add_convert_fusion.3), channel_id=1, source_target_pairs={{0,8},{8,16},{16,24},{24,32},{32,40},{40,48},{48,56},{56,64},{64,7... | collective-permute-start | bytes 1572872 | tf_op jit(solution)/shard_map/ppermute | solution.py:209
  140.7 4.4 %collective-permute-start.13 = (bf16[128,16,128]{2,1,0:T(8,128)(2,1)S(1)}, bf16[128,16,128]{2,1,0:T(8,128)(2,1)S(1)}, u32[]{:S(2)}, u32[]{:S(2)}) collective-permute-start(bf16[128,16,128]{2,1,0:T(8,128)(2,1)S(1)} %get-tuple-element.34), channel_id=1, source_target_pairs={{0,8},{8,16},{16,24},{24,32},{32,40},{40,48},{48,56},{56,64},{64,7... | collective-permute-start | bytes 1572872 | tf_op jit(solution)/shard_map/ppermute | solution.py:209
  145.3 2.4 %collective-permute-start.15 = (bf16[128,16,128]{2,1,0:T(8,128)(2,1)S(1)}, bf16[128,16,128]{2,1,0:T(8,128)(2,1)S(1)}, u32[]{:S(2)}, u32[]{:S(2)}) collective-permute-start(bf16[128,16,128]{2,1,0:T(8,128)(2,1)S(1)} %add_convert_fusion.1), channel_id=1, source_target_pairs={{0,120},{8,0},{16,8},{24,16},{32,24},{40,32},{48,40},{56,48},{64,5... | collective-permute-start | bytes 1572872 | tf_op jit(solution)/shard_map/ppermute | solution.py:212
  147.7 7.0 %collective-permute-done.10 = bf16[128,16,128]{2,1,0:T(8,128)(2,1)S(1)} collective-permute-done((bf16[128,16,128]{2,1,0:T(8,128)(2,1)S(1)}, bf16[128,16,128]{2,1,0:T(8,128)(2,1)S(1)}, u32[]{:S(2)}, u32[]{:S(2)}) %collective-permute-start.10) | collective-permute-done | bytes 524320 | tf_op jit(solution)/shard_map/ppermute | solution.py:212
  155.0 3.1 %collective-permute-done.13 = bf16[128,16,128]{2,1,0:T(8,128)(2,1)S(1)} collective-permute-done((bf16[128,16,128]{2,1,0:T(8,128)(2,1)S(1)}, bf16[128,16,128]{2,1,0:T(8,128)(2,1)S(1)}, u32[]{:S(2)}, u32[]{:S(2)}) %collective-permute-start.13) | collective-permute-done | bytes 524320 | tf_op jit(solution)/shard_map/ppermute | solution.py:209
  158.1 2.3 %collective-permute-done.15 = bf16[128,16,128]{2,1,0:T(8,128)(2,1)S(1)} collective-permute-done((bf16[128,16,128]{2,1,0:T(8,128)(2,1)S(1)}, bf16[128,16,128]{2,1,0:T(8,128)(2,1)S(1)}, u32[]{:S(2)}, u32[]{:S(2)}) %collective-permute-start.15) | collective-permute-done | bytes 524320 | tf_op jit(solution)/shard_map/ppermute | solution.py:212
  161.7 3.6 %all-to-all-start.4 = ((bf16[4,8,8,16,128]{4,3,2,1,0:T(8,128)(2,1)}), bf16[4,8,8,16,128]{4,3,2,1,0:T(8,128)(2,1)S(1)}, u32[]{:S(2)}, u32[]{:S(2)}) async-start(bf16[4,8,8,16,128]{4,3,2,1,0:T(8,128)(2,1)} %pad_maximum_fusion), calls=%async_computation.4 | async-start | bytes 2097152 | tf_op jit(solution)/shard_map/all_to_all | solution.py:279
  165.4 1.9 collective-permute-start.9
  167.3 2.4 %collective-permute-start.8 = (bf16[8,16,1024]{2,1,0:T(8,128)(2,1)S(1)}, bf16[8,16,1024]{2,1,0:T(8,128)(2,1)S(1)}, u32[]{:S(2)}, u32[]{:S(2)}) collective-permute-start(bf16[8,16,1024]{2,1,0:T(8,128)(2,1)S(1)} %copy-done.3), channel_id=1, source_target_pairs={{0,4},{4,0},{1,5},{5,1},{2,6},{6,2},{3,7},{7,3},{8,12},{12,8},{9,1... | collective-permute-start | bytes 786440 | tf_op jit(solution)/shard_map/ppermute | solution.py:288
  169.7 6.5 %all-to-all-done.4 = bf16[4,8,8,16,128]{4,3,2,1,0:T(8,128)(2,1)S(1)} async-done(((bf16[4,8,8,16,128]{4,3,2,1,0:T(8,128)(2,1)}), bf16[4,8,8,16,128]{4,3,2,1,0:T(8,128)(2,1)S(1)}, u32[]{:S(2)}, u32[]{:S(2)}) %all-to-all-start.4) | async-done | bytes 1048608 | tf_op jit(solution)/shard_map/all_to_all | solution.py:279
  177.0 7.1 %all-to-all-start.5 = ((bf16[8,8,16,128]{3,2,1,0:T(8,128)(2,1)}), bf16[8,8,16,128]{3,2,1,0:T(8,128)(2,1)S(1)}, u32[]{:S(2)}, u32[]{:S(2)}) async-start(bf16[8,8,16,128]{3,2,1,0:T(8,128)(2,1)} %fusion), calls=%async_computation.5 | async-start | bytes 524288 | tf_op jit(solution)/shard_map/all_to_all | solution.py:281
  186.3 19.6 %all-to-all-done.5 = bf16[8,8,16,128]{3,2,1,0:T(8,128)(2,1)S(1)} async-done(((bf16[8,8,16,128]{3,2,1,0:T(8,128)(2,1)}), bf16[8,8,16,128]{3,2,1,0:T(8,128)(2,1)S(1)}, u32[]{:S(2)}, u32[]{:S(2)}) %all-to-all-start.5) | async-done | bytes 262176 | tf_op jit(solution)/shard_map/all_to_all | solution.py:281
  (83 shorter events, 18.1 us)
Async XLA Ops:
  0.6 17.4 %copy-start.11 = (s32[8,16]{1,0:T(8,128)S(1)}, s32[8,16]{1,0:T(8,128)}, u32[]{:S(2)}) copy-start(s32[8,16]{1,0:T(8,128)} %param.15) | copy-start | bytes 1540
  0.6 17.4 %copy-start.10 = (s32[8,16]{1,0:T(8,128)S(1)}, s32[8,16]{1,0:T(8,128)}, u32[]{:S(2)}) copy-start(s32[8,16]{1,0:T(8,128)} %param.16) | copy-start | bytes 1540
  0.7 19.8 %copy-start.6 = (bf16[8,16,2048]{2,1,0:T(8,128)(2,1)S(1)}, bf16[8,16,2048]{2,1,0:T(8,128)(2,1)}, u32[]{:S(2)}) copy-start(bf16[8,16,2048]{2,1,0:T(8,128)(2,1)} %param.14) | copy-start | bytes 1572868
  0.7 19.8 %copy-start.7 = (bf16[8,16,2048]{2,1,0:T(8,128)(2,1)S(1)}, bf16[8,16,2048]{2,1,0:T(8,128)(2,1)}, u32[]{:S(2)}) copy-start(bf16[8,16,2048]{2,1,0:T(8,128)(2,1)} %param.9) | copy-start | bytes 1572868
  3.8 37.0 %all-to-all-start = ((bf16[8,9,16,128]{3,2,1,0:T(8,128)(2,1)}), bf16[8,9,16,128]{3,2,1,0:T(8,128)(2,1)S(1)}, u32[]{:S(2)}, u32[]{:S(2)}) async-start(bf16[8,9,16,128]{3,2,1,0:T(8,128)(2,1)} %bitcast.13), calls=%async_computation | async-start | bytes 589824 | tf_op jit(solution)/shard_map/all_to_all | solution.py:190
  18.0 41.8 %collective-permute-start = (s32[2,8,16]{2,1,0:T(8,128)S(1)}, s32[2,8,16]{2,1,0:T(8,128)S(1)}, u32[]{:S(2)}, u32[]{:S(2)}) collective-permute-start(s32[2,8,16]{2,1,0:T(8,128)S(1)} %pad_add_fusion), channel_id=1, source_target_pairs={{0,4},{4,0},{1,5},{5,1},{2,6},{6,2},{3,7},{7,3},{8,12},{12,8},{9,1... | collective-permute-start | bytes 3080 | tf_op jit(solution)/shard_map/ppermute | solution.py:232
  20.6 25.4 %copy-start.8 = (bf16[8,16,256]{2,1,0:T(8,128)(2,1)S(1)}, bf16[8,16,256]{2,1,0:T(8,128)(2,1)}, u32[]{:S(2)}) copy-start(bf16[8,16,256]{2,1,0:T(8,128)(2,1)} %param.11) | copy-start | bytes 196612
  20.6 25.4 %copy-start.9 = (bf16[8,16,256]{2,1,0:T(8,128)(2,1)S(1)}, bf16[8,16,256]{2,1,0:T(8,128)(2,1)}, u32[]{:S(2)}) copy-start(bf16[8,16,256]{2,1,0:T(8,128)(2,1)} %param.10) | copy-start | bytes 196612
  41.7 13.7 %all-to-all-start.1 = ((bf16[4,4,8,16,128]{4,3,2,1,0:T(8,128)(2,1)}), bf16[4,4,8,16,128]{4,3,2,1,0:T(8,128)(2,1)S(1)}, u32[]{:S(2)}, u32[]{:S(2)}) async-start(bf16[4,4,8,16,128]{4,3,2,1,0:T(8,128)(2,1)} %broadcast_in_dim.17), calls=%async_computation.1 | async-start | bytes 1048576 | tf_op jit(solution)/shard_map/all_to_all | solution.py:200
  46.9 54.8 %collective-permute-start.7 = (bf16[8,16,2304]{2,1,0:T(8,128)(2,1)}, bf16[8,16,2304]{2,1,0:T(8,128)(2,1)S(1)}, u32[]{:S(2)}, u32[]{:S(2)}) collective-permute-start(bf16[8,16,2304]{2,1,0:T(8,128)(2,1)} %pad_maximum_fusion.2), channel_id=1, source_target_pairs={{0,4},{4,0},{1,5},{5,1},{2,6},{6,2},{3,7},{7,3},{8,12},{12,8},{9,1... | collective-permute-start | bytes 1769480 | tf_op jit(solution)/shard_map/ppermute | solution.py:230
  56.3 11.7 %all-to-all-start.3 = ((bf16[4,4,8,16,128]{4,3,2,1,0:T(8,128)(2,1)}), bf16[4,4,8,16,128]{4,3,2,1,0:T(8,128)(2,1)S(1)}, u32[]{:S(2)}, u32[]{:S(2)}) async-start(bf16[4,4,8,16,128]{4,3,2,1,0:T(8,128)(2,1)} %broadcast_in_dim.21), calls=%async_computation.3 | async-start | bytes 1048576 | tf_op jit(solution)/shard_map/all_to_all | solution.py:200
  60.0 34.7 %collective-permute-start.1 = (bf16[128,16,128]{2,1,0:T(8,128)(2,1)S(1)}, bf16[128,16,128]{2,1,0:T(8,128)(2,1)S(1)}, u32[]{:S(2)}, u32[]{:S(2)}) collective-permute-start(bf16[128,16,128]{2,1,0:T(8,128)(2,1)S(1)} %bitcast.47), channel_id=1, source_target_pairs={{0,120},{8,0},{16,8},{24,16},{32,24},{40,32},{48,40},{56,48},{64,5... | collective-permute-start | bytes 1572872 | tf_op jit(solution)/shard_map/ppermute | solution.py:212
  68.0 31.4 %collective-permute-start.4 = (bf16[128,16,128]{2,1,0:T(8,128)(2,1)S(1)}, bf16[128,16,128]{2,1,0:T(8,128)(2,1)S(1)}, u32[]{:S(2)}, u32[]{:S(2)}) collective-permute-start(bf16[128,16,128]{2,1,0:T(8,128)(2,1)S(1)} %bitcast.50), channel_id=1, source_target_pairs={{0,8},{8,16},{16,24},{24,32},{32,40},{40,48},{48,56},{56,64},{64,7... | collective-permute-start | bytes 1572872 | tf_op jit(solution)/shard_map/ppermute | solution.py:209
  71.6 15.9 %all-to-all-start.2 = ((s32[64,1,8]{2,1,0:T(1,128)}), s32[64,1,8]{2,1,0:T(1,128)S(1)}, u32[]{:S(2)}, u32[]{:S(2)}) async-start(s32[64,1,8]{2,1,0:T(1,128)} %broadcast_in_dim.18), calls=%async_computation.2 | async-start | bytes 65536 | tf_op jit(solution)/shard_map/all_to_all | solution.py:237
  88.8 12.9 %collective-permute-start.6 = (bf16[128,16,128]{2,1,0:T(8,128)(2,1)S(1)}, bf16[128,16,128]{2,1,0:T(8,128)(2,1)S(1)}, u32[]{:S(2)}, u32[]{:S(2)}) collective-permute-start(bf16[128,16,128]{2,1,0:T(8,128)(2,1)S(1)} %bitcast.48), channel_id=1, source_target_pairs={{0,8},{8,16},{16,24},{24,32},{32,40},{40,48},{48,56},{56,64},{64,7... | collective-permute-start | bytes 1572872 | tf_op jit(solution)/shard_map/ppermute | solution.py:209
  91.3 16.1 %collective-permute-start.2 = (bf16[128,16,128]{2,1,0:T(8,128)(2,1)S(1)}, bf16[128,16,128]{2,1,0:T(8,128)(2,1)S(1)}, u32[]{:S(2)}, u32[]{:S(2)}) collective-permute-start(bf16[128,16,128]{2,1,0:T(8,128)(2,1)S(1)} %bitcast.51), channel_id=1, source_target_pairs={{0,120},{8,0},{16,8},{24,16},{32,24},{40,32},{48,40},{56,48},{64,5... | collective-permute-start | bytes 1572872 | tf_op jit(solution)/shard_map/ppermute | solution.py:212
  94.7 18.3 %collective-permute-start.3 = (bf16[128,16,128]{2,1,0:T(8,128)(2,1)S(1)}, bf16[128,16,128]{2,1,0:T(8,128)(2,1)S(1)}, u32[]{:S(2)}, u32[]{:S(2)}) collective-permute-start(bf16[128,16,128]{2,1,0:T(8,128)(2,1)S(1)} %collective-permute-done.1.refs_2_), channel_id=1, source_target_pairs={{0,120},{8,0},{16,8},{24,16},{32,24},{40,32},{48,40},{56,48},{64,5... | collective-permute-start | bytes 1572872 | tf_op jit(solution)/shard_map/ppermute | solution.py:212
  99.4 13.5 %collective-permute-start.5 = (bf16[128,16,128]{2,1,0:T(8,128)(2,1)S(1)}, bf16[128,16,128]{2,1,0:T(8,128)(2,1)S(1)}, u32[]{:S(2)}, u32[]{:S(2)}) collective-permute-start(bf16[128,16,128]{2,1,0:T(8,128)(2,1)S(1)} %collective-permute-done.4.refs_7_), channel_id=1, source_target_pairs={{0,8},{8,16},{16,24},{24,32},{32,40},{40,48},{48,56},{56,64},{64,7... | collective-permute-start | bytes 1572872 | tf_op jit(solution)/shard_map/ppermute | solution.py:209
  123.9 21.4 %copy-start = (bf16[8,16,256]{2,1,0:T(8,128)(2,1)}, bf16[8,16,256]{2,1,0:T(8,128)(2,1)S(1)}, u32[]{:S(2)}) copy-start(bf16[8,16,256]{2,1,0:T(8,128)(2,1)S(1)} %get-tuple-element.27) | copy-start | bytes 196612
  123.9 21.4 %copy-start.2 = (bf16[8,16,1024]{2,1,0:T(8,128)(2,1)}, bf16[8,16,1024]{2,1,0:T(8,128)(2,1)S(1)}, u32[]{:S(2)}) copy-start(bf16[8,16,1024]{2,1,0:T(8,128)(2,1)S(1)} %get-tuple-element.26) | copy-start | bytes 786436
  123.9 21.4 %copy-start.4 = (bf16[8,16,256]{2,1,0:T(8,128)(2,1)}, bf16[8,16,256]{2,1,0:T(8,128)(2,1)S(1)}, u32[]{:S(2)}) copy-start(bf16[8,16,256]{2,1,0:T(8,128)(2,1)S(1)} %get-tuple-element.28) | copy-start | bytes 196612
  123.9 11.6 %collective-permute-start.11 = (bf16[128,16,128]{2,1,0:T(8,128)(2,1)S(1)}, bf16[128,16,128]{2,1,0:T(8,128)(2,1)S(1)}, u32[]{:S(2)}, u32[]{:S(2)}) collective-permute-start(bf16[128,16,128]{2,1,0:T(8,128)(2,1)S(1)} %get-tuple-element.32), channel_id=1, source_target_pairs={{0,8},{8,16},{16,24},{24,32},{32,40},{40,48},{48,56},{56,64},{64,7... | collective-permute-start | bytes 1572872 | tf_op jit(solution)/shard_map/ppermute | solution.py:209
  126.9 18.2 %collective-permute-start.14 = (bf16[128,16,128]{2,1,0:T(8,128)(2,1)S(1)}, bf16[128,16,128]{2,1,0:T(8,128)(2,1)S(1)}, u32[]{:S(2)}, u32[]{:S(2)}) collective-permute-start(bf16[128,16,128]{2,1,0:T(8,128)(2,1)S(1)} %get-tuple-element.36), channel_id=1, source_target_pairs={{0,120},{8,0},{16,8},{24,16},{32,24},{40,32},{48,40},{56,48},{64,5... | collective-permute-start | bytes 1572872 | tf_op jit(solution)/shard_map/ppermute | solution.py:212
  129.8 25.0 %collective-permute-start.10 = (bf16[128,16,128]{2,1,0:T(8,128)(2,1)S(1)}, bf16[128,16,128]{2,1,0:T(8,128)(2,1)S(1)}, u32[]{:S(2)}, u32[]{:S(2)}) collective-permute-start(bf16[128,16,128]{2,1,0:T(8,128)(2,1)S(1)} %get-tuple-element.30), channel_id=1, source_target_pairs={{0,120},{8,0},{16,8},{24,16},{32,24},{40,32},{48,40},{56,48},{64,5... | collective-permute-start | bytes 1572872 | tf_op jit(solution)/shard_map/ppermute | solution.py:212
  135.7 19.1 %collective-permute-start.12 = (bf16[128,16,128]{2,1,0:T(8,128)(2,1)S(1)}, bf16[128,16,128]{2,1,0:T(8,128)(2,1)S(1)}, u32[]{:S(2)}, u32[]{:S(2)}) collective-permute-start(bf16[128,16,128]{2,1,0:T(8,128)(2,1)S(1)} %add_convert_fusion.3), channel_id=1, source_target_pairs={{0,8},{8,16},{16,24},{24,32},{32,40},{40,48},{48,56},{56,64},{64,7... | collective-permute-start | bytes 1572872 | tf_op jit(solution)/shard_map/ppermute | solution.py:209
  140.7 17.4 %collective-permute-start.13 = (bf16[128,16,128]{2,1,0:T(8,128)(2,1)S(1)}, bf16[128,16,128]{2,1,0:T(8,128)(2,1)S(1)}, u32[]{:S(2)}, u32[]{:S(2)}) collective-permute-start(bf16[128,16,128]{2,1,0:T(8,128)(2,1)S(1)} %get-tuple-element.34), channel_id=1, source_target_pairs={{0,8},{8,16},{16,24},{24,32},{32,40},{40,48},{48,56},{56,64},{64,7... | collective-permute-start | bytes 1572872 | tf_op jit(solution)/shard_map/ppermute | solution.py:209
  145.3 15.1 %collective-permute-start.15 = (bf16[128,16,128]{2,1,0:T(8,128)(2,1)S(1)}, bf16[128,16,128]{2,1,0:T(8,128)(2,1)S(1)}, u32[]{:S(2)}, u32[]{:S(2)}) collective-permute-start(bf16[128,16,128]{2,1,0:T(8,128)(2,1)S(1)} %add_convert_fusion.1), channel_id=1, source_target_pairs={{0,120},{8,0},{16,8},{24,16},{32,24},{40,32},{48,40},{56,48},{64,5... | collective-permute-start | bytes 1572872 | tf_op jit(solution)/shard_map/ppermute | solution.py:212
  161.7 14.5 %all-to-all-start.4 = ((bf16[4,8,8,16,128]{4,3,2,1,0:T(8,128)(2,1)}), bf16[4,8,8,16,128]{4,3,2,1,0:T(8,128)(2,1)S(1)}, u32[]{:S(2)}, u32[]{:S(2)}) async-start(bf16[4,8,8,16,128]{4,3,2,1,0:T(8,128)(2,1)} %pad_maximum_fusion), calls=%async_computation.4 | async-start | bytes 2097152 | tf_op jit(solution)/shard_map/all_to_all | solution.py:279
  165.3 18.8 %copy-start.1 = (bf16[8,16,256]{2,1,0:T(8,128)(2,1)S(1)}, bf16[8,16,256]{2,1,0:T(8,128)(2,1)}, u32[]{:S(2)}) copy-start(bf16[8,16,256]{2,1,0:T(8,128)(2,1)} %copy-done) | copy-start | bytes 196612
  165.4 18.7 %collective-permute-start.9 = (bf16[8,16,256]{2,1,0:T(8,128)(2,1)S(1)}, bf16[8,16,256]{2,1,0:T(8,128)(2,1)S(1)}, u32[]{:S(2)}, u32[]{:S(2)}) collective-permute-start(bf16[8,16,256]{2,1,0:T(8,128)(2,1)S(1)} %copy-done.5), channel_id=1, source_target_pairs={{0,4},{4,0},{1,5},{5,1},{2,6},{6,2},{3,7},{7,3},{8,12},{12,8},{9,1... | collective-permute-start | bytes 196616 | tf_op jit(solution)/shard_map/ppermute | solution.py:289
  167.3 18.1 %collective-permute-start.8 = (bf16[8,16,1024]{2,1,0:T(8,128)(2,1)S(1)}, bf16[8,16,1024]{2,1,0:T(8,128)(2,1)S(1)}, u32[]{:S(2)}, u32[]{:S(2)}) collective-permute-start(bf16[8,16,1024]{2,1,0:T(8,128)(2,1)S(1)} %copy-done.3), channel_id=1, source_target_pairs={{0,4},{4,0},{1,5},{5,1},{2,6},{6,2},{3,7},{7,3},{8,12},{12,8},{9,1... | collective-permute-start | bytes 786440 | tf_op jit(solution)/shard_map/ppermute | solution.py:288
  177.0 28.9 %all-to-all-start.5 = ((bf16[8,8,16,128]{3,2,1,0:T(8,128)(2,1)}), bf16[8,8,16,128]{3,2,1,0:T(8,128)(2,1)S(1)}, u32[]{:S(2)}, u32[]{:S(2)}) async-start(bf16[8,8,16,128]{3,2,1,0:T(8,128)(2,1)} %fusion), calls=%async_computation.5 | async-start | bytes 524288 | tf_op jit(solution)/shard_map/all_to_all | solution.py:281
  (2 other events, 9.3 us)

commit v4 on v3

--- a/solution.py
+++ b/solution.py
@@ -16,8 +16,10 @@
 XS, ZH, ZL, TP = 4, 4, 4, 4
 ZS = ZH * ZL
 TILES = 2 * P_DEV
-HALF = XS * ZH * TILES
+BLOCK = ZH * TILES
+HALF = XS * BLOCK
 PARTS = 2 * ZL
+CODES = TP * ZH * 2
 SCALE = HD ** (-0.5)
 SPAN = NB * LP
 BF = jnp.bfloat16
@@ -41,10 +43,15 @@
     outs = refs[PARTS + 2 : 2 * PARTS + 2]
     dq_mine, dq_other, self_mine, self_other = refs[2 * PARTS + 2 : 2 * PARTS + 6]
     store, grads, sem_in, sem_out = refs[2 * PARTS + 6 :]
-    loads = [
-        pltpu.make_async_copy(src, store.at[pl.ds(i * HALF, HALF)], sem_in.at[i])
-        for i, src in enumerate(stored)
-    ]
+    loads = []
+    for i, src in enumerate(stored):
+        pieces = [(0, 0, HALF)] if i % 2 == 0 else [(x * (BLOCK + 1), x * BLOCK, BLOCK) for x in range(XS)]
+        for start, to, size in pieces:
+            loads.append(
+                pltpu.make_async_copy(
+                    src.at[pl.ds(start, size)], store.at[pl.ds(i * HALF + to, size)], sem_in.at[len(loads)]
+                )
+            )
     for copy in loads:
         copy.start()
 
@@ -136,7 +143,7 @@
         scratch_shapes=[
             pltpu.VMEM((PARTS * HALF, LP, HD), BF),
             pltpu.VMEM((PARTS * HALF, LP, HD), BF),
-            pltpu.SemaphoreType.DMA((PARTS,)),
+            pltpu.SemaphoreType.DMA((ZL * (1 + XS),)),
             pltpu.SemaphoreType.DMA((PARTS,)),
         ],
         compiler_params=pltpu.CompilerParams(vmem_limit_bytes=40 * 2**20),
@@ -166,6 +173,7 @@
 ):
     core = lax.axis_index("core")
     my_zl = lax.axis_index("zl")
+    my_tp = lax.axis_index("tp")
     swap = ring(2, 1)
     around = ("zh", "zl")
     feat = GROUP * HD
@@ -196,14 +204,14 @@
     )
     far_halves = far.reshape(2, ZH, TILES + 1, LP, HD)
 
-    def along_x(h):
+    def along_x(block):
         return lax.all_to_all(
-            jnp.broadcast_to(far_halves[h][None, :, :TILES], (XS, ZH, TILES, LP, HD)),
+            jnp.broadcast_to(block[None], (XS,) + block.shape),
             "x",
             split_axis=0,
             concat_axis=0,
             tiled=True,
-        ).reshape(HALF, LP, HD)
+        ).reshape(-1, LP, HD)
 
     def up(part):
         return lax.ppermute(part, around, ring(ZS, 1))
@@ -211,9 +219,20 @@
     def down(part):
         return lax.ppermute(part, around, ring(ZS, -1))
 
-    s0a, s0b = along_x(0), along_x(1)
+    s0a = along_x(far_halves[0, :, :TILES].reshape(BLOCK, LP, HD))
+    codes = far[:, TILES, 0, :2].astype(jnp.int32)
+    known = codes[:, 0] * 16 + codes[:, 1]
+    all_known = jnp.concatenate(
+        [known] + [lax.ppermute(known, "tp", ring(TP, d)) for d in range(1, TP)]
+    )
+    coded = jnp.concatenate([all_known // 16, all_known % 16]).astype(BF)
+    spread_tile = jnp.pad(coded.reshape(1, 1, 2 * CODES), ((0, 0), (0, LP - 1), (0, HD - 2 * CODES)))
+    s0b = along_x(
+        jnp.concatenate([far_halves[1, :, :TILES].reshape(BLOCK, LP, HD), spread_tile], axis=0)
+    )
     s1a, s3a = down(s0a), up(s0a)
     s3b, s1b = up(s0b), down(s0b)
+    s2a, s2b = down(s1a), up(s3b)
 
     def pack(c):
         return jnp.concatenate(
@@ -231,18 +250,10 @@
     lists = jnp.stack([block_ids, block_valid])
     lists_other = lax.ppermute(lists, "core", swap)
 
-    codes = far[:, TILES, 0, :2].astype(jnp.int32)
-    known = codes[:, 0] * 16 + codes[:, 1]
-    known, _ = lax.optimization_barrier((known, s0a[:1, 0, :1]))
-    slot_of = lax.all_to_all(
-        jnp.broadcast_to(known[None], (XS * ZL * TP, 2 * ZH)),
-        ("x", "zl", "tp"),
-        split_axis=0,
-        concat_axis=0,
-        tiled=True,
-    ).reshape(-1)
-    s1a, slot_of = lax.optimization_barrier((s1a, slot_of))
-    s2a, s2b = down(s1a), up(s3b)
+    spread = jnp.concatenate(
+        [s.reshape(XS, BLOCK + 1, LP, HD)[:, BLOCK, 0, : 2 * CODES] for s in (s0b, s1b, s2b, s3b)]
+    ).astype(jnp.int32)
+    slot_of = (spread[:, :CODES] * 16 + spread[:, CODES:]).reshape(-1)
 
     def parts(number):
         pool = number // P_DEV
@@ -252,7 +263,7 @@
     ids = jnp.concatenate([block_ids, lists_other[0]]).reshape(-1)
     valid = jnp.concatenate([block_valid, lists_other[1]]).reshape(-1)
     x, zh, zl, c, inner = parts(ids)
-    id_at = (((x * ZL + zl) * TP + inner) * ZH + zh) * 2 + c
+    id_at = ((((zl - my_zl) % ZL * XS + x) * TP + (my_tp - inner) % TP) * ZH + zh) * 2 + c
     every = jnp.arange(slot_of.shape[0], dtype=jnp.int32)
     slots = jnp.sum(jnp.where(id_at[:, None] == every[None, :], slot_of[None, :], 0), axis=1)
     x, zh, zl, c, inner = parts(slots)
@@ -284,7 +295,6 @@
     key_grad = jnp.concatenate([grad[0, :, 0], grad[1, :, 0]], axis=2)
     value_grad = jnp.concatenate([grad[0, :, 1], grad[1, :, 1]], axis=2)
 
-    dq_other, self_other, _ = lax.optimization_barrier((dq_other, self_other, from_below_b[:1, 0, :1]))
     dq_taken = lax.ppermute(dq_other, "core", swap)
     self_taken = lax.ppermute(self_other, "core", swap)
     query_grad = by_core(dq_mine, dq_taken, 2)

time: 208 us -> 223 us (1.072)
  the two profiles are of different devices: /device:TPU:32 before, /device:TPU:1 now
where the time goes in v4:
time: 223 us; the launch traced here: 220 us
  starting transfers between devices  87.4 us (39%)
  waiting for transfers between devices  69.3 us (31%)
  blocking collectives  35.8 us (16%)
  Pallas kernels  13.2 us (6%)
  other arithmetic  7.72 us (3%)
  local copies, waits for them, and re-layouts  4.55 us (2%)
    all_to_all x1, blocking collectives, per_device(): lax.all_to_all(jnp.broadcast_to(heads[None], (ZH, 2, TILES + 1, LP, HD))....  35.8 us
    ppermute x6, waiting for transfers between devices, down(): return lax.ppermute(part, around, ring(ZS, -1))  22.6 us
    ppermute x6, waiting for transfers between devices, up(): return lax.ppermute(part, around, ring(ZS, 1))  21.5 us
    ppermute x6, starting transfers between devices, up(): return lax.ppermute(part, around, ring(ZS, 1))  19.1 us
    ppermute x6, starting transfers between devices, down(): return lax.ppermute(part, around, ring(ZS, -1))  17 us
    all_to_all x1, waiting for transfers between devices, per_device(): lax.all_to_all(x_sum, ('zh', 'core'), split_axis=0, concat_axis=0, tiled=...  15.1 us
    pallas_call x1, Pallas kernels, attention(): pl.pallas_call(attention_kernel, out_shape=(tiles,) * PARTS + (query, que...  13.2 us
    ppermute x3, starting transfers between devices, per_device(): lax.ppermute(known, 'tp', ring(TP, d))  9.49 us
  transfers between devices with their start and end apart: 23, of which 13 were waited for; matrix products, arithmetic and copies ran while one was open for 3% of the time, Pallas kernels for 0%

profile of v4, /device:TPU:1, one launch (start us, length us, event | category | flops | bytes accessed | tf_op | source)
XLA Modules:
  0.0 219.8 jit_solution(9201030759630495903)
XLA Ops:
  3.0 35.8 %all_to_all.25 = bf16[8,9,16,128]{3,2,1,0:T(8,128)(2,1)S(1)} all-to-all(bf16[8,9,16,128]{3,2,1,0:T(8,128)(2,1)S(1)} %bitcast.79), channel_id=1, replica_groups=mesh['x'=4,'zh'=4,'zl'=4,'core'=2,'tp'=4] {'zh','core'}, dimensions={0} | all-to-all | bytes 589824 | tf_op jit(solution)/shard_map/all_to_all | solution.py:198
  38.8 4.6 %collective-permute-start.3 = (s32[8]{0:T(128)S(1)}, s32[8]{0:T(128)S(1)}, u32[]{:S(2)}, u32[]{:S(2)}) collective-permute-start(s32[8]{0:T(128)S(1)} %add_bitcast_fusion), channel_id=1, source_target_pairs={{0,3},{1,0},{2,1},{3,2},{4,7},{5,4},{6,5},{7,6},{8,11},{9,8},{10,9... | collective-permute-start | bytes 104 | tf_op jit(solution)/shard_map/ppermute | solution.py:226
  43.5 2.3 %collective-permute-start.2 = (s32[8]{0:T(128)S(1)}, s32[8]{0:T(128)S(1)}, u32[]{:S(2)}, u32[]{:S(2)}) collective-permute-start(s32[8]{0:T(128)S(1)} %add_bitcast_fusion), channel_id=1, source_target_pairs={{0,2},{1,3},{2,0},{3,1},{4,6},{5,7},{6,4},{7,5},{8,10},{9,11},{10,... | collective-permute-start | bytes 104 | tf_op jit(solution)/shard_map/ppermute | solution.py:226
  45.7 2.6 %collective-permute-start.1 = (s32[8]{0:T(128)S(1)}, s32[8]{0:T(128)S(1)}, u32[]{:S(2)}, u32[]{:S(2)}) collective-permute-start(s32[8]{0:T(128)S(1)} %add_bitcast_fusion), channel_id=1, source_target_pairs={{0,1},{1,2},{2,3},{3,0},{4,5},{5,6},{6,7},{7,4},{8,9},{9,10},{10,1... | collective-permute-start | bytes 104 | tf_op jit(solution)/shard_map/ppermute | solution.py:226
  49.3 2.0 collective-permute-done.1
  52.4 4.0 %all-to-all-start.1 = ((bf16[4,33,16,128]{3,2,1,0:T(8,128)(2,1)}), bf16[4,33,16,128]{3,2,1,0:T(8,128)(2,1)S(1)}, u32[]{:S(2)}, u32[]{:S(2)}) async-start(bf16[4,33,16,128]{3,2,1,0:T(8,128)(2,1)} %broadcast_in_dim.36), calls=%async_computation.1 | async-start | bytes 1081344 | tf_op jit(solution)/shard_map/all_to_all | solution.py:208
  56.4 4.6 %collective-permute-start = (s32[2,8,16]{2,1,0:T(8,128)S(1)}, s32[2,8,16]{2,1,0:T(8,128)S(1)}, u32[]{:S(2)}, u32[]{:S(2)}) collective-permute-start(s32[2,8,16]{2,1,0:T(8,128)S(1)} %pad_add_fusion), channel_id=1, source_target_pairs={{0,4},{4,0},{1,5},{5,1},{2,6},{6,2},{3,7},{7,3},{8,12},{12,8},{9,1... | collective-permute-start | bytes 3080 | tf_op jit(solution)/shard_map/ppermute | solution.py:251
  61.2 2.2 all-to-all-done.1
  64.3 3.5 %all-to-all-start.2 = ((bf16[4,32,16,128]{3,2,1,0:T(8,128)(2,1)}), bf16[4,32,16,128]{3,2,1,0:T(8,128)(2,1)S(1)}, u32[]{:S(2)}, u32[]{:S(2)}) async-start(bf16[4,32,16,128]{3,2,1,0:T(8,128)(2,1)} %broadcast_in_dim.41), calls=%async_computation.2 | async-start | bytes 1048576 | tf_op jit(solution)/shard_map/all_to_all | solution.py:208
  67.7 6.2 %collective-permute-start.5 = (bf16[132,16,128]{2,1,0:T(8,128)(2,1)S(1)}, bf16[132,16,128]{2,1,0:T(8,128)(2,1)S(1)}, u32[]{:S(2)}, u32[]{:S(2)}) collective-permute-start(bf16[132,16,128]{2,1,0:T(8,128)(2,1)S(1)} %bitcast.69), channel_id=1, source_target_pairs={{0,8},{8,16},{16,24},{24,32},{32,40},{40,48},{48,56},{56,64},{64,7... | collective-permute-start | bytes 1622024 | tf_op jit(solution)/shard_map/ppermute | solution.py:217
  74.8 6.2 %collective-permute-start.10 = (bf16[8,16,2304]{2,1,0:T(8,128)(2,1)}, bf16[8,16,2304]{2,1,0:T(8,128)(2,1)S(1)}, u32[]{:S(2)}, u32[]{:S(2)}) collective-permute-start(bf16[8,16,2304]{2,1,0:T(8,128)(2,1)} %pad_maximum_fusion.2), channel_id=1, source_target_pairs={{0,4},{4,0},{1,5},{5,1},{2,6},{6,2},{3,7},{7,3},{8,12},{12,8},{9,1... | collective-permute-start | bytes 1769480 | tf_op jit(solution)/shard_map/ppermute | solution.py:249
  83.0 2.2 %collective-permute-start.4 = (bf16[132,16,128]{2,1,0:T(8,128)(2,1)S(1)}, bf16[132,16,128]{2,1,0:T(8,128)(2,1)S(1)}, u32[]{:S(2)}, u32[]{:S(2)}) collective-permute-start(bf16[132,16,128]{2,1,0:T(8,128)(2,1)S(1)} %bitcast.70), channel_id=1, source_target_pairs={{0,120},{8,0},{16,8},{24,16},{32,24},{40,32},{48,40},{56,48},{64,5... | collective-permute-start | bytes 1622024 | tf_op jit(solution)/shard_map/ppermute | solution.py:220
  85.2 3.0 %collective-permute-start.6 = (bf16[132,16,128]{2,1,0:T(8,128)(2,1)S(1)}, bf16[132,16,128]{2,1,0:T(8,128)(2,1)}, u32[]{:S(2)}, u32[]{:S(2)}) collective-permute-start(bf16[132,16,128]{2,1,0:T(8,128)(2,1)S(1)} %collective-permute-done.5.refs_7_), channel_id=1, source_target_pairs={{0,8},{8,16},{16,24},{24,32},{32,40},{40,48},{48,56},{56,64},{64,7... | collective-permute-start | bytes 1622024 | tf_op jit(solution)/shard_map/ppermute | solution.py:217
  88.6 3.4 %collective-permute-start.9 = (bf16[128,16,128]{2,1,0:T(8,128)(2,1)S(1)}, bf16[128,16,128]{2,1,0:T(8,128)(2,1)}, u32[]{:S(2)}, u32[]{:S(2)}) collective-permute-start(bf16[128,16,128]{2,1,0:T(8,128)(2,1)S(1)} %bitcast.73), channel_id=1, source_target_pairs={{0,8},{8,16},{16,24},{24,32},{32,40},{40,48},{48,56},{56,64},{64,7... | collective-permute-start | bytes 1572872 | tf_op jit(solution)/shard_map/ppermute | solution.py:217
  91.9 3.3 %collective-permute-done.7.refs_2_ = bf16[128,16,128]{2,1,0:T(8,128)(2,1)} collective-permute-done((bf16[128,16,128]{2,1,0:T(8,128)(2,1)S(1)}, bf16[128,16,128]{2,1,0:T(8,128)(2,1)}, u32[]{:S(2)}, u32[]{:S(2)}) %collective-permute-start.7) | collective-permute-done | bytes 524320 | tf_op jit(solution)/shard_map/ppermute | solution.py:220
  95.2 2.5 %collective-permute-start.8 = (bf16[128,16,128]{2,1,0:T(8,128)(2,1)}, bf16[128,16,128]{2,1,0:T(8,128)(2,1)}, u32[]{:S(2)}, u32[]{:S(2)}) collective-permute-start(bf16[128,16,128]{2,1,0:T(8,128)(2,1)} %collective-permute-done.7.refs_2_), channel_id=1, source_target_pairs={{0,120},{8,0},{16,8},{24,16},{32,24},{40,32},{48,40},{56,48},{64,5... | collective-permute-start | bytes 1572872 | tf_op jit(solution)/shard_map/ppermute | solution.py:220
  97.8 9.0 %collective-permute-done.4.refs_3_ = bf16[132,16,128]{2,1,0:T(8,128)(2,1)S(1)} collective-permute-done((bf16[132,16,128]{2,1,0:T(8,128)(2,1)S(1)}, bf16[132,16,128]{2,1,0:T(8,128)(2,1)S(1)}, u32[]{:S(2)}, u32[]{:S(2)}) %collective-permute-start.4) | collective-permute-done | bytes 540704 | tf_op jit(solution)/shard_map/ppermute | solution.py:220
  108.0 3.2 %collective-permute-done.9.refs_6_ = bf16[128,16,128]{2,1,0:T(8,128)(2,1)} collective-permute-done((bf16[128,16,128]{2,1,0:T(8,128)(2,1)S(1)}, bf16[128,16,128]{2,1,0:T(8,128)(2,1)}, u32[]{:S(2)}, u32[]{:S(2)}) %collective-permute-start.9) | collective-permute-done | bytes 524320 | tf_op jit(solution)/shard_map/ppermute | solution.py:217
  111.1 6.9 %collective-permute-done.8.refs_4_ = bf16[128,16,128]{2,1,0:T(8,128)(2,1)} collective-permute-done((bf16[128,16,128]{2,1,0:T(8,128)(2,1)}, bf16[128,16,128]{2,1,0:T(8,128)(2,1)}, u32[]{:S(2)}, u32[]{:S(2)}) %collective-permute-start.8) | collective-permute-done | bytes 524320 | tf_op jit(solution)/shard_map/ppermute | solution.py:220
  118.0 13.2 %shard_map.128 = (bf16[128,16,128]{2,1,0:T(8,128)(2,1)S(1)}, bf16[128,16,128]{2,1,0:T(8,128)(2,1)S(1)}, bf16[128,16,128]{2,1,0:T(8,128)(2,1)S(1)}, bf16[128,16,1...) custom-call(s32[256]{0:T(256)S(1)} %fusion.28.where_ref, ...), custom_call_target="tpu_custom_call" | custom-call | flops 713031680 | bytes 12582912 | tf_op jit(solution)/shard_map/pallas_call | solution.py:138
  131.3 2.6 %collective-permute-start.14 = (bf16[128,16,128]{2,1,0:T(8,128)(2,1)S(1)}, bf16[128,16,128]{2,1,0:T(8,128)(2,1)S(1)}, u32[]{:S(2)}, u32[]{:S(2)}) collective-permute-start(bf16[128,16,128]{2,1,0:T(8,128)(2,1)S(1)} %get-tuple-element.24), channel_id=1, source_target_pairs={{0,8},{8,16},{16,24},{24,32},{32,40},{40,48},{48,56},{56,64},{64,7... | collective-permute-start | bytes 1572872 | tf_op jit(solution)/shard_map/ppermute | solution.py:217
  133.9 3.9 %collective-permute-start.17 = (bf16[128,16,128]{2,1,0:T(8,128)(2,1)S(1)}, bf16[128,16,128]{2,1,0:T(8,128)(2,1)S(1)}, u32[]{:S(2)}, u32[]{:S(2)}) collective-permute-start(bf16[128,16,128]{2,1,0:T(8,128)(2,1)S(1)} %get-tuple-element.28), channel_id=1, source_target_pairs={{0,120},{8,0},{16,8},{24,16},{32,24},{40,32},{48,40},{56,48},{64,5... | collective-permute-start | bytes 1572872 | tf_op jit(solution)/shard_map/ppermute | solution.py:220
  139.7 5.9 %collective-permute-done.14 = bf16[128,16,128]{2,1,0:T(8,128)(2,1)S(1)} collective-permute-done((bf16[128,16,128]{2,1,0:T(8,128)(2,1)S(1)}, bf16[128,16,128]{2,1,0:T(8,128)(2,1)S(1)}, u32[]{:S(2)}, u32[]{:S(2)}) %collective-permute-start.14) | collective-permute-done | bytes 524320 | tf_op jit(solution)/shard_map/ppermute | solution.py:217
  149.8 4.6 %collective-permute-start.18 = (bf16[128,16,128]{2,1,0:T(8,128)(2,1)S(1)}, bf16[128,16,128]{2,1,0:T(8,128)(2,1)S(1)}, u32[]{:S(2)}, u32[]{:S(2)}) collective-permute-start(bf16[128,16,128]{2,1,0:T(8,128)(2,1)S(1)} %add_convert_fusion.1), channel_id=1, source_target_pairs={{0,120},{8,0},{16,8},{24,16},{32,24},{40,32},{48,40},{56,48},{64,5... | collective-permute-start | bytes 1572872 | tf_op jit(solution)/shard_map/ppermute | solution.py:220
  154.3 3.4 %collective-permute-done.13 = bf16[128,16,128]{2,1,0:T(8,128)(2,1)S(1)} collective-permute-done((bf16[128,16,128]{2,1,0:T(8,128)(2,1)S(1)}, bf16[128,16,128]{2,1,0:T(8,128)(2,1)S(1)}, u32[]{:S(2)}, u32[]{:S(2)}) %collective-permute-start.13) | collective-permute-done | bytes 524320 | tf_op jit(solution)/shard_map/ppermute | solution.py:220
  159.3 11.0 %collective-permute-done.16 = bf16[128,16,128]{2,1,0:T(8,128)(2,1)S(1)} collective-permute-done((bf16[128,16,128]{2,1,0:T(8,128)(2,1)S(1)}, bf16[128,16,128]{2,1,0:T(8,128)(2,1)S(1)}, u32[]{:S(2)}, u32[]{:S(2)}) %collective-permute-start.16) | collective-permute-done | bytes 524320 | tf_op jit(solution)/shard_map/ppermute | solution.py:217
  171.7 8.9 %all-to-all-start.3 = ((bf16[4,8,8,16,128]{4,3,2,1,0:T(8,128)(2,1)}), bf16[4,8,8,16,128]{4,3,2,1,0:T(8,128)(2,1)S(1)}, u32[]{:S(2)}, u32[]{:S(2)}) async-start(bf16[4,8,8,16,128]{4,3,2,1,0:T(8,128)(2,1)} %pad_maximum_fusion), calls=%async_computation.3 | async-start | bytes 2097152 | tf_op jit(solution)/shard_map/all_to_all | solution.py:290
  180.6 4.8 %collective-permute-start.12 = (bf16[8,16,256]{2,1,0:T(8,128)(2,1)S(1)}, bf16[8,16,256]{2,1,0:T(8,128)(2,1)S(1)}, u32[]{:S(2)}, u32[]{:S(2)}) collective-permute-start(bf16[8,16,256]{2,1,0:T(8,128)(2,1)S(1)} %get-tuple-element.20), channel_id=1, source_target_pairs={{0,4},{4,0},{1,5},{5,1},{2,6},{6,2},{3,7},{7,3},{8,12},{12,8},{9,1... | collective-permute-start | bytes 196616 | tf_op jit(solution)/shard_map/ppermute | solution.py:299
  185.4 2.1 collective-permute-start.11
  187.4 5.1 %all-to-all-done.3 = bf16[4,8,8,16,128]{4,3,2,1,0:T(8,128)(2,1)S(1)} async-done(((bf16[4,8,8,16,128]{4,3,2,1,0:T(8,128)(2,1)}), bf16[4,8,8,16,128]{4,3,2,1,0:T(8,128)(2,1)S(1)}, u32[]{:S(2)}, u32[]{:S(2)}) %all-to-all-start.3) | async-done | bytes 1048608 | tf_op jit(solution)/shard_map/all_to_all | solution.py:290
  193.4 7.8 %all-to-all-start.4 = ((bf16[8,8,16,128]{3,2,1,0:T(8,128)(2,1)}), bf16[8,8,16,128]{3,2,1,0:T(8,128)(2,1)S(1)}, u32[]{:S(2)}, u32[]{:S(2)}) async-start(bf16[8,8,16,128]{3,2,1,0:T(8,128)(2,1)} %fusion), calls=%async_computation.4 | async-start | bytes 524288 | tf_op jit(solution)/shard_map/all_to_all | solution.py:292
  203.4 15.1 %all-to-all-done.4 = bf16[8,8,16,128]{3,2,1,0:T(8,128)(2,1)S(1)} async-done(((bf16[8,8,16,128]{3,2,1,0:T(8,128)(2,1)}), bf16[8,8,16,128]{3,2,1,0:T(8,128)(2,1)S(1)}, u32[]{:S(2)}, u32[]{:S(2)}) %all-to-all-start.4) | async-done | bytes 262176 | tf_op jit(solution)/shard_map/all_to_all | solution.py:292
  (93 shorter events, 22.2 us)
Async XLA Ops:
  38.8 9.6 %collective-permute-start.3 = (s32[8]{0:T(128)S(1)}, s32[8]{0:T(128)S(1)}, u32[]{:S(2)}, u32[]{:S(2)}) collective-permute-start(s32[8]{0:T(128)S(1)} %add_bitcast_fusion), channel_id=1, source_target_pairs={{0,3},{1,0},{2,1},{3,2},{4,7},{5,4},{6,5},{7,6},{8,11},{9,8},{10,9... | collective-permute-start | bytes 104 | tf_op jit(solution)/shard_map/ppermute | solution.py:226
  43.5 5.8 %collective-permute-start.2 = (s32[8]{0:T(128)S(1)}, s32[8]{0:T(128)S(1)}, u32[]{:S(2)}, u32[]{:S(2)}) collective-permute-start(s32[8]{0:T(128)S(1)} %add_bitcast_fusion), channel_id=1, source_target_pairs={{0,2},{1,3},{2,0},{3,1},{4,6},{5,7},{6,4},{7,5},{8,10},{9,11},{10,... | collective-permute-start | bytes 104 | tf_op jit(solution)/shard_map/ppermute | solution.py:226
  45.7 5.5 %collective-permute-start.1 = (s32[8]{0:T(128)S(1)}, s32[8]{0:T(128)S(1)}, u32[]{:S(2)}, u32[]{:S(2)}) collective-permute-start(s32[8]{0:T(128)S(1)} %add_bitcast_fusion), channel_id=1, source_target_pairs={{0,1},{1,2},{2,3},{3,0},{4,5},{5,6},{6,7},{7,4},{8,9},{9,10},{10,1... | collective-permute-start | bytes 104 | tf_op jit(solution)/shard_map/ppermute | solution.py:226
  48.4 8.0 %copy-start.8 = (s32[8,16]{1,0:T(8,128)S(1)}, s32[8,16]{1,0:T(8,128)}, u32[]{:S(2)}) copy-start(s32[8,16]{1,0:T(8,128)} %param.16) | copy-start | bytes 1540
  51.3 9.7 %copy-start.6 = (bf16[8,16,256]{2,1,0:T(8,128)(2,1)S(1)}, bf16[8,16,256]{2,1,0:T(8,128)(2,1)}, u32[]{:S(2)}) copy-start(bf16[8,16,256]{2,1,0:T(8,128)(2,1)} %param.11) | copy-start | bytes 196612
  51.4 9.7 %copy-start.7 = (bf16[8,16,256]{2,1,0:T(8,128)(2,1)S(1)}, bf16[8,16,256]{2,1,0:T(8,128)(2,1)}, u32[]{:S(2)}) copy-start(bf16[8,16,256]{2,1,0:T(8,128)(2,1)} %param.10) | copy-start | bytes 196612
  51.5 9.6 %copy-start.4 = (bf16[8,16,2048]{2,1,0:T(8,128)(2,1)S(1)}, bf16[8,16,2048]{2,1,0:T(8,128)(2,1)}, u32[]{:S(2)}) copy-start(bf16[8,16,2048]{2,1,0:T(8,128)(2,1)} %param.14) | copy-start | bytes 1572868
  51.5 9.6 %copy-start.5 = (bf16[8,16,2048]{2,1,0:T(8,128)(2,1)S(1)}, bf16[8,16,2048]{2,1,0:T(8,128)(2,1)}, u32[]{:S(2)}) copy-start(bf16[8,16,2048]{2,1,0:T(8,128)(2,1)} %param.9) | copy-start | bytes 1572868
  52.4 11.0 %all-to-all-start.1 = ((bf16[4,33,16,128]{3,2,1,0:T(8,128)(2,1)}), bf16[4,33,16,128]{3,2,1,0:T(8,128)(2,1)S(1)}, u32[]{:S(2)}, u32[]{:S(2)}) async-start(bf16[4,33,16,128]{3,2,1,0:T(8,128)(2,1)} %broadcast_in_dim.36), calls=%async_computation.1 | async-start | bytes 1081344 | tf_op jit(solution)/shard_map/all_to_all | solution.py:208
  56.4 31.9 %collective-permute-start = (s32[2,8,16]{2,1,0:T(8,128)S(1)}, s32[2,8,16]{2,1,0:T(8,128)S(1)}, u32[]{:S(2)}, u32[]{:S(2)}) collective-permute-start(s32[2,8,16]{2,1,0:T(8,128)S(1)} %pad_add_fusion), channel_id=1, source_target_pairs={{0,4},{4,0},{1,5},{5,1},{2,6},{6,2},{3,7},{7,3},{8,12},{12,8},{9,1... | collective-permute-start | bytes 3080 | tf_op jit(solution)/shard_map/ppermute | solution.py:251
  64.3 16.8 %all-to-all-start.2 = ((bf16[4,32,16,128]{3,2,1,0:T(8,128)(2,1)}), bf16[4,32,16,128]{3,2,1,0:T(8,128)(2,1)S(1)}, u32[]{:S(2)}, u32[]{:S(2)}) async-start(bf16[4,32,16,128]{3,2,1,0:T(8,128)(2,1)} %broadcast_in_dim.41), calls=%async_computation.2 | async-start | bytes 1048576 | tf_op jit(solution)/shard_map/all_to_all | solution.py:208
  67.7 17.5 %collective-permute-start.5 = (bf16[132,16,128]{2,1,0:T(8,128)(2,1)S(1)}, bf16[132,16,128]{2,1,0:T(8,128)(2,1)S(1)}, u32[]{:S(2)}, u32[]{:S(2)}) collective-permute-start(bf16[132,16,128]{2,1,0:T(8,128)(2,1)S(1)} %bitcast.69), channel_id=1, source_target_pairs={{0,8},{8,16},{16,24},{24,32},{32,40},{40,48},{48,56},{56,64},{64,7... | collective-permute-start | bytes 1622024 | tf_op jit(solution)/shard_map/ppermute | solution.py:217
  74.8 33.2 %collective-permute-start.10 = (bf16[8,16,2304]{2,1,0:T(8,128)(2,1)}, bf16[8,16,2304]{2,1,0:T(8,128)(2,1)S(1)}, u32[]{:S(2)}, u32[]{:S(2)}) collective-permute-start(bf16[8,16,2304]{2,1,0:T(8,128)(2,1)} %pad_maximum_fusion.2), channel_id=1, source_target_pairs={{0,4},{4,0},{1,5},{5,1},{2,6},{6,2},{3,7},{7,3},{8,12},{12,8},{9,1... | collective-permute-start | bytes 1769480 | tf_op jit(solution)/shard_map/ppermute | solution.py:249
  81.1 14.1 %collective-permute-start.7 = (bf16[128,16,128]{2,1,0:T(8,128)(2,1)S(1)}, bf16[128,16,128]{2,1,0:T(8,128)(2,1)}, u32[]{:S(2)}, u32[]{:S(2)}) collective-permute-start(bf16[128,16,128]{2,1,0:T(8,128)(2,1)S(1)} %bitcast.72), channel_id=1, source_target_pairs={{0,120},{8,0},{16,8},{24,16},{32,24},{40,32},{48,40},{56,48},{64,5... | collective-permute-start | bytes 1572872 | tf_op jit(solution)/shard_map/ppermute | solution.py:220
  83.0 23.8 %collective-permute-start.4 = (bf16[132,16,128]{2,1,0:T(8,128)(2,1)S(1)}, bf16[132,16,128]{2,1,0:T(8,128)(2,1)S(1)}, u32[]{:S(2)}, u32[]{:S(2)}) collective-permute-start(bf16[132,16,128]{2,1,0:T(8,128)(2,1)S(1)} %bitcast.70), channel_id=1, source_target_pairs={{0,120},{8,0},{16,8},{24,16},{32,24},{40,32},{48,40},{56,48},{64,5... | collective-permute-start | bytes 1622024 | tf_op jit(solution)/shard_map/ppermute | solution.py:220
  85.2 21.6 %collective-permute-start.6 = (bf16[132,16,128]{2,1,0:T(8,128)(2,1)S(1)}, bf16[132,16,128]{2,1,0:T(8,128)(2,1)}, u32[]{:S(2)}, u32[]{:S(2)}) collective-permute-start(bf16[132,16,128]{2,1,0:T(8,128)(2,1)S(1)} %collective-permute-done.5.refs_7_), channel_id=1, source_target_pairs={{0,8},{8,16},{16,24},{24,32},{32,40},{40,48},{48,56},{56,64},{64,7... | collective-permute-start | bytes 1622024 | tf_op jit(solution)/shard_map/ppermute | solution.py:217
  88.6 22.6 %collective-permute-start.9 = (bf16[128,16,128]{2,1,0:T(8,128)(2,1)S(1)}, bf16[128,16,128]{2,1,0:T(8,128)(2,1)}, u32[]{:S(2)}, u32[]{:S(2)}) collective-permute-start(bf16[128,16,128]{2,1,0:T(8,128)(2,1)S(1)} %bitcast.73), channel_id=1, source_target_pairs={{0,8},{8,16},{16,24},{24,32},{32,40},{40,48},{48,56},{56,64},{64,7... | collective-permute-start | bytes 1572872 | tf_op jit(solution)/shard_map/ppermute | solution.py:217
  95.2 22.8 %collective-permute-start.8 = (bf16[128,16,128]{2,1,0:T(8,128)(2,1)}, bf16[128,16,128]{2,1,0:T(8,128)(2,1)}, u32[]{:S(2)}, u32[]{:S(2)}) collective-permute-start(bf16[128,16,128]{2,1,0:T(8,128)(2,1)} %collective-permute-done.7.refs_2_), channel_id=1, source_target_pairs={{0,120},{8,0},{16,8},{24,16},{32,24},{40,32},{48,40},{56,48},{64,5... | collective-permute-start | bytes 1572872 | tf_op jit(solution)/shard_map/ppermute | solution.py:220
  131.2 18.5 %copy-start = (bf16[8,16,1024]{2,1,0:T(8,128)(2,1)}, bf16[8,16,1024]{2,1,0:T(8,128)(2,1)S(1)}, u32[]{:S(2)}) copy-start(bf16[8,16,1024]{2,1,0:T(8,128)(2,1)S(1)} %get-tuple-element.17) | copy-start | bytes 786436
  131.2 18.5 %copy-start.2 = (bf16[8,16,1024]{2,1,0:T(8,128)(2,1)}, bf16[8,16,1024]{2,1,0:T(8,128)(2,1)S(1)}, u32[]{:S(2)}) copy-start(bf16[8,16,1024]{2,1,0:T(8,128)(2,1)S(1)} %get-tuple-element.18) | copy-start | bytes 786436
  131.3 14.3 %collective-permute-start.14 = (bf16[128,16,128]{2,1,0:T(8,128)(2,1)S(1)}, bf16[128,16,128]{2,1,0:T(8,128)(2,1)S(1)}, u32[]{:S(2)}, u32[]{:S(2)}) collective-permute-start(bf16[128,16,128]{2,1,0:T(8,128)(2,1)S(1)} %get-tuple-element.24), channel_id=1, source_target_pairs={{0,8},{8,16},{16,24},{24,32},{32,40},{40,48},{48,56},{56,64},{64,7... | collective-permute-start | bytes 1572872 | tf_op jit(solution)/shard_map/ppermute | solution.py:217
  133.9 15.7 %collective-permute-start.17 = (bf16[128,16,128]{2,1,0:T(8,128)(2,1)S(1)}, bf16[128,16,128]{2,1,0:T(8,128)(2,1)S(1)}, u32[]{:S(2)}, u32[]{:S(2)}) collective-permute-start(bf16[128,16,128]{2,1,0:T(8,128)(2,1)S(1)} %get-tuple-element.28), channel_id=1, source_target_pairs={{0,120},{8,0},{16,8},{24,16},{32,24},{40,32},{48,40},{56,48},{64,5... | collective-permute-start | bytes 1572872 | tf_op jit(solution)/shard_map/ppermute | solution.py:220
  137.8 20.0 %collective-permute-start.13 = (bf16[128,16,128]{2,1,0:T(8,128)(2,1)S(1)}, bf16[128,16,128]{2,1,0:T(8,128)(2,1)S(1)}, u32[]{:S(2)}, u32[]{:S(2)}) collective-permute-start(bf16[128,16,128]{2,1,0:T(8,128)(2,1)S(1)} %get-tuple-element.22), channel_id=1, source_target_pairs={{0,120},{8,0},{16,8},{24,16},{32,24},{40,32},{48,40},{56,48},{64,5... | collective-permute-start | bytes 1572872 | tf_op jit(solution)/shard_map/ppermute | solution.py:220
  145.7 13.4 %collective-permute-start.15 = (bf16[128,16,128]{2,1,0:T(8,128)(2,1)S(1)}, bf16[128,16,128]{2,1,0:T(8,128)(2,1)S(1)}, u32[]{:S(2)}, u32[]{:S(2)}) collective-permute-start(bf16[128,16,128]{2,1,0:T(8,128)(2,1)S(1)} %add_convert_fusion.3), channel_id=1, source_target_pairs={{0,8},{8,16},{16,24},{24,32},{32,40},{40,48},{48,56},{56,64},{64,7... | collective-permute-start | bytes 1572872 | tf_op jit(solution)/shard_map/ppermute | solution.py:217
  147.7 22.7 %collective-permute-start.16 = (bf16[128,16,128]{2,1,0:T(8,128)(2,1)S(1)}, bf16[128,16,128]{2,1,0:T(8,128)(2,1)S(1)}, u32[]{:S(2)}, u32[]{:S(2)}) collective-permute-start(bf16[128,16,128]{2,1,0:T(8,128)(2,1)S(1)} %get-tuple-element.26), channel_id=1, source_target_pairs={{0,8},{8,16},{16,24},{24,32},{32,40},{40,48},{48,56},{56,64},{64,7... | collective-permute-start | bytes 1572872 | tf_op jit(solution)/shard_map/ppermute | solution.py:217
  149.8 20.6 %collective-permute-start.18 = (bf16[128,16,128]{2,1,0:T(8,128)(2,1)S(1)}, bf16[128,16,128]{2,1,0:T(8,128)(2,1)S(1)}, u32[]{:S(2)}, u32[]{:S(2)}) collective-permute-start(bf16[128,16,128]{2,1,0:T(8,128)(2,1)S(1)} %add_convert_fusion.1), channel_id=1, source_target_pairs={{0,120},{8,0},{16,8},{24,16},{32,24},{40,32},{48,40},{56,48},{64,5... | collective-permute-start | bytes 1572872 | tf_op jit(solution)/shard_map/ppermute | solution.py:220
  171.7 13.7 %copy-start.3 = (bf16[8,16,1024]{2,1,0:T(8,128)(2,1)S(1)}, bf16[8,16,1024]{2,1,0:T(8,128)(2,1)}, u32[]{:S(2)}) copy-start(bf16[8,16,1024]{2,1,0:T(8,128)(2,1)} %copy-done.2) | copy-start | bytes 786436
  171.7 20.8 %all-to-all-start.3 = ((bf16[4,8,8,16,128]{4,3,2,1,0:T(8,128)(2,1)}), bf16[4,8,8,16,128]{4,3,2,1,0:T(8,128)(2,1)S(1)}, u32[]{:S(2)}, u32[]{:S(2)}) async-start(bf16[4,8,8,16,128]{4,3,2,1,0:T(8,128)(2,1)} %pad_maximum_fusion), calls=%async_computation.3 | async-start | bytes 2097152 | tf_op jit(solution)/shard_map/all_to_all | solution.py:290
  180.6 20.6 %collective-permute-start.12 = (bf16[8,16,256]{2,1,0:T(8,128)(2,1)S(1)}, bf16[8,16,256]{2,1,0:T(8,128)(2,1)S(1)}, u32[]{:S(2)}, u32[]{:S(2)}) collective-permute-start(bf16[8,16,256]{2,1,0:T(8,128)(2,1)S(1)} %get-tuple-element.20), channel_id=1, source_target_pairs={{0,4},{4,0},{1,5},{5,1},{2,6},{6,2},{3,7},{7,3},{8,12},{12,8},{9,1... | collective-permute-start | bytes 196616 | tf_op jit(solution)/shard_map/ppermute | solution.py:299
  185.4 17.1 %copy-start.1 = (bf16[8,16,1024]{2,1,0:T(8,128)(2,1)S(1)}, bf16[8,16,1024]{2,1,0:T(8,128)(2,1)}, u32[]{:S(2)}) copy-start(bf16[8,16,1024]{2,1,0:T(8,128)(2,1)} %copy-done) | copy-start | bytes 786436
  185.4 17.1 %collective-permute-start.11 = (bf16[8,16,1024]{2,1,0:T(8,128)(2,1)S(1)}, bf16[8,16,1024]{2,1,0:T(8,128)(2,1)S(1)}, u32[]{:S(2)}, u32[]{:S(2)}) collective-permute-start(bf16[8,16,1024]{2,1,0:T(8,128)(2,1)S(1)} %copy-done.3), channel_id=1, source_target_pairs={{0,4},{4,0},{1,5},{5,1},{2,6},{6,2},{3,7},{7,3},{8,12},{12,8},{9,1... | collective-permute-start | bytes 786440 | tf_op jit(solution)/shard_map/ppermute | solution.py:298
  193.4 25.1 %all-to-all-start.4 = ((bf16[8,8,16,128]{3,2,1,0:T(8,128)(2,1)}), bf16[8,8,16,128]{3,2,1,0:T(8,128)(2,1)S(1)}, u32[]{:S(2)}, u32[]{:S(2)}) async-start(bf16[8,8,16,128]{3,2,1,0:T(8,128)(2,1)} %fusion), calls=%async_computation.4 | async-start | bytes 524288 | tf_op jit(solution)/shard_map/all_to_all | solution.py:292
  (1 other events, 8.0 us)

commit v5 on v3

--- a/solution.py
+++ b/solution.py
@@ -37,13 +37,13 @@
     valid_ref,
     *refs,
 ):
-    stored, (mine, other) = refs[:PARTS], refs[PARTS : PARTS + 2]
-    outs = refs[PARTS + 2 : 2 * PARTS + 2]
-    dq_mine, dq_other, self_mine, self_other = refs[2 * PARTS + 2 : 2 * PARTS + 6]
-    store, grads, sem_in, sem_out = refs[2 * PARTS + 6 :]
+    stored, (mine, other) = refs[:5], refs[5:7]
+    outs = refs[7 : PARTS + 7]
+    dq_mine, dq_other, self_mine, self_other = refs[PARTS + 7 : PARTS + 11]
+    store, grads, sem_in, sem_out = refs[PARTS + 11 :]
     loads = [
-        pltpu.make_async_copy(src, store.at[pl.ds(i * HALF, HALF)], sem_in.at[i])
-        for i, src in enumerate(stored)
+        pltpu.make_async_copy(src, store.at[pl.ds(start * HALF, size * HALF)], sem_in.at[i])
+        for i, (src, start, size) in enumerate(zip(stored, (0, 2, 4, 5, 6), (2, 2, 1, 1, 2)))
     ]
     for copy in loads:
         copy.start()
@@ -131,12 +131,12 @@
     return pl.pallas_call(
         attention_kernel,
         out_shape=(tiles,) * PARTS + (query, query, own, own),
-        in_specs=[smem] * 2 + [hbm] * PARTS + [vmem] * 2,
+        in_specs=[smem] * 2 + [hbm] * 5 + [vmem] * 2,
         out_specs=(hbm,) * PARTS + (vmem,) * 4,
         scratch_shapes=[
             pltpu.VMEM((PARTS * HALF, LP, HD), BF),
             pltpu.VMEM((PARTS * HALF, LP, HD), BF),
-            pltpu.SemaphoreType.DMA((PARTS,)),
+            pltpu.SemaphoreType.DMA((5,)),
             pltpu.SemaphoreType.DMA((PARTS,)),
         ],
         compiler_params=pltpu.CompilerParams(vmem_limit_bytes=40 * 2**20),
@@ -194,16 +194,13 @@
         concat_axis=0,
         tiled=True,
     )
-    far_halves = far.reshape(2, ZH, TILES + 1, LP, HD)
-
-    def along_x(h):
-        return lax.all_to_all(
-            jnp.broadcast_to(far_halves[h][None, :, :TILES], (XS, ZH, TILES, LP, HD)),
-            "x",
-            split_axis=0,
-            concat_axis=0,
-            tiled=True,
-        ).reshape(HALF, LP, HD)
+    s0 = lax.all_to_all(
+        jnp.broadcast_to(far[None, :, :TILES], (XS, 2 * ZH, TILES, LP, HD)),
+        "x",
+        split_axis=0,
+        concat_axis=0,
+        tiled=True,
+    ).reshape(2 * HALF, LP, HD)
 
     def up(part):
         return lax.ppermute(part, around, ring(ZS, 1))
@@ -211,9 +208,7 @@
     def down(part):
         return lax.ppermute(part, around, ring(ZS, -1))
 
-    s0a, s0b = along_x(0), along_x(1)
-    s1a, s3a = down(s0a), up(s0a)
-    s3b, s1b = up(s0b), down(s0b)
+    s1, s3 = down(s0), up(s0)
 
     def pack(c):
         return jnp.concatenate(
@@ -233,7 +228,7 @@
 
     codes = far[:, TILES, 0, :2].astype(jnp.int32)
     known = codes[:, 0] * 16 + codes[:, 1]
-    known, _ = lax.optimization_barrier((known, s0a[:1, 0, :1]))
+    known = known + jnp.minimum(jnp.abs(s0[0, 0, 0]).astype(jnp.int32), 0)
     slot_of = lax.all_to_all(
         jnp.broadcast_to(known[None], (XS * ZL * TP, 2 * ZH)),
         ("x", "zl", "tp"),
@@ -241,8 +236,9 @@
         concat_axis=0,
         tiled=True,
     ).reshape(-1)
-    s1a, slot_of = lax.optimization_barrier((s1a, slot_of))
-    s2a, s2b = down(s1a), up(s3b)
+    zero = jnp.minimum(slot_of[0], 0)
+    s2a = down(lax.dynamic_slice_in_dim(s1, zero, HALF))
+    s2b = up(lax.dynamic_slice_in_dim(s3, HALF + zero, HALF))
 
     def parts(number):
         pool = number // P_DEV
@@ -256,11 +252,10 @@
     every = jnp.arange(slot_of.shape[0], dtype=jnp.int32)
     slots = jnp.sum(jnp.where(id_at[:, None] == every[None, :], slot_of[None, :], 0), axis=1)
     x, zh, zl, c, inner = parts(slots)
-    part = (zl - my_zl) % ZL * 2 + zh // 2
-    where = (((part * XS + x) * 2 + zh % 2) * 2 + c) * TILES + 2 * inner
+    where = ((((zl - my_zl) % ZL * XS + x) * ZH + zh) * 2 + c) * TILES + 2 * inner
 
     *grads, dq_mine, dq_other, self_mine, self_other = attention(
-        where, valid, (s0a, s0b, s1a, s1b, s2a, s2b, s3a, s3b), mine, other
+        where, valid, (s0, s1, s2a, s2b, s3), mine, other
     )
     g0a, g0b, g1a, g1b, g2a, g2b, g3a, g3b = grads
 
@@ -268,14 +263,9 @@
     from_below_b, from_above_a = up(g1b), down(g3a)
     from_below_a = up(total(g1a, via_a))
     from_above_b = down(total(g3b, via_b))
-    halves = (XS, ZH, TILES, LP, HD)
     summed = jnp.concatenate(
-        [
-            total(g0a, from_above_a, from_below_a).reshape(halves),
-            total(g0b, from_below_b, from_above_b).reshape(halves),
-        ],
-        axis=1,
-    )
+        [total(g0a, from_above_a, from_below_a), total(g0b, from_below_b, from_above_b)]
+    ).reshape(XS, 2 * ZH, TILES, LP, HD)
     x_parts = lax.all_to_all(summed, "x", split_axis=0, concat_axis=0, tiled=True)
     x_sum = total(*[x_parts[i] for i in range(XS)])
     far_parts = lax.all_to_all(x_sum, ("zh", "core"), split_axis=0, concat_axis=0, tiled=True)
@@ -284,7 +274,6 @@
     key_grad = jnp.concatenate([grad[0, :, 0], grad[1, :, 0]], axis=2)
     value_grad = jnp.concatenate([grad[0, :, 1], grad[1, :, 1]], axis=2)
 
-    dq_other, self_other, _ = lax.optimization_barrier((dq_other, self_other, from_below_b[:1, 0, :1]))
     dq_taken = lax.ppermute(dq_other, "core", swap)
     self_taken = lax.ppermute(self_other, "core", swap)
     query_grad = by_core(dq_mine, dq_taken, 2)

time: 208 us -> 209 us (level)
  blocking collectives: 0 us -> 37.8 us
  starting transfers between devices: 88.8 us -> 66 us
  waiting for transfers between devices: 91.6 us -> 70.9 us
  local copies, waits for them, and re-layouts: 5.73 us -> 9.34 us
    all_to_all x0 -> x1, blocking collectives: none -> 37.8 us  [per_device(): lax.all_to_all(jnp.broadcast_to(heads[None], (ZH, 2, TILES + 1, LP, HD))....]
    all_to_all x3 -> x1, waiting for transfers between devices: 32.8 us -> 7.63 us  [per_device(): lax.all_to_all(jnp.broadcast_to(far[None, :, :TILES], (XS, 2 * ZH, TILES,...]
    all_to_all x3 -> x1, starting transfers between devices: 22 us -> 4.44 us  [per_device(): lax.all_to_all(jnp.broadcast_to(far[None, :, :TILES], (XS, 2 * ZH, TILES,...]
    ppermute x6 -> x5, waiting for transfers between devices: 20.6 us -> 12.1 us  [down(): return lax.ppermute(part, around, ring(ZS, -1))]
    ppermute x6 -> x5, waiting for transfers between devices: 3.47 us -> 10.4 us  [up(): return lax.ppermute(part, around, ring(ZS, 1))]
    all_to_all x1, waiting for transfers between devices: 8.61 us -> 14.6 us  [per_device(): lax.all_to_all(jnp.broadcast_to(known[None], (XS * ZL * TP, 2 * ZH)), ('x...]
    ppermute x6 -> x5, starting transfers between devices: 19.7 us -> 14.6 us  [up(): return lax.ppermute(part, around, ring(ZS, 1))]
    ppermute x6 -> x5, starting transfers between devices: 20.7 us -> 19.4 us  [down(): return lax.ppermute(part, around, ring(ZS, -1))]
  transfers between devices with their start and end apart: 22 -> 18, of which waited for: 12 -> 11; matrix products, arithmetic and copies ran while one was open for 4% -> 6% of each run, Pallas kernels for 0% -> 0%
where the time goes in v5:
time: 209 us; the launch traced here: 208 us
  waiting for transfers between devices  70.9 us (34%)
  starting transfers between devices  66 us (32%)
  blocking collectives  37.8 us (18%)
  Pallas kernels  11.3 us (5%)
  other arithmetic  9.71 us (5%)
  local copies, waits for them, and re-layouts  9.34 us (4%)
  between operations  3.07 us (1%)
    all_to_all x1, blocking collectives, per_device(): lax.all_to_all(jnp.broadcast_to(heads[None], (ZH, 2, TILES + 1, LP, HD))....  37.8 us
    all_to_all x1, waiting for transfers between devices, per_device(): lax.all_to_all(x_sum, ('zh', 'core'), split_axis=0, concat_axis=0, tiled=...  19.6 us
    ppermute x5, starting transfers between devices, down(): return lax.ppermute(part, around, ring(ZS, -1))  19.4 us
    all_to_all x1, waiting for transfers between devices, per_device(): lax.all_to_all(jnp.broadcast_to(known[None], (XS * ZL * TP, 2 * ZH)), ('x...  14.6 us
    ppermute x5, starting transfers between devices, up(): return lax.ppermute(part, around, ring(ZS, 1))  14.6 us
    ppermute x5, waiting for transfers between devices, down(): return lax.ppermute(part, around, ring(ZS, -1))  12.1 us
    pallas_call x1, Pallas kernels, attention(): pl.pallas_call(attention_kernel, out_shape=(tiles,) * PARTS + (query, que...  11.3 us
    ppermute x5, waiting for transfers between devices, up(): return lax.ppermute(part, around, ring(ZS, 1))  10.4 us
  transfers between devices with their start and end apart: 18, of which 11 were waited for; matrix products, arithmetic and copies ran while one was open for 6% of the time, Pallas kernels for 0%

profile of v5, /device:TPU:32, one launch (start us, length us, event | category | flops | bytes accessed | tf_op | source)
XLA Modules:
  0.0 208.0 jit_solution(13521046227751335166)
XLA Ops:
  3.0 37.8 %all_to_all.26 = bf16[8,9,16,128]{3,2,1,0:T(8,128)(2,1)S(1)} all-to-all(bf16[8,9,16,128]{3,2,1,0:T(8,128)(2,1)S(1)} %bitcast.51), channel_id=1, replica_groups=mesh['x'=4,'zh'=4,'zl'=4,'core'=2,'tp'=4] {'zh','core'}, dimensions={0} | all-to-all | bytes 589824 | tf_op jit(solution)/shard_map/all_to_all | solution.py:190
  41.5 1.2 broadcast_in_dim.17
  42.7 4.4 %all-to-all-start.1 = ((bf16[4,8,8,16,128]{4,3,2,1,0:T(8,128)(2,1)}), bf16[4,8,8,16,128]{4,3,2,1,0:T(8,128)(2,1)S(1)}, u32[]{:S(2)}, u32[]{:S(2)}) async-start(bf16[4,8,8,16,128]{4,3,2,1,0:T(8,128)(2,1)} %broadcast_in_dim.17), calls=%async_computation.1 | async-start | bytes 2097152 | tf_op jit(solution)/shard_map/all_to_all | solution.py:197
  47.8 1.9 collective-permute-start
  52.0 2.4 %collective-permute-start.5 = (bf16[8,16,2304]{2,1,0:T(8,128)(2,1)}, bf16[8,16,2304]{2,1,0:T(8,128)(2,1)S(1)}, u32[]{:S(2)}, u32[]{:S(2)}) collective-permute-start(bf16[8,16,2304]{2,1,0:T(8,128)(2,1)} %pad_maximum_fusion.2), channel_id=1, source_target_pairs={{0,4},{4,0},{1,5},{5,1},{2,6},{6,2},{3,7},{7,3},{8,12},{12,8},{9,1... | collective-permute-start | bytes 1769480 | tf_op jit(solution)/shard_map/ppermute | solution.py:225
  54.4 7.6 %all-to-all-done.1 = bf16[4,8,8,16,128]{4,3,2,1,0:T(8,128)(2,1)S(1)} async-done(((bf16[4,8,8,16,128]{4,3,2,1,0:T(8,128)(2,1)}), bf16[4,8,8,16,128]{4,3,2,1,0:T(8,128)(2,1)S(1)}, u32[]{:S(2)}, u32[]{:S(2)}) %all-to-all-start.1) | async-done | bytes 1048608 | tf_op jit(solution)/shard_map/all_to_all | solution.py:197
  62.1 3.6 %collective-permute-start.3 = (bf16[256,16,128]{2,1,0:T(8,128)(2,1)S(1)}, bf16[256,16,128]{2,1,0:T(8,128)(2,1)S(1)}, u32[]{:S(2)}, u32[]{:S(2)}) collective-permute-start(bf16[256,16,128]{2,1,0:T(8,128)(2,1)S(1)} %bitcast.47), channel_id=1, source_target_pairs={{0,8},{8,16},{16,24},{24,32},{32,40},{40,48},{48,56},{56,64},{64,7... | collective-permute-start | bytes 3145736 | tf_op jit(solution)/shard_map/ppermute | solution.py:206
  65.6 2.3 %collective-permute-start.1 = (bf16[256,16,128]{2,1,0:T(8,128)(2,1)S(1)}, bf16[256,16,128]{2,1,0:T(8,128)(2,1)}, u32[]{:S(2)}, u32[]{:S(2)}) collective-permute-start(bf16[256,16,128]{2,1,0:T(8,128)(2,1)S(1)} %bitcast.48), channel_id=1, source_target_pairs={{0,120},{8,0},{16,8},{24,16},{32,24},{40,32},{48,40},{56,48},{64,5... | collective-permute-start | bytes 3145736 | tf_op jit(solution)/shard_map/ppermute | solution.py:209
  71.6 8.2 %all-to-all-start.2 = ((s32[64,1,8]{2,1,0:T(1,128)}), s32[64,1,8]{2,1,0:T(1,128)S(1)}, u32[]{:S(2)}, u32[]{:S(2)}) async-start(s32[64,1,8]{2,1,0:T(1,128)} %broadcast_in_dim.36), calls=%async_computation.2 | async-start | bytes 65536 | tf_op jit(solution)/shard_map/all_to_all | solution.py:232
  80.0 14.6 %all-to-all-done.2 = s32[64,1,8]{2,1,0:T(1,128)S(1)} async-done(((s32[64,1,8]{2,1,0:T(1,128)}), s32[64,1,8]{2,1,0:T(1,128)S(1)}, u32[]{:S(2)}, u32[]{:S(2)}) %all-to-all-start.2) | async-done | bytes 2080 | tf_op jit(solution)/shard_map/all_to_all | solution.py:232
  97.2 2.0 collective-permute-start.4
  99.2 1.1 constant_dynamic-slice_fusion.9
  100.3 3.9 %collective-permute-start.2 = (bf16[128,16,128]{2,1,0:T(8,128)(2,1)S(1)}, bf16[128,16,128]{2,1,0:T(8,128)(2,1)S(1)}, u32[]{:S(2)}, u32[]{:S(2)}) collective-permute-start(bf16[128,16,128]{2,1,0:T(8,128)(2,1)S(1)} %constant_dynamic-slice_fusion.9), channel_id=1, source_target_pairs={{0,120},{8,0},{16,8},{24,16},{32,24},{40,32},{48,40},{56,48},{64,5... | collective-permute-start | bytes 1572872 | tf_op jit(solution)/shard_map/ppermute | solution.py:209
  104.5 5.5 %collective-permute-done.4.refs_3_ = bf16[128,16,128]{2,1,0:T(8,128)(2,1)S(1)} collective-permute-done((bf16[128,16,128]{2,1,0:T(8,128)(2,1)S(1)}, bf16[128,16,128]{2,1,0:T(8,128)(2,1)S(1)}, u32[]{:S(2)}, u32[]{:S(2)}) %collective-permute-start.4) | collective-permute-done | bytes 524320 | tf_op jit(solution)/shard_map/ppermute | solution.py:206
  110.0 3.0 %collective-permute-done.2.refs_2_ = bf16[128,16,128]{2,1,0:T(8,128)(2,1)S(1)} collective-permute-done((bf16[128,16,128]{2,1,0:T(8,128)(2,1)S(1)}, bf16[128,16,128]{2,1,0:T(8,128)(2,1)S(1)}, u32[]{:S(2)}, u32[]{:S(2)}) %collective-permute-start.2) | collective-permute-done | bytes 524320 | tf_op jit(solution)/shard_map/ppermute | solution.py:209
  113.0 11.3 %shard_map.128 = (bf16[128,16,128]{2,1,0:T(8,128)(2,1)S(1)}, bf16[128,16,128]{2,1,0:T(8,128)(2,1)S(1)}, bf16[128,16,128]{2,1,0:T(8,128)(2,1)S(1)}, bf16[128,16,1...) custom-call(s32[256]{0:T(256)S(1)} %fusion.19.where_ref, ...), custom_call_target="tpu_custom_call" | custom-call | flops 713031680 | bytes 12582912 | tf_op jit(solution)/shard_map/pallas_call | solution.py:131
  124.3 2.1 %collective-permute-start.9 = (bf16[128,16,128]{2,1,0:T(8,128)(2,1)S(1)}, bf16[128,16,128]{2,1,0:T(8,128)(2,1)S(1)}, u32[]{:S(2)}, u32[]{:S(2)}) collective-permute-start(bf16[128,16,128]{2,1,0:T(8,128)(2,1)S(1)} %get-tuple-element.24), channel_id=1, source_target_pairs={{0,8},{8,16},{16,24},{24,32},{32,40},{40,48},{48,56},{56,64},{64,7... | collective-permute-start | bytes 1572872 | tf_op jit(solution)/shard_map/ppermute | solution.py:206
  126.5 3.7 %collective-permute-start.12 = (bf16[128,16,128]{2,1,0:T(8,128)(2,1)S(1)}, bf16[128,16,128]{2,1,0:T(8,128)(2,1)S(1)}, u32[]{:S(2)}, u32[]{:S(2)}) collective-permute-start(bf16[128,16,128]{2,1,0:T(8,128)(2,1)S(1)} %get-tuple-element.28), channel_id=1, source_target_pairs={{0,120},{8,0},{16,8},{24,16},{32,24},{40,32},{48,40},{56,48},{64,5... | collective-permute-start | bytes 1572872 | tf_op jit(solution)/shard_map/ppermute | solution.py:209
  130.2 5.5 %collective-permute-start.8 = (bf16[128,16,128]{2,1,0:T(8,128)(2,1)S(1)}, bf16[128,16,128]{2,1,0:T(8,128)(2,1)S(1)}, u32[]{:S(2)}, u32[]{:S(2)}) collective-permute-start(bf16[128,16,128]{2,1,0:T(8,128)(2,1)S(1)} %get-tuple-element.22), channel_id=1, source_target_pairs={{0,120},{8,0},{16,8},{24,16},{32,24},{40,32},{48,40},{56,48},{64,5... | collective-permute-start | bytes 1572872 | tf_op jit(solution)/shard_map/ppermute | solution.py:209
  136.2 2.6 %collective-permute-start.10 = (bf16[128,16,128]{2,1,0:T(8,128)(2,1)S(1)}, bf16[128,16,128]{2,1,0:T(8,128)(2,1)S(1)}, u32[]{:S(2)}, u32[]{:S(2)}) collective-permute-start(bf16[128,16,128]{2,1,0:T(8,128)(2,1)S(1)} %add_convert_fusion.3), channel_id=1, source_target_pairs={{0,8},{8,16},{16,24},{24,32},{32,40},{40,48},{48,56},{56,64},{64,7... | collective-permute-start | bytes 1572872 | tf_op jit(solution)/shard_map/ppermute | solution.py:206
  138.8 4.4 %collective-permute-start.11 = (bf16[128,16,128]{2,1,0:T(8,128)(2,1)S(1)}, bf16[128,16,128]{2,1,0:T(8,128)(2,1)S(1)}, u32[]{:S(2)}, u32[]{:S(2)}) collective-permute-start(bf16[128,16,128]{2,1,0:T(8,128)(2,1)S(1)} %get-tuple-element.26), channel_id=1, source_target_pairs={{0,8},{8,16},{16,24},{24,32},{32,40},{40,48},{48,56},{56,64},{64,7... | collective-permute-start | bytes 1572872 | tf_op jit(solution)/shard_map/ppermute | solution.py:206
  144.1 4.1 %collective-permute-start.13 = (bf16[128,16,128]{2,1,0:T(8,128)(2,1)S(1)}, bf16[128,16,128]{2,1,0:T(8,128)(2,1)S(1)}, u32[]{:S(2)}, u32[]{:S(2)}) collective-permute-start(bf16[128,16,128]{2,1,0:T(8,128)(2,1)S(1)} %add_convert_fusion.1), channel_id=1, source_target_pairs={{0,120},{8,0},{16,8},{24,16},{32,24},{40,32},{48,40},{56,48},{64,5... | collective-permute-start | bytes 1572872 | tf_op jit(solution)/shard_map/ppermute | solution.py:209
  148.2 7.0 %collective-permute-done.8 = bf16[128,16,128]{2,1,0:T(8,128)(2,1)S(1)} collective-permute-done((bf16[128,16,128]{2,1,0:T(8,128)(2,1)S(1)}, bf16[128,16,128]{2,1,0:T(8,128)(2,1)S(1)}, u32[]{:S(2)}, u32[]{:S(2)}) %collective-permute-start.8) | collective-permute-done | bytes 524320 | tf_op jit(solution)/shard_map/ppermute | solution.py:209
  155.4 4.6 %collective-permute-done.11 = bf16[128,16,128]{2,1,0:T(8,128)(2,1)S(1)} collective-permute-done((bf16[128,16,128]{2,1,0:T(8,128)(2,1)S(1)}, bf16[128,16,128]{2,1,0:T(8,128)(2,1)S(1)}, u32[]{:S(2)}, u32[]{:S(2)}) %collective-permute-start.11) | collective-permute-done | bytes 524320 | tf_op jit(solution)/shard_map/ppermute | solution.py:206
  160.0 1.4 collective-permute-done.13
  161.5 1.1 pad_maximum_fusion
  162.6 3.9 %all-to-all-start.3 = ((bf16[4,8,8,16,128]{4,3,2,1,0:T(8,128)(2,1)}), bf16[4,8,8,16,128]{4,3,2,1,0:T(8,128)(2,1)S(1)}, u32[]{:S(2)}, u32[]{:S(2)}) async-start(bf16[4,8,8,16,128]{4,3,2,1,0:T(8,128)(2,1)} %bitcast.21), calls=%async_computation.3 | async-start | bytes 2097152 | tf_op jit(solution)/shard_map/all_to_all | solution.py:269
  166.5 2.0 collective-permute-start.7
  168.6 2.4 %collective-permute-start.6 = (bf16[8,16,1024]{2,1,0:T(8,128)(2,1)S(1)}, bf16[8,16,1024]{2,1,0:T(8,128)(2,1)S(1)}, u32[]{:S(2)}, u32[]{:S(2)}) collective-permute-start(bf16[8,16,1024]{2,1,0:T(8,128)(2,1)S(1)} %copy-done.3), channel_id=1, source_target_pairs={{0,4},{4,0},{1,5},{5,1},{2,6},{6,2},{3,7},{7,3},{8,12},{12,8},{9,1... | collective-permute-start | bytes 786440 | tf_op jit(solution)/shard_map/ppermute | solution.py:277
  171.0 6.4 %all-to-all-done.3 = bf16[4,8,8,16,128]{4,3,2,1,0:T(8,128)(2,1)S(1)} async-done(((bf16[4,8,8,16,128]{4,3,2,1,0:T(8,128)(2,1)}), bf16[4,8,8,16,128]{4,3,2,1,0:T(8,128)(2,1)S(1)}, u32[]{:S(2)}, u32[]{:S(2)}) %all-to-all-start.3) | async-done | bytes 1048608 | tf_op jit(solution)/shard_map/all_to_all | solution.py:269
  178.3 6.6 %all-to-all-start.4 = ((bf16[8,8,16,128]{3,2,1,0:T(8,128)(2,1)}), bf16[8,8,16,128]{3,2,1,0:T(8,128)(2,1)S(1)}, u32[]{:S(2)}, u32[]{:S(2)}) async-start(bf16[8,8,16,128]{3,2,1,0:T(8,128)(2,1)} %fusion), calls=%async_computation.4 | async-start | bytes 524288 | tf_op jit(solution)/shard_map/all_to_all | solution.py:271
  187.1 19.6 %all-to-all-done.4 = bf16[8,8,16,128]{3,2,1,0:T(8,128)(2,1)S(1)} async-done(((bf16[8,8,16,128]{3,2,1,0:T(8,128)(2,1)}), bf16[8,8,16,128]{3,2,1,0:T(8,128)(2,1)S(1)}, u32[]{:S(2)}, u32[]{:S(2)}) %all-to-all-start.4) | async-done | bytes 262176 | tf_op jit(solution)/shard_map/all_to_all | solution.py:271
  (81 shorter events, 16.8 us)
Async XLA Ops:
  40.7 0.7 copy-start.6
  42.7 4.5 %copy-start.11 = (s32[8,16]{1,0:T(8,128)S(1)}, s32[8,16]{1,0:T(8,128)}, u32[]{:S(2)}) copy-start(s32[8,16]{1,0:T(8,128)} %param.16) | copy-start | bytes 1540
  42.7 4.5 %copy-start.12 = (s32[8,16]{1,0:T(8,128)S(1)}, s32[8,16]{1,0:T(8,128)}, u32[]{:S(2)}) copy-start(s32[8,16]{1,0:T(8,128)} %param.15) | copy-start | bytes 1540
  42.7 7.0 %copy-start.9 = (bf16[8,16,256]{2,1,0:T(8,128)(2,1)S(1)}, bf16[8,16,256]{2,1,0:T(8,128)(2,1)}, u32[]{:S(2)}) copy-start(bf16[8,16,256]{2,1,0:T(8,128)(2,1)} %param.11) | copy-start | bytes 196612
  42.7 7.0 %copy-start.10 = (bf16[8,16,256]{2,1,0:T(8,128)(2,1)S(1)}, bf16[8,16,256]{2,1,0:T(8,128)(2,1)}, u32[]{:S(2)}) copy-start(bf16[8,16,256]{2,1,0:T(8,128)(2,1)} %param.10) | copy-start | bytes 196612
  42.7 7.7 %copy-start.7 = (bf16[8,16,2048]{2,1,0:T(8,128)(2,1)S(1)}, bf16[8,16,2048]{2,1,0:T(8,128)(2,1)}, u32[]{:S(2)}) copy-start(bf16[8,16,2048]{2,1,0:T(8,128)(2,1)} %param.14) | copy-start | bytes 1572868
  42.7 7.7 %copy-start.8 = (bf16[8,16,2048]{2,1,0:T(8,128)(2,1)S(1)}, bf16[8,16,2048]{2,1,0:T(8,128)(2,1)}, u32[]{:S(2)}) copy-start(bf16[8,16,2048]{2,1,0:T(8,128)(2,1)} %param.9) | copy-start | bytes 1572868
  42.7 19.3 %all-to-all-start.1 = ((bf16[4,8,8,16,128]{4,3,2,1,0:T(8,128)(2,1)}), bf16[4,8,8,16,128]{4,3,2,1,0:T(8,128)(2,1)S(1)}, u32[]{:S(2)}, u32[]{:S(2)}) async-start(bf16[4,8,8,16,128]{4,3,2,1,0:T(8,128)(2,1)} %broadcast_in_dim.17), calls=%async_computation.1 | async-start | bytes 2097152 | tf_op jit(solution)/shard_map/all_to_all | solution.py:197
  47.8 21.2 %collective-permute-start = (s32[2,8,16]{2,1,0:T(8,128)}, s32[2,8,16]{2,1,0:T(8,128)S(1)}, u32[]{:S(2)}, u32[]{:S(2)}) collective-permute-start(s32[2,8,16]{2,1,0:T(8,128)} %pad_add_fusion), channel_id=1, source_target_pairs={{0,4},{4,0},{1,5},{5,1},{2,6},{6,2},{3,7},{7,3},{8,12},{12,8},{9,1... | collective-permute-start | bytes 3080 | tf_op jit(solution)/shard_map/ppermute | solution.py:227
  52.0 52.5 %collective-permute-start.5 = (bf16[8,16,2304]{2,1,0:T(8,128)(2,1)}, bf16[8,16,2304]{2,1,0:T(8,128)(2,1)S(1)}, u32[]{:S(2)}, u32[]{:S(2)}) collective-permute-start(bf16[8,16,2304]{2,1,0:T(8,128)(2,1)} %pad_maximum_fusion.2), channel_id=1, source_target_pairs={{0,4},{4,0},{1,5},{5,1},{2,6},{6,2},{3,7},{7,3},{8,12},{12,8},{9,1... | collective-permute-start | bytes 1769480 | tf_op jit(solution)/shard_map/ppermute | solution.py:225
  62.1 35.1 %collective-permute-start.3 = (bf16[256,16,128]{2,1,0:T(8,128)(2,1)S(1)}, bf16[256,16,128]{2,1,0:T(8,128)(2,1)S(1)}, u32[]{:S(2)}, u32[]{:S(2)}) collective-permute-start(bf16[256,16,128]{2,1,0:T(8,128)(2,1)S(1)} %bitcast.47), channel_id=1, source_target_pairs={{0,8},{8,16},{16,24},{24,32},{32,40},{40,48},{48,56},{56,64},{64,7... | collective-permute-start | bytes 3145736 | tf_op jit(solution)/shard_map/ppermute | solution.py:206
  65.6 33.6 %collective-permute-start.1 = (bf16[256,16,128]{2,1,0:T(8,128)(2,1)S(1)}, bf16[256,16,128]{2,1,0:T(8,128)(2,1)}, u32[]{:S(2)}, u32[]{:S(2)}) collective-permute-start(bf16[256,16,128]{2,1,0:T(8,128)(2,1)S(1)} %bitcast.48), channel_id=1, source_target_pairs={{0,120},{8,0},{16,8},{24,16},{32,24},{40,32},{48,40},{56,48},{64,5... | collective-permute-start | bytes 3145736 | tf_op jit(solution)/shard_map/ppermute | solution.py:209
  71.6 23.0 %all-to-all-start.2 = ((s32[64,1,8]{2,1,0:T(1,128)}), s32[64,1,8]{2,1,0:T(1,128)S(1)}, u32[]{:S(2)}, u32[]{:S(2)}) async-start(s32[64,1,8]{2,1,0:T(1,128)} %broadcast_in_dim.36), calls=%async_computation.2 | async-start | bytes 65536 | tf_op jit(solution)/shard_map/all_to_all | solution.py:232
  97.2 12.7 %collective-permute-start.4 = (bf16[128,16,128]{2,1,0:T(8,128)(2,1)S(1)}, bf16[128,16,128]{2,1,0:T(8,128)(2,1)S(1)}, u32[]{:S(2)}, u32[]{:S(2)}) collective-permute-start(bf16[128,16,128]{2,1,0:T(8,128)(2,1)S(1)} %constant_dynamic-slice_fusion.8), channel_id=1, source_target_pairs={{0,8},{8,16},{16,24},{24,32},{32,40},{40,48},{48,56},{56,64},{64,7... | collective-permute-start | bytes 1572872 | tf_op jit(solution)/shard_map/ppermute | solution.py:206
  100.3 12.7 %collective-permute-start.2 = (bf16[128,16,128]{2,1,0:T(8,128)(2,1)S(1)}, bf16[128,16,128]{2,1,0:T(8,128)(2,1)S(1)}, u32[]{:S(2)}, u32[]{:S(2)}) collective-permute-start(bf16[128,16,128]{2,1,0:T(8,128)(2,1)S(1)} %constant_dynamic-slice_fusion.9), channel_id=1, source_target_pairs={{0,120},{8,0},{16,8},{24,16},{32,24},{40,32},{48,40},{56,48},{64,5... | collective-permute-start | bytes 1572872 | tf_op jit(solution)/shard_map/ppermute | solution.py:209
  124.3 19.8 %copy-start = (bf16[8,16,256]{2,1,0:T(8,128)(2,1)}, bf16[8,16,256]{2,1,0:T(8,128)(2,1)S(1)}, u32[]{:S(2)}) copy-start(bf16[8,16,256]{2,1,0:T(8,128)(2,1)S(1)} %get-tuple-element.19) | copy-start | bytes 196612
  124.3 19.8 %copy-start.2 = (bf16[8,16,1024]{2,1,0:T(8,128)(2,1)}, bf16[8,16,1024]{2,1,0:T(8,128)(2,1)S(1)}, u32[]{:S(2)}) copy-start(bf16[8,16,1024]{2,1,0:T(8,128)(2,1)S(1)} %get-tuple-element.18) | copy-start | bytes 786436
  124.3 19.8 %copy-start.4 = (bf16[8,16,256]{2,1,0:T(8,128)(2,1)}, bf16[8,16,256]{2,1,0:T(8,128)(2,1)S(1)}, u32[]{:S(2)}) copy-start(bf16[8,16,256]{2,1,0:T(8,128)(2,1)S(1)} %get-tuple-element.20) | copy-start | bytes 196612
  124.3 11.8 %collective-permute-start.9 = (bf16[128,16,128]{2,1,0:T(8,128)(2,1)S(1)}, bf16[128,16,128]{2,1,0:T(8,128)(2,1)S(1)}, u32[]{:S(2)}, u32[]{:S(2)}) collective-permute-start(bf16[128,16,128]{2,1,0:T(8,128)(2,1)S(1)} %get-tuple-element.24), channel_id=1, source_target_pairs={{0,8},{8,16},{16,24},{24,32},{32,40},{40,48},{48,56},{56,64},{64,7... | collective-permute-start | bytes 1572872 | tf_op jit(solution)/shard_map/ppermute | solution.py:206
  126.5 17.5 %collective-permute-start.12 = (bf16[128,16,128]{2,1,0:T(8,128)(2,1)S(1)}, bf16[128,16,128]{2,1,0:T(8,128)(2,1)S(1)}, u32[]{:S(2)}, u32[]{:S(2)}) collective-permute-start(bf16[128,16,128]{2,1,0:T(8,128)(2,1)S(1)} %get-tuple-element.28), channel_id=1, source_target_pairs={{0,120},{8,0},{16,8},{24,16},{32,24},{40,32},{48,40},{56,48},{64,5... | collective-permute-start | bytes 1572872 | tf_op jit(solution)/shard_map/ppermute | solution.py:209
  130.2 25.0 %collective-permute-start.8 = (bf16[128,16,128]{2,1,0:T(8,128)(2,1)S(1)}, bf16[128,16,128]{2,1,0:T(8,128)(2,1)S(1)}, u32[]{:S(2)}, u32[]{:S(2)}) collective-permute-start(bf16[128,16,128]{2,1,0:T(8,128)(2,1)S(1)} %get-tuple-element.22), channel_id=1, source_target_pairs={{0,120},{8,0},{16,8},{24,16},{32,24},{40,32},{48,40},{56,48},{64,5... | collective-permute-start | bytes 1572872 | tf_op jit(solution)/shard_map/ppermute | solution.py:209
  136.2 19.0 %collective-permute-start.10 = (bf16[128,16,128]{2,1,0:T(8,128)(2,1)S(1)}, bf16[128,16,128]{2,1,0:T(8,128)(2,1)S(1)}, u32[]{:S(2)}, u32[]{:S(2)}) collective-permute-start(bf16[128,16,128]{2,1,0:T(8,128)(2,1)S(1)} %add_convert_fusion.3), channel_id=1, source_target_pairs={{0,8},{8,16},{16,24},{24,32},{32,40},{40,48},{48,56},{56,64},{64,7... | collective-permute-start | bytes 1572872 | tf_op jit(solution)/shard_map/ppermute | solution.py:206
  138.8 21.1 %collective-permute-start.11 = (bf16[128,16,128]{2,1,0:T(8,128)(2,1)S(1)}, bf16[128,16,128]{2,1,0:T(8,128)(2,1)S(1)}, u32[]{:S(2)}, u32[]{:S(2)}) collective-permute-start(bf16[128,16,128]{2,1,0:T(8,128)(2,1)S(1)} %get-tuple-element.26), channel_id=1, source_target_pairs={{0,8},{8,16},{16,24},{24,32},{32,40},{40,48},{48,56},{56,64},{64,7... | collective-permute-start | bytes 1572872 | tf_op jit(solution)/shard_map/ppermute | solution.py:206
  144.1 17.2 %collective-permute-start.13 = (bf16[128,16,128]{2,1,0:T(8,128)(2,1)S(1)}, bf16[128,16,128]{2,1,0:T(8,128)(2,1)S(1)}, u32[]{:S(2)}, u32[]{:S(2)}) collective-permute-start(bf16[128,16,128]{2,1,0:T(8,128)(2,1)S(1)} %add_convert_fusion.1), channel_id=1, source_target_pairs={{0,120},{8,0},{16,8},{24,16},{32,24},{40,32},{48,40},{56,48},{64,5... | collective-permute-start | bytes 1572872 | tf_op jit(solution)/shard_map/ppermute | solution.py:209
  162.6 3.9 %copy-start.5 = (bf16[8,16,256]{2,1,0:T(8,128)(2,1)S(1)}, bf16[8,16,256]{2,1,0:T(8,128)(2,1)}, u32[]{:S(2)}) copy-start(bf16[8,16,256]{2,1,0:T(8,128)(2,1)} %copy-done.4) | copy-start | bytes 196612
  162.6 6.0 %copy-start.3 = (bf16[8,16,1024]{2,1,0:T(8,128)(2,1)S(1)}, bf16[8,16,1024]{2,1,0:T(8,128)(2,1)}, u32[]{:S(2)}) copy-start(bf16[8,16,1024]{2,1,0:T(8,128)(2,1)} %copy-done.2) | copy-start | bytes 786436
  162.6 14.8 %all-to-all-start.3 = ((bf16[4,8,8,16,128]{4,3,2,1,0:T(8,128)(2,1)}), bf16[4,8,8,16,128]{4,3,2,1,0:T(8,128)(2,1)S(1)}, u32[]{:S(2)}, u32[]{:S(2)}) async-start(bf16[4,8,8,16,128]{4,3,2,1,0:T(8,128)(2,1)} %bitcast.21), calls=%async_computation.3 | async-start | bytes 2097152 | tf_op jit(solution)/shard_map/all_to_all | solution.py:269
  166.5 18.4 %copy-start.1 = (bf16[8,16,256]{2,1,0:T(8,128)(2,1)S(1)}, bf16[8,16,256]{2,1,0:T(8,128)(2,1)}, u32[]{:S(2)}) copy-start(bf16[8,16,256]{2,1,0:T(8,128)(2,1)} %copy-done) | copy-start | bytes 196612
  166.5 18.4 %collective-permute-start.7 = (bf16[8,16,256]{2,1,0:T(8,128)(2,1)S(1)}, bf16[8,16,256]{2,1,0:T(8,128)(2,1)S(1)}, u32[]{:S(2)}, u32[]{:S(2)}) collective-permute-start(bf16[8,16,256]{2,1,0:T(8,128)(2,1)S(1)} %copy-done.5), channel_id=1, source_target_pairs={{0,4},{4,0},{1,5},{5,1},{2,6},{6,2},{3,7},{7,3},{8,12},{12,8},{9,1... | collective-permute-start | bytes 196616 | tf_op jit(solution)/shard_map/ppermute | solution.py:278
  168.6 17.6 %collective-permute-start.6 = (bf16[8,16,1024]{2,1,0:T(8,128)(2,1)S(1)}, bf16[8,16,1024]{2,1,0:T(8,128)(2,1)S(1)}, u32[]{:S(2)}, u32[]{:S(2)}) collective-permute-start(bf16[8,16,1024]{2,1,0:T(8,128)(2,1)S(1)} %copy-done.3), channel_id=1, source_target_pairs={{0,4},{4,0},{1,5},{5,1},{2,6},{6,2},{3,7},{7,3},{8,12},{12,8},{9,1... | collective-permute-start | bytes 786440 | tf_op jit(solution)/shard_map/ppermute | solution.py:277
  178.3 28.5 %all-to-all-start.4 = ((bf16[8,8,16,128]{3,2,1,0:T(8,128)(2,1)}), bf16[8,8,16,128]{3,2,1,0:T(8,128)(2,1)S(1)}, u32[]{:S(2)}, u32[]{:S(2)}) async-start(bf16[8,8,16,128]{3,2,1,0:T(8,128)(2,1)} %fusion), calls=%async_computation.4 | async-start | bytes 524288 | tf_op jit(solution)/shard_map/all_to_all | solution.py:271

commit v6 on v5

--- a/solution.py
+++ b/solution.py
@@ -16,8 +16,10 @@
 XS, ZH, ZL, TP = 4, 4, 4, 4
 ZS = ZH * ZL
 TILES = 2 * P_DEV
-HALF = XS * ZH * TILES
+BLOCK = 2 * ZH * TILES
+HALF = XS // 2 * BLOCK
 PARTS = 2 * ZL
+CODES = 4 * ZH
 SCALE = HD ** (-0.5)
 SPAN = NB * LP
 BF = jnp.bfloat16
@@ -41,10 +43,15 @@
     outs = refs[7 : PARTS + 7]
     dq_mine, dq_other, self_mine, self_other = refs[PARTS + 7 : PARTS + 11]
     store, grads, sem_in, sem_out = refs[PARTS + 11 :]
-    loads = [
-        pltpu.make_async_copy(src, store.at[pl.ds(start * HALF, size * HALF)], sem_in.at[i])
-        for i, (src, start, size) in enumerate(zip(stored, (0, 2, 4, 5, 6), (2, 2, 1, 1, 2)))
-    ]
+    loads, to = [], 0
+    for src in stored:
+        for i in range(src.shape[0] // (BLOCK + 1)):
+            loads.append(
+                pltpu.make_async_copy(
+                    src.at[pl.ds(i * (BLOCK + 1), BLOCK)], store.at[pl.ds(to, BLOCK)], sem_in.at[to // BLOCK]
+                )
+            )
+            to += BLOCK
     for copy in loads:
         copy.start()
 
@@ -136,7 +143,7 @@
         scratch_shapes=[
             pltpu.VMEM((PARTS * HALF, LP, HD), BF),
             pltpu.VMEM((PARTS * HALF, LP, HD), BF),
-            pltpu.SemaphoreType.DMA((5,)),
+            pltpu.SemaphoreType.DMA((ZL * XS,)),
             pltpu.SemaphoreType.DMA((PARTS,)),
         ],
         compiler_params=pltpu.CompilerParams(vmem_limit_bytes=40 * 2**20),
@@ -178,8 +185,10 @@
         second = jnp.where(core == 0, other_part, mine_part)
         return jnp.concatenate([first, second], axis=axis)
 
-    code = jnp.concatenate([passage_slot // 16, passage_slot % 16]).astype(BF)
-    code_tile = jnp.pad(code.reshape(1, 1, 2), ((0, 0), (0, LP - 1), (0, HD - 2)))
+    lane = lax.broadcasted_iota(jnp.int32, (1, LP, HD), 2)
+    at = 4 * lax.axis_index("zh") + 2 * core
+    code_tile = jnp.where(lane == at, passage_slot // 16, jnp.where(lane == at + 1, passage_slot % 16, 0))
+    code_tile = code_tile.astype(BF)
 
     def passages(c):
         lanes = slice(c * HD, (c + 1) * HD)
@@ -194,13 +203,15 @@
         concat_axis=0,
         tiled=True,
     )
+    codes = jnp.sum(far[:, TILES:].astype(F32), axis=0).astype(BF)
+    block = jnp.concatenate([far[:, :TILES].reshape(BLOCK, LP, HD), codes], axis=0)
     s0 = lax.all_to_all(
-        jnp.broadcast_to(far[None, :, :TILES], (XS, 2 * ZH, TILES, LP, HD)),
+        jnp.broadcast_to(block[None], (XS, BLOCK + 1, LP, HD)),
         "x",
         split_axis=0,
         concat_axis=0,
         tiled=True,
-    ).reshape(2 * HALF, LP, HD)
+    ).reshape(XS * (BLOCK + 1), LP, HD)
 
     def up(part):
         return lax.ppermute(part, around, ring(ZS, 1))
@@ -209,6 +220,8 @@
         return lax.ppermute(part, around, ring(ZS, -1))
 
     s1, s3 = down(s0), up(s0)
+    half = s0.shape[0] // 2
+    s2a, s2b = down(s1[:half]), up(s3[half:])
 
     def pack(c):
         return jnp.concatenate(
@@ -226,19 +239,16 @@
     lists = jnp.stack([block_ids, block_valid])
     lists_other = lax.ppermute(lists, "core", swap)
 
-    codes = far[:, TILES, 0, :2].astype(jnp.int32)
-    known = codes[:, 0] * 16 + codes[:, 1]
-    known = known + jnp.minimum(jnp.abs(s0[0, 0, 0]).astype(jnp.int32), 0)
+    def codes_of(part):
+        return part.reshape(XS, BLOCK + 1, LP, HD)[:, BLOCK, 0, :CODES]
+
+    c0 = codes_of(s0)
+    c2 = lax.ppermute(c0, around, ring(ZS, 2))
+    seen = jnp.stack([c0, codes_of(s1), c2, codes_of(s3)]).astype(jnp.int32).reshape(-1, 2)
+    known = seen[:, 0] * 16 + seen[:, 1]
     slot_of = lax.all_to_all(
-        jnp.broadcast_to(known[None], (XS * ZL * TP, 2 * ZH)),
-        ("x", "zl", "tp"),
-        split_axis=0,
-        concat_axis=0,
-        tiled=True,
+        jnp.broadcast_to(known[None], (TP,) + known.shape), "tp", split_axis=0, concat_axis=0, tiled=True
     ).reshape(-1)
-    zero = jnp.minimum(slot_of[0], 0)
-    s2a = down(lax.dynamic_slice_in_dim(s1, zero, HALF))
-    s2b = up(lax.dynamic_slice_in_dim(s3, HALF + zero, HALF))
 
     def parts(number):
         pool = number // P_DEV
@@ -248,7 +258,7 @@
     ids = jnp.concatenate([block_ids, lists_other[0]]).reshape(-1)
     valid = jnp.concatenate([block_valid, lists_other[1]]).reshape(-1)
     x, zh, zl, c, inner = parts(ids)
-    id_at = (((x * ZL + zl) * TP + inner) * ZH + zh) * 2 + c
+    id_at = (((inner * ZL + (zl - my_zl) % ZL) * XS + x) * ZH + zh) * 2 + c
     every = jnp.arange(slot_of.shape[0], dtype=jnp.int32)
     slots = jnp.sum(jnp.where(id_at[:, None] == every[None, :], slot_of[None, :], 0), axis=1)
     x, zh, zl, c, inner = parts(slots)

time: 209 us -> 206 us (0.986)
  the two profiles are of different devices: /device:TPU:32 before, /device:TPU:1 now
where the time goes in v6:
time: 206 us; the launch traced here: 204 us
  starting transfers between devices  76.4 us (37%)
  waiting for transfers between devices  59.9 us (29%)
  blocking collectives  35.8 us (17%)
  Pallas kernels  12 us (6%)
  other arithmetic  10.1 us (5%)
  local copies, waits for them, and re-layouts  8.68 us (4%)
    all_to_all x1, blocking collectives, per_device(): lax.all_to_all(jnp.broadcast_to(heads[None], (ZH, 2, TILES + 1, LP, HD))....  35.8 us
    all_to_all x1, waiting for transfers between devices, per_device(): lax.all_to_all(x_sum, ('zh', 'core'), split_axis=0, concat_axis=0, tiled=...  20.4 us
    ppermute x5, waiting for transfers between devices, up(): return lax.ppermute(part, around, ring(ZS, 1))  19.4 us
    ppermute x5, starting transfers between devices, up(): return lax.ppermute(part, around, ring(ZS, 1))  18.1 us
    ppermute x5, starting transfers between devices, down(): return lax.ppermute(part, around, ring(ZS, -1))  14.1 us
    pallas_call x1, Pallas kernels, attention(): pl.pallas_call(attention_kernel, out_shape=(tiles,) * PARTS + (query, que...  12 us
    all_to_all x1, starting transfers between devices, per_device(): lax.all_to_all(x_sum, ('zh', 'core'), split_axis=0, concat_axis=0, tiled=...  11.1 us
    all_to_all x1, waiting for transfers between devices, per_device(): lax.all_to_all(jnp.broadcast_to(block[None], (XS, BLOCK + 1, LP, HD)), 'x...  9.16 us
  transfers between devices with their start and end apart: 19, of which 10 were waited for; matrix products, arithmetic and copies ran while one was open for 6% of the time, Pallas kernels for 0%

profile of v6, /device:TPU:1, one launch (start us, length us, event | category | flops | bytes accessed | tf_op | source)
XLA Modules:
  0.0 204.5 jit_solution(2350228903378738719)
XLA Ops:
  2.9 35.8 %all_to_all.26 = bf16[8,9,16,128]{3,2,1,0:T(8,128)(2,1)S(1)} all-to-all(bf16[8,9,16,128]{3,2,1,0:T(8,128)(2,1)S(1)} %bitcast.62), channel_id=1, replica_groups=mesh['x'=4,'zh'=4,'zl'=4,'core'=2,'tp'=4] {'zh','core'}, dimensions={0} | all-to-all | bytes 589824 | tf_op jit(solution)/shard_map/all_to_all | solution.py:199
  38.8 1.1 broadcast_in_dim.58
  39.9 4.2 %all-to-all-start.1 = ((bf16[4,65,16,128]{3,2,1,0:T(8,128)(2,1)}), bf16[4,65,16,128]{3,2,1,0:T(8,128)(2,1)S(1)}, u32[]{:S(2)}, u32[]{:S(2)}) async-start(bf16[4,65,16,128]{3,2,1,0:T(8,128)(2,1)} %broadcast_in_dim.58), calls=%async_computation.1 | async-start | bytes 2129920 | tf_op jit(solution)/shard_map/all_to_all | solution.py:208
  44.7 2.9 %collective-permute-start = (s32[2,8,16]{2,1,0:T(8,128)}, s32[2,8,16]{2,1,0:T(8,128)}, u32[]{:S(2)}, u32[]{:S(2)}) collective-permute-start(s32[2,8,16]{2,1,0:T(8,128)} %pad_add_fusion), channel_id=1, source_target_pairs={{0,4},{4,0},{1,5},{5,1},{2,6},{6,2},{3,7},{7,3},{8,12},{12,8},{9,1... | collective-permute-start | bytes 3080 | tf_op jit(solution)/shard_map/ppermute | solution.py:240
  49.2 9.2 %all-to-all-done.1 = bf16[4,65,16,128]{3,2,1,0:T(8,128)(2,1)S(1)} async-done(((bf16[4,65,16,128]{3,2,1,0:T(8,128)(2,1)}), bf16[4,65,16,128]{3,2,1,0:T(8,128)(2,1)S(1)}, u32[]{:S(2)}, u32[]{:S(2)}) %all-to-all-start.1) | async-done | bytes 1064992 | tf_op jit(solution)/shard_map/all_to_all | solution.py:208
  58.4 6.2 %collective-permute-start.3 = (bf16[260,16,128]{2,1,0:T(8,128)(2,1)S(1)}, bf16[260,16,128]{2,1,0:T(8,128)(2,1)S(1)}, u32[]{:S(2)}, u32[]{:S(2)}) collective-permute-start(bf16[260,16,128]{2,1,0:T(8,128)(2,1)S(1)} %bitcast.57), channel_id=1, source_target_pairs={{0,8},{8,16},{16,24},{24,32},{32,40},{40,48},{48,56},{56,64},{64,7... | collective-permute-start | bytes 3194888 | tf_op jit(solution)/shard_map/ppermute | solution.py:217
  64.5 1.9 collective-permute-start.1
  66.5 2.0 pad_maximum_fusion.2
  68.4 4.4 %collective-permute-start.6 = (bf16[8,16,2304]{2,1,0:T(8,128)(2,1)}, bf16[8,16,2304]{2,1,0:T(8,128)(2,1)}, u32[]{:S(2)}, u32[]{:S(2)}) collective-permute-start(bf16[8,16,2304]{2,1,0:T(8,128)(2,1)} %pad_maximum_fusion.2), channel_id=1, source_target_pairs={{0,4},{4,0},{1,5},{5,1},{2,6},{6,2},{3,7},{7,3},{8,12},{12,8},{9,1... | collective-permute-start | bytes 1769480 | tf_op jit(solution)/shard_map/ppermute | solution.py:238
  74.6 4.7 %collective-permute-start.2 = (bf16[4,16]{1,0:T(4,128)(2,1)S(1)}, bf16[4,16]{1,0:T(4,128)(2,1)S(1)}, u32[]{:S(2)}, u32[]{:S(2)}) collective-permute-start(bf16[4,16]{1,0:T(4,128)(2,1)S(1)} %bitcast.71), channel_id=1, source_target_pairs={{0,16},{8,24},{16,32},{24,40},{32,48},{40,56},{48,64},{56,72},{64,... | collective-permute-start | bytes 392 | tf_op jit(solution)/shard_map/ppermute | solution.py:246
  79.3 6.3 %collective-permute-done.3.refs_4_ = bf16[260,16,128]{2,1,0:T(8,128)(2,1)S(1)} collective-permute-done((bf16[260,16,128]{2,1,0:T(8,128)(2,1)S(1)}, bf16[260,16,128]{2,1,0:T(8,128)(2,1)S(1)}, u32[]{:S(2)}, u32[]{:S(2)}) %collective-permute-start.3) | collective-permute-done | bytes 1064992 | tf_op jit(solution)/shard_map/ppermute | solution.py:217
  86.5 3.8 %collective-permute-start.5 = (bf16[130,16,128]{2,1,0:T(8,128)(2,1)}, bf16[130,16,128]{2,1,0:T(8,128)(2,1)}, u32[]{:S(2)}, u32[]{:S(2)}) collective-permute-start(bf16[130,16,128]{2,1,0:T(8,128)(2,1)} %slice.138), channel_id=1, source_target_pairs={{0,8},{8,16},{16,24},{24,32},{32,40},{40,48},{48,56},{56,64},{64,7... | collective-permute-start | bytes 1597448 | tf_op jit(solution)/shard_map/ppermute | solution.py:217
  91.3 2.7 %collective-permute-start.4 = (bf16[130,16,128]{2,1,0:T(8,128)(2,1)}, bf16[130,16,128]{2,1,0:T(8,128)(2,1)}, u32[]{:S(2)}, u32[]{:S(2)}) collective-permute-start(bf16[130,16,128]{2,1,0:T(8,128)(2,1)} %slice.137), channel_id=1, source_target_pairs={{0,120},{8,0},{16,8},{24,16},{32,24},{40,32},{48,40},{56,48},{64,5... | collective-permute-start | bytes 1597448 | tf_op jit(solution)/shard_map/ppermute | solution.py:220
  94.8 4.2 %all-to-all-start.2 = ((s32[4,1,128]{2,1,0:T(1,128)}), s32[4,1,128]{2,1,0:T(1,128)S(1)}, u32[]{:S(2)}, u32[]{:S(2)}) async-start(s32[4,1,128]{2,1,0:T(1,128)} %broadcast_in_dim.59), calls=%async_computation.2 | async-start | bytes 4096 | tf_op jit(solution)/shard_map/all_to_all | solution.py:249
  99.1 4.0 %all-to-all-done.2 = s32[4,1,128]{2,1,0:T(1,128)S(1)} async-done(((s32[4,1,128]{2,1,0:T(1,128)}), s32[4,1,128]{2,1,0:T(1,128)S(1)}, u32[]{:S(2)}, u32[]{:S(2)}) %all-to-all-start.2) | async-done | bytes 2080 | tf_op jit(solution)/shard_map/all_to_all | solution.py:249
  105.3 12.0 %shard_map.128 = (bf16[128,16,128]{2,1,0:T(8,128)(2,1)S(1)}, bf16[128,16,128]{2,1,0:T(8,128)(2,1)S(1)}, bf16[128,16,128]{2,1,0:T(8,128)(2,1)S(1)}, bf16[128,16,1...) custom-call(s32[256]{0:T(256)S(1)} %fusion.15.where_ref, ...), custom_call_target="tpu_custom_call" | custom-call | flops 713031680 | bytes 12582912 | tf_op jit(solution)/shard_map/pallas_call | solution.py:138
  117.3 3.3 %collective-permute-start.10 = (bf16[128,16,128]{2,1,0:T(8,128)(2,1)S(1)}, bf16[128,16,128]{2,1,0:T(8,128)(2,1)S(1)}, u32[]{:S(2)}, u32[]{:S(2)}) collective-permute-start(bf16[128,16,128]{2,1,0:T(8,128)(2,1)S(1)} %get-tuple-element.24), channel_id=1, source_target_pairs={{0,8},{8,16},{16,24},{24,32},{32,40},{40,48},{48,56},{56,64},{64,7... | collective-permute-start | bytes 1572872 | tf_op jit(solution)/shard_map/ppermute | solution.py:217
  120.6 3.2 %collective-permute-start.13 = (bf16[128,16,128]{2,1,0:T(8,128)(2,1)S(1)}, bf16[128,16,128]{2,1,0:T(8,128)(2,1)S(1)}, u32[]{:S(2)}, u32[]{:S(2)}) collective-permute-start(bf16[128,16,128]{2,1,0:T(8,128)(2,1)S(1)} %get-tuple-element.28), channel_id=1, source_target_pairs={{0,120},{8,0},{16,8},{24,16},{32,24},{40,32},{48,40},{56,48},{64,5... | collective-permute-start | bytes 1572872 | tf_op jit(solution)/shard_map/ppermute | solution.py:220
  123.8 2.6 %collective-permute-start.9 = (bf16[128,16,128]{2,1,0:T(8,128)(2,1)S(1)}, bf16[128,16,128]{2,1,0:T(8,128)(2,1)S(1)}, u32[]{:S(2)}, u32[]{:S(2)}) collective-permute-start(bf16[128,16,128]{2,1,0:T(8,128)(2,1)S(1)} %get-tuple-element.22), channel_id=1, source_target_pairs={{0,120},{8,0},{16,8},{24,16},{32,24},{40,32},{48,40},{56,48},{64,5... | collective-permute-start | bytes 1572872 | tf_op jit(solution)/shard_map/ppermute | solution.py:220
  126.4 3.4 %collective-permute-done.10 = bf16[128,16,128]{2,1,0:T(8,128)(2,1)S(1)} collective-permute-done((bf16[128,16,128]{2,1,0:T(8,128)(2,1)S(1)}, bf16[128,16,128]{2,1,0:T(8,128)(2,1)S(1)}, u32[]{:S(2)}, u32[]{:S(2)}) %collective-permute-start.10) | collective-permute-done | bytes 524320 | tf_op jit(solution)/shard_map/ppermute | solution.py:217
  129.9 2.0 collective-permute-start.11
  132.0 2.8 %collective-permute-start.12 = (bf16[128,16,128]{2,1,0:T(8,128)(2,1)S(1)}, bf16[128,16,128]{2,1,0:T(8,128)(2,1)S(1)}, u32[]{:S(2)}, u32[]{:S(2)}) collective-permute-start(bf16[128,16,128]{2,1,0:T(8,128)(2,1)S(1)} %get-tuple-element.26), channel_id=1, source_target_pairs={{0,8},{8,16},{16,24},{24,32},{32,40},{40,48},{48,56},{56,64},{64,7... | collective-permute-start | bytes 1572872 | tf_op jit(solution)/shard_map/ppermute | solution.py:217
  135.0 3.7 %collective-permute-start.14 = (bf16[128,16,128]{2,1,0:T(8,128)(2,1)S(1)}, bf16[128,16,128]{2,1,0:T(8,128)(2,1)S(1)}, u32[]{:S(2)}, u32[]{:S(2)}) collective-permute-start(bf16[128,16,128]{2,1,0:T(8,128)(2,1)S(1)} %add_convert_fusion.1), channel_id=1, source_target_pairs={{0,120},{8,0},{16,8},{24,16},{32,24},{40,32},{48,40},{56,48},{64,5... | collective-permute-start | bytes 1572872 | tf_op jit(solution)/shard_map/ppermute | solution.py:220
  138.6 4.1 %collective-permute-done.9 = bf16[128,16,128]{2,1,0:T(8,128)(2,1)S(1)} collective-permute-done((bf16[128,16,128]{2,1,0:T(8,128)(2,1)S(1)}, bf16[128,16,128]{2,1,0:T(8,128)(2,1)S(1)}, u32[]{:S(2)}, u32[]{:S(2)}) %collective-permute-start.9) | collective-permute-done | bytes 524320 | tf_op jit(solution)/shard_map/ppermute | solution.py:220
  143.0 9.8 %collective-permute-done.12 = bf16[128,16,128]{2,1,0:T(8,128)(2,1)S(1)} collective-permute-done((bf16[128,16,128]{2,1,0:T(8,128)(2,1)S(1)}, bf16[128,16,128]{2,1,0:T(8,128)(2,1)S(1)}, u32[]{:S(2)}, u32[]{:S(2)}) %collective-permute-start.12) | collective-permute-done | bytes 524320 | tf_op jit(solution)/shard_map/ppermute | solution.py:217
  152.7 1.3 collective-permute-done.14
  154.2 1.1 pad_maximum_fusion
  155.3 3.6 %all-to-all-start.3 = ((bf16[4,8,8,16,128]{4,3,2,1,0:T(8,128)(2,1)}), bf16[4,8,8,16,128]{4,3,2,1,0:T(8,128)(2,1)S(1)}, u32[]{:S(2)}, u32[]{:S(2)}) async-start(bf16[4,8,8,16,128]{4,3,2,1,0:T(8,128)(2,1)} %bitcast.24), calls=%async_computation.3 | async-start | bytes 2097152 | tf_op jit(solution)/shard_map/all_to_all | solution.py:279
  159.0 7.2 %collective-permute-start.8 = (bf16[8,16,256]{2,1,0:T(8,128)(2,1)S(1)}, bf16[8,16,256]{2,1,0:T(8,128)(2,1)S(1)}, u32[]{:S(2)}, u32[]{:S(2)}) collective-permute-start(bf16[8,16,256]{2,1,0:T(8,128)(2,1)S(1)} %copy-done.4), channel_id=1, source_target_pairs={{0,4},{4,0},{1,5},{5,1},{2,6},{6,2},{3,7},{7,3},{8,12},{12,8},{9,1... | collective-permute-start | bytes 196616 | tf_op jit(solution)/shard_map/ppermute | solution.py:288
  166.2 1.9 collective-permute-start.7
  169.5 11.1 %all-to-all-start.4 = ((bf16[8,8,16,128]{3,2,1,0:T(8,128)(2,1)}), bf16[8,8,16,128]{3,2,1,0:T(8,128)(2,1)S(1)}, u32[]{:S(2)}, u32[]{:S(2)}) async-start(bf16[8,8,16,128]{3,2,1,0:T(8,128)(2,1)} %fusion), calls=%async_computation.4 | async-start | bytes 524288 | tf_op jit(solution)/shard_map/all_to_all | solution.py:281
  182.8 20.4 %all-to-all-done.4 = bf16[8,8,16,128]{3,2,1,0:T(8,128)(2,1)S(1)} async-done(((bf16[8,8,16,128]{3,2,1,0:T(8,128)(2,1)}), bf16[8,8,16,128]{3,2,1,0:T(8,128)(2,1)S(1)}, u32[]{:S(2)}, u32[]{:S(2)}) %all-to-all-start.4) | async-done | bytes 262176 | tf_op jit(solution)/shard_map/all_to_all | solution.py:281
  (89 shorter events, 16.0 us)
Async XLA Ops:
  39.9 4.2 %copy-start.10 = (s32[8,16]{1,0:T(8,128)S(1)}, s32[8,16]{1,0:T(8,128)}, u32[]{:S(2)}) copy-start(s32[8,16]{1,0:T(8,128)} %param.15) | copy-start | bytes 1540
  39.9 4.2 %copy-start.12 = (s32[8,16]{1,0:T(8,128)S(1)}, s32[8,16]{1,0:T(8,128)}, u32[]{:S(2)}) copy-start(s32[8,16]{1,0:T(8,128)} %param.16) | copy-start | bytes 1540
  39.9 7.7 %copy-start.8 = (bf16[8,16,256]{2,1,0:T(8,128)(2,1)S(1)}, bf16[8,16,256]{2,1,0:T(8,128)(2,1)}, u32[]{:S(2)}) copy-start(bf16[8,16,256]{2,1,0:T(8,128)(2,1)} %param.11) | copy-start | bytes 196612
  39.9 7.7 %copy-start.9 = (bf16[8,16,256]{2,1,0:T(8,128)(2,1)S(1)}, bf16[8,16,256]{2,1,0:T(8,128)(2,1)}, u32[]{:S(2)}) copy-start(bf16[8,16,256]{2,1,0:T(8,128)(2,1)} %param.10) | copy-start | bytes 196612
  39.9 8.4 %copy-start.6 = (bf16[8,16,2048]{2,1,0:T(8,128)(2,1)S(1)}, bf16[8,16,2048]{2,1,0:T(8,128)(2,1)}, u32[]{:S(2)}) copy-start(bf16[8,16,2048]{2,1,0:T(8,128)(2,1)} %param.14) | copy-start | bytes 1572868
  39.9 8.4 %copy-start.7 = (bf16[8,16,2048]{2,1,0:T(8,128)(2,1)S(1)}, bf16[8,16,2048]{2,1,0:T(8,128)(2,1)}, u32[]{:S(2)}) copy-start(bf16[8,16,2048]{2,1,0:T(8,128)(2,1)} %param.9) | copy-start | bytes 1572868
  39.9 18.4 %all-to-all-start.1 = ((bf16[4,65,16,128]{3,2,1,0:T(8,128)(2,1)}), bf16[4,65,16,128]{3,2,1,0:T(8,128)(2,1)S(1)}, u32[]{:S(2)}, u32[]{:S(2)}) async-start(bf16[4,65,16,128]{3,2,1,0:T(8,128)(2,1)} %broadcast_in_dim.58), calls=%async_computation.1 | async-start | bytes 2129920 | tf_op jit(solution)/shard_map/all_to_all | solution.py:208
  44.7 29.0 %collective-permute-start = (s32[2,8,16]{2,1,0:T(8,128)}, s32[2,8,16]{2,1,0:T(8,128)}, u32[]{:S(2)}, u32[]{:S(2)}) collective-permute-start(s32[2,8,16]{2,1,0:T(8,128)} %pad_add_fusion), channel_id=1, source_target_pairs={{0,4},{4,0},{1,5},{5,1},{2,6},{6,2},{3,7},{7,3},{8,12},{12,8},{9,1... | collective-permute-start | bytes 3080 | tf_op jit(solution)/shard_map/ppermute | solution.py:240
  58.4 14.5 %copy-start.5 = (bf16[8,16,1024]{2,1,0:T(8,128)(2,1)S(1)}, bf16[8,16,1024]{2,1,0:T(8,128)(2,1)}, u32[]{:S(2)}) copy-start(bf16[8,16,1024]{2,1,0:T(8,128)(2,1)} %get-tuple-element.61) | copy-start | bytes 786436
  58.4 27.2 %collective-permute-start.3 = (bf16[260,16,128]{2,1,0:T(8,128)(2,1)S(1)}, bf16[260,16,128]{2,1,0:T(8,128)(2,1)S(1)}, u32[]{:S(2)}, u32[]{:S(2)}) collective-permute-start(bf16[260,16,128]{2,1,0:T(8,128)(2,1)S(1)} %bitcast.57), channel_id=1, source_target_pairs={{0,8},{8,16},{16,24},{24,32},{32,40},{40,48},{48,56},{56,64},{64,7... | collective-permute-start | bytes 3194888 | tf_op jit(solution)/shard_map/ppermute | solution.py:217
  64.5 25.7 %collective-permute-start.1 = (bf16[260,16,128]{2,1,0:T(8,128)(2,1)S(1)}, bf16[260,16,128]{2,1,0:T(8,128)(2,1)S(1)}, u32[]{:S(2)}, u32[]{:S(2)}) collective-permute-start(bf16[260,16,128]{2,1,0:T(8,128)(2,1)S(1)} %bitcast.58), channel_id=1, source_target_pairs={{0,120},{8,0},{16,8},{24,16},{32,24},{40,32},{48,40},{56,48},{64,5... | collective-permute-start | bytes 3194888 | tf_op jit(solution)/shard_map/ppermute | solution.py:220
  68.4 6.0 %copy-start.11 = (s32[8,16]{1,0:T(8,128)S(1)}, s32[8,16]{1,0:T(8,128)}, u32[]{:S(2)}) copy-start(s32[8,16]{1,0:T(8,128)} %param.15) | copy-start | bytes 1540
  68.4 34.9 %collective-permute-start.6 = (bf16[8,16,2304]{2,1,0:T(8,128)(2,1)}, bf16[8,16,2304]{2,1,0:T(8,128)(2,1)}, u32[]{:S(2)}, u32[]{:S(2)}) collective-permute-start(bf16[8,16,2304]{2,1,0:T(8,128)(2,1)} %pad_maximum_fusion.2), channel_id=1, source_target_pairs={{0,4},{4,0},{1,5},{5,1},{2,6},{6,2},{3,7},{7,3},{8,12},{12,8},{9,1... | collective-permute-start | bytes 1769480 | tf_op jit(solution)/shard_map/ppermute | solution.py:238
  74.6 15.7 %collective-permute-start.2 = (bf16[4,16]{1,0:T(4,128)(2,1)S(1)}, bf16[4,16]{1,0:T(4,128)(2,1)S(1)}, u32[]{:S(2)}, u32[]{:S(2)}) collective-permute-start(bf16[4,16]{1,0:T(4,128)(2,1)S(1)} %bitcast.71), channel_id=1, source_target_pairs={{0,16},{8,24},{16,32},{24,40},{32,48},{40,56},{48,64},{56,72},{64,... | collective-permute-start | bytes 392 | tf_op jit(solution)/shard_map/ppermute | solution.py:246
  85.6 13.4 %copy-start.13 = (s32[8,16]{1,0:T(8,128)S(1)}, s32[8,16]{1,0:T(8,128)}, u32[]{:S(2)}) copy-start(s32[8,16]{1,0:T(8,128)} %param.16) | copy-start | bytes 1540
  86.5 16.9 %collective-permute-start.5 = (bf16[130,16,128]{2,1,0:T(8,128)(2,1)}, bf16[130,16,128]{2,1,0:T(8,128)(2,1)}, u32[]{:S(2)}, u32[]{:S(2)}) collective-permute-start(bf16[130,16,128]{2,1,0:T(8,128)(2,1)} %slice.138), channel_id=1, source_target_pairs={{0,8},{8,16},{16,24},{24,32},{32,40},{40,48},{48,56},{56,64},{64,7... | collective-permute-start | bytes 1597448 | tf_op jit(solution)/shard_map/ppermute | solution.py:217
  91.3 12.9 %collective-permute-start.4 = (bf16[130,16,128]{2,1,0:T(8,128)(2,1)}, bf16[130,16,128]{2,1,0:T(8,128)(2,1)}, u32[]{:S(2)}, u32[]{:S(2)}) collective-permute-start(bf16[130,16,128]{2,1,0:T(8,128)(2,1)} %slice.137), channel_id=1, source_target_pairs={{0,120},{8,0},{16,8},{24,16},{32,24},{40,32},{48,40},{56,48},{64,5... | collective-permute-start | bytes 1597448 | tf_op jit(solution)/shard_map/ppermute | solution.py:220
  94.8 8.3 %all-to-all-start.2 = ((s32[4,1,128]{2,1,0:T(1,128)}), s32[4,1,128]{2,1,0:T(1,128)S(1)}, u32[]{:S(2)}, u32[]{:S(2)}) async-start(s32[4,1,128]{2,1,0:T(1,128)} %broadcast_in_dim.59), calls=%async_computation.2 | async-start | bytes 4096 | tf_op jit(solution)/shard_map/all_to_all | solution.py:249
  117.3 17.7 %copy-start.1 = (bf16[8,16,1024]{2,1,0:T(8,128)(2,1)}, bf16[8,16,1024]{2,1,0:T(8,128)(2,1)S(1)}, u32[]{:S(2)}) copy-start(bf16[8,16,1024]{2,1,0:T(8,128)(2,1)S(1)} %get-tuple-element.18) | copy-start | bytes 786436
  117.3 17.7 %copy-start.3 = (bf16[8,16,256]{2,1,0:T(8,128)(2,1)}, bf16[8,16,256]{2,1,0:T(8,128)(2,1)S(1)}, u32[]{:S(2)}) copy-start(bf16[8,16,256]{2,1,0:T(8,128)(2,1)S(1)} %get-tuple-element.20) | copy-start | bytes 196612
  117.3 12.5 %collective-permute-start.10 = (bf16[128,16,128]{2,1,0:T(8,128)(2,1)S(1)}, bf16[128,16,128]{2,1,0:T(8,128)(2,1)S(1)}, u32[]{:S(2)}, u32[]{:S(2)}) collective-permute-start(bf16[128,16,128]{2,1,0:T(8,128)(2,1)S(1)} %get-tuple-element.24), channel_id=1, source_target_pairs={{0,8},{8,16},{16,24},{24,32},{32,40},{40,48},{48,56},{56,64},{64,7... | collective-permute-start | bytes 1572872 | tf_op jit(solution)/shard_map/ppermute | solution.py:217
  120.6 14.2 %collective-permute-start.13 = (bf16[128,16,128]{2,1,0:T(8,128)(2,1)S(1)}, bf16[128,16,128]{2,1,0:T(8,128)(2,1)S(1)}, u32[]{:S(2)}, u32[]{:S(2)}) collective-permute-start(bf16[128,16,128]{2,1,0:T(8,128)(2,1)S(1)} %get-tuple-element.28), channel_id=1, source_target_pairs={{0,120},{8,0},{16,8},{24,16},{32,24},{40,32},{48,40},{56,48},{64,5... | collective-permute-start | bytes 1572872 | tf_op jit(solution)/shard_map/ppermute | solution.py:220
  123.8 19.0 %collective-permute-start.9 = (bf16[128,16,128]{2,1,0:T(8,128)(2,1)S(1)}, bf16[128,16,128]{2,1,0:T(8,128)(2,1)S(1)}, u32[]{:S(2)}, u32[]{:S(2)}) collective-permute-start(bf16[128,16,128]{2,1,0:T(8,128)(2,1)S(1)} %get-tuple-element.22), channel_id=1, source_target_pairs={{0,120},{8,0},{16,8},{24,16},{32,24},{40,32},{48,40},{56,48},{64,5... | collective-permute-start | bytes 1572872 | tf_op jit(solution)/shard_map/ppermute | solution.py:220
  129.9 12.9 %collective-permute-start.11 = (bf16[128,16,128]{2,1,0:T(8,128)(2,1)S(1)}, bf16[128,16,128]{2,1,0:T(8,128)(2,1)S(1)}, u32[]{:S(2)}, u32[]{:S(2)}) collective-permute-start(bf16[128,16,128]{2,1,0:T(8,128)(2,1)S(1)} %add_convert_fusion.3), channel_id=1, source_target_pairs={{0,8},{8,16},{16,24},{24,32},{32,40},{40,48},{48,56},{56,64},{64,7... | collective-permute-start | bytes 1572872 | tf_op jit(solution)/shard_map/ppermute | solution.py:217
  132.0 20.8 %collective-permute-start.12 = (bf16[128,16,128]{2,1,0:T(8,128)(2,1)S(1)}, bf16[128,16,128]{2,1,0:T(8,128)(2,1)S(1)}, u32[]{:S(2)}, u32[]{:S(2)}) collective-permute-start(bf16[128,16,128]{2,1,0:T(8,128)(2,1)S(1)} %get-tuple-element.26), channel_id=1, source_target_pairs={{0,8},{8,16},{16,24},{24,32},{32,40},{40,48},{48,56},{56,64},{64,7... | collective-permute-start | bytes 1572872 | tf_op jit(solution)/shard_map/ppermute | solution.py:217
  135.0 19.0 %collective-permute-start.14 = (bf16[128,16,128]{2,1,0:T(8,128)(2,1)S(1)}, bf16[128,16,128]{2,1,0:T(8,128)(2,1)S(1)}, u32[]{:S(2)}, u32[]{:S(2)}) collective-permute-start(bf16[128,16,128]{2,1,0:T(8,128)(2,1)S(1)} %add_convert_fusion.1), channel_id=1, source_target_pairs={{0,120},{8,0},{16,8},{24,16},{32,24},{40,32},{48,40},{56,48},{64,5... | collective-permute-start | bytes 1572872 | tf_op jit(solution)/shard_map/ppermute | solution.py:220
  155.3 3.7 %copy-start.4 = (bf16[8,16,256]{2,1,0:T(8,128)(2,1)S(1)}, bf16[8,16,256]{2,1,0:T(8,128)(2,1)}, u32[]{:S(2)}) copy-start(bf16[8,16,256]{2,1,0:T(8,128)(2,1)} %copy-done.3) | copy-start | bytes 196612
  155.3 10.9 %copy-start.2 = (bf16[8,16,1024]{2,1,0:T(8,128)(2,1)S(1)}, bf16[8,16,1024]{2,1,0:T(8,128)(2,1)}, u32[]{:S(2)}) copy-start(bf16[8,16,1024]{2,1,0:T(8,128)(2,1)} %copy-done.1) | copy-start | bytes 786436
  155.3 13.4 %all-to-all-start.3 = ((bf16[4,8,8,16,128]{4,3,2,1,0:T(8,128)(2,1)}), bf16[4,8,8,16,128]{4,3,2,1,0:T(8,128)(2,1)S(1)}, u32[]{:S(2)}, u32[]{:S(2)}) async-start(bf16[4,8,8,16,128]{4,3,2,1,0:T(8,128)(2,1)} %bitcast.24), calls=%async_computation.3 | async-start | bytes 2097152 | tf_op jit(solution)/shard_map/all_to_all | solution.py:279
  159.0 21.6 %collective-permute-start.8 = (bf16[8,16,256]{2,1,0:T(8,128)(2,1)S(1)}, bf16[8,16,256]{2,1,0:T(8,128)(2,1)S(1)}, u32[]{:S(2)}, u32[]{:S(2)}) collective-permute-start(bf16[8,16,256]{2,1,0:T(8,128)(2,1)S(1)} %copy-done.4), channel_id=1, source_target_pairs={{0,4},{4,0},{1,5},{5,1},{2,6},{6,2},{3,7},{7,3},{8,12},{12,8},{9,1... | collective-permute-start | bytes 196616 | tf_op jit(solution)/shard_map/ppermute | solution.py:288
  166.2 15.7 %collective-permute-start.7 = (bf16[8,16,1024]{2,1,0:T(8,128)(2,1)S(1)}, bf16[8,16,1024]{2,1,0:T(8,128)(2,1)S(1)}, u32[]{:S(2)}, u32[]{:S(2)}) collective-permute-start(bf16[8,16,1024]{2,1,0:T(8,128)(2,1)S(1)} %copy-done.2), channel_id=1, source_target_pairs={{0,4},{4,0},{1,5},{5,1},{2,6},{6,2},{3,7},{7,3},{8,12},{12,8},{9,1... | collective-permute-start | bytes 786440 | tf_op jit(solution)/shard_map/ppermute | solution.py:287
  169.5 33.7 %all-to-all-start.4 = ((bf16[8,8,16,128]{3,2,1,0:T(8,128)(2,1)}), bf16[8,8,16,128]{3,2,1,0:T(8,128)(2,1)S(1)}, u32[]{:S(2)}, u32[]{:S(2)}) async-start(bf16[8,8,16,128]{3,2,1,0:T(8,128)(2,1)} %fusion), calls=%async_computation.4 | async-start | bytes 524288 | tf_op jit(solution)/shard_map/all_to_all | solution.py:281
  (1 other events, 1.1 us)

commit v7 on v6

--- a/solution.py
+++ b/solution.py
@@ -20,6 +20,7 @@
 HALF = XS // 2 * BLOCK
 PARTS = 2 * ZL
 CODES = 4 * ZH
+LOADS = 2 * ZL - 1
 SCALE = HD ** (-0.5)
 SPAN = NB * LP
 BF = jnp.bfloat16
@@ -39,10 +40,10 @@
     valid_ref,
     *refs,
 ):
-    stored, (mine, other) = refs[:5], refs[5:7]
-    outs = refs[7 : PARTS + 7]
-    dq_mine, dq_other, self_mine, self_other = refs[PARTS + 7 : PARTS + 11]
-    store, grads, sem_in, sem_out = refs[PARTS + 11 :]
+    stored, (mine, other) = refs[:LOADS], refs[LOADS : LOADS + 2]
+    outs = refs[LOADS + 2 : LOADS + 2 + PARTS]
+    dq_mine, dq_other, self_mine, self_other = refs[LOADS + 2 + PARTS : LOADS + 6 + PARTS]
+    store, grads, sem_in, sem_out = refs[LOADS + 6 + PARTS :]
     loads, to = [], 0
     for src in stored:
         for i in range(src.shape[0] // (BLOCK + 1)):
@@ -138,7 +139,7 @@
     return pl.pallas_call(
         attention_kernel,
         out_shape=(tiles,) * PARTS + (query, query, own, own),
-        in_specs=[smem] * 2 + [hbm] * 5 + [vmem] * 2,
+        in_specs=[smem] * 2 + [hbm] * LOADS + [vmem] * 2,
         out_specs=(hbm,) * PARTS + (vmem,) * 4,
         scratch_shapes=[
             pltpu.VMEM((PARTS * HALF, LP, HD), BF),
@@ -219,9 +220,10 @@
     def down(part):
         return lax.ppermute(part, around, ring(ZS, -1))
 
-    s1, s3 = down(s0), up(s0)
     half = s0.shape[0] // 2
-    s2a, s2b = down(s1[:half]), up(s3[half:])
+    s1a, s3b = down(s0[:half]), up(s0[half:])
+    s2a, s2b = down(s1a), up(s3b)
+    s1b, s3a = down(s0[half:]), up(s0[:half])
 
     def pack(c):
         return jnp.concatenate(
@@ -240,11 +242,12 @@
     lists_other = lax.ppermute(lists, "core", swap)
 
     def codes_of(part):
-        return part.reshape(XS, BLOCK + 1, LP, HD)[:, BLOCK, 0, :CODES]
+        return part.reshape(-1, BLOCK + 1, LP, HD)[:, BLOCK, 0, :CODES]
 
     c0 = codes_of(s0)
     c2 = lax.ppermute(c0, around, ring(ZS, 2))
-    seen = jnp.stack([c0, codes_of(s1), c2, codes_of(s3)]).astype(jnp.int32).reshape(-1, 2)
+    seen = jnp.concatenate([c0, codes_of(s1a), codes_of(s1b), c2, codes_of(s3a), codes_of(s3b)])
+    seen = seen.astype(jnp.int32).reshape(-1, 2)
     known = seen[:, 0] * 16 + seen[:, 1]
     slot_of = lax.all_to_all(
         jnp.broadcast_to(known[None], (TP,) + known.shape), "tp", split_axis=0, concat_axis=0, tiled=True
@@ -265,7 +268,7 @@
     where = ((((zl - my_zl) % ZL * XS + x) * ZH + zh) * 2 + c) * TILES + 2 * inner
 
     *grads, dq_mine, dq_other, self_mine, self_other = attention(
-        where, valid, (s0, s1, s2a, s2b, s3), mine, other
+        where, valid, (s0, s1a, s1b, s2a, s2b, s3a, s3b), mine, other
     )
     g0a, g0b, g1a, g1b, g2a, g2b, g3a, g3b = grads
 

time: 206 us -> 205 us (level)
  the two profiles are of different devices: /device:TPU:1 before, /device:TPU:9 now
where the time goes in v7:
time: 205 us; the launch traced here: 204 us
  starting transfers between devices  96.9 us (47%)
  waiting for transfers between devices  78.7 us (38%)
  Pallas kernels  11.7 us (6%)
  other arithmetic  7.56 us (4%)
  local copies, waits for them, and re-layouts  7.02 us (3%)
    ppermute x6, waiting for transfers between devices, up(): return lax.ppermute(part, around, ring(ZS, 1))  26.7 us
    ppermute x6, starting transfers between devices, up(): return lax.ppermute(part, around, ring(ZS, 1))  20.8 us
    ppermute x6, starting transfers between devices, down(): return lax.ppermute(part, around, ring(ZS, -1))  19.5 us
    all_to_all x1, waiting for transfers between devices, per_device(): lax.all_to_all(x_sum, ('zh', 'core'), split_axis=0, concat_axis=0, tiled=...  19.1 us
    all_to_all x1, starting transfers between devices, per_device(): lax.all_to_all(jnp.broadcast_to(heads[None], (ZH, 2, TILES + 1, LP, HD))....  15.8 us
    all_to_all x1, waiting for transfers between devices, per_device(): lax.all_to_all(jnp.broadcast_to(heads[None], (ZH, 2, TILES + 1, LP, HD))....  14.9 us
    pallas_call x1, Pallas kernels, attention(): pl.pallas_call(attention_kernel, out_shape=(tiles,) * PARTS + (query, que...  11.7 us
    all_to_all x1, starting transfers between devices, per_device(): lax.all_to_all(x_sum, ('zh', 'core'), split_axis=0, concat_axis=0, tiled=...  9.91 us
  transfers between devices with their start and end apart: 22, of which 14 were waited for; matrix products, arithmetic and copies ran while one was open for 5% of the time, Pallas kernels for 0%

profile of v7, /device:TPU:9, one launch (start us, length us, event | category | flops | bytes accessed | tf_op | source)
XLA Modules:
  0.0 203.8 jit_solution(11362295476239484515)
XLA Ops:
  3.8 15.8 %all-to-all-start = ((bf16[8,9,16,128]{3,2,1,0:T(8,128)(2,1)}), bf16[8,9,16,128]{3,2,1,0:T(8,128)(2,1)S(1)}, u32[]{:S(2)}, u32[]{:S(2)}) async-start(bf16[8,9,16,128]{3,2,1,0:T(8,128)(2,1)} %bitcast.13), calls=%async_computation | async-start | bytes 589824 | tf_op jit(solution)/shard_map/all_to_all | solution.py:200
  19.5 1.9 collective-permute-start
  21.6 14.9 %all-to-all-done = bf16[8,9,16,128]{3,2,1,0:T(8,128)(2,1)S(1)} async-done(((bf16[8,9,16,128]{3,2,1,0:T(8,128)(2,1)}), bf16[8,9,16,128]{3,2,1,0:T(8,128)(2,1)S(1)}, u32[]{:S(2)}, u32[]{:S(2)}) %all-to-all-start) | async-done | bytes 294944 | tf_op jit(solution)/shard_map/all_to_all | solution.py:200
  37.8 4.1 %all-to-all-start.1 = ((bf16[4,65,16,128]{3,2,1,0:T(8,128)(2,1)}), bf16[4,65,16,128]{3,2,1,0:T(8,128)(2,1)S(1)}, u32[]{:S(2)}, u32[]{:S(2)}) async-start(bf16[4,65,16,128]{3,2,1,0:T(8,128)(2,1)} %broadcast_in_dim.58), calls=%async_computation.1 | async-start | bytes 2129920 | tf_op jit(solution)/shard_map/all_to_all | solution.py:209
  42.8 4.6 %collective-permute-start.8 = (bf16[8,16,2304]{2,1,0:T(8,128)(2,1)}, bf16[8,16,2304]{2,1,0:T(8,128)(2,1)S(1)}, u32[]{:S(2)}, u32[]{:S(2)}) collective-permute-start(bf16[8,16,2304]{2,1,0:T(8,128)(2,1)} %pad_maximum_fusion.2), channel_id=1, source_target_pairs={{0,4},{4,0},{1,5},{5,1},{2,6},{6,2},{3,7},{7,3},{8,12},{12,8},{9,1... | collective-permute-start | bytes 1769480 | tf_op jit(solution)/shard_map/ppermute | solution.py:240
  47.5 6.7 %all-to-all-done.1 = bf16[4,65,16,128]{3,2,1,0:T(8,128)(2,1)S(1)} async-done(((bf16[4,65,16,128]{3,2,1,0:T(8,128)(2,1)}), bf16[4,65,16,128]{3,2,1,0:T(8,128)(2,1)S(1)}, u32[]{:S(2)}, u32[]{:S(2)}) %all-to-all-start.1) | async-done | bytes 1064992 | tf_op jit(solution)/shard_map/all_to_all | solution.py:209
  55.3 9.7 %collective-permute-start.4 = (bf16[130,16,128]{2,1,0:T(8,128)(2,1)}, bf16[130,16,128]{2,1,0:T(8,128)(2,1)S(1)}, u32[]{:S(2)}, u32[]{:S(2)}) collective-permute-start(bf16[130,16,128]{2,1,0:T(8,128)(2,1)} %bitcast.16), channel_id=1, source_target_pairs={{0,8},{8,16},{16,24},{24,32},{32,40},{40,48},{48,56},{56,64},{64,7... | collective-permute-start | bytes 1597448 | tf_op jit(solution)/shard_map/ppermute | solution.py:218
  67.0 3.4 %collective-permute-start.5 = (bf16[130,16,128]{2,1,0:T(8,128)(2,1)}, bf16[130,16,128]{2,1,0:T(8,128)(2,1)}, u32[]{:S(2)}, u32[]{:S(2)}) collective-permute-start(bf16[130,16,128]{2,1,0:T(8,128)(2,1)} %bitcast.19), channel_id=1, source_target_pairs={{0,8},{8,16},{16,24},{24,32},{32,40},{40,48},{48,56},{56,64},{64,7... | collective-permute-start | bytes 1597448 | tf_op jit(solution)/shard_map/ppermute | solution.py:218
  70.4 3.1 %collective-permute-start.2 = (bf16[130,16,128]{2,1,0:T(8,128)(2,1)}, bf16[130,16,128]{2,1,0:T(8,128)(2,1)}, u32[]{:S(2)}, u32[]{:S(2)}) collective-permute-start(bf16[130,16,128]{2,1,0:T(8,128)(2,1)} %bitcast.19), channel_id=1, source_target_pairs={{0,120},{8,0},{16,8},{24,16},{32,24},{40,32},{48,40},{56,48},{64,5... | collective-permute-start | bytes 1597448 | tf_op jit(solution)/shard_map/ppermute | solution.py:221
  74.8 2.9 %collective-permute-start.3 = (bf16[4,16]{1,0:T(4,128)(2,1)S(1)}, bf16[4,16]{1,0:T(4,128)(2,1)S(1)}, u32[]{:S(2)}, u32[]{:S(2)}) collective-permute-start(bf16[4,16]{1,0:T(4,128)(2,1)S(1)} %bitcast.75), channel_id=1, source_target_pairs={{0,16},{8,24},{16,32},{24,40},{32,48},{40,56},{48,64},{56,72},{64,... | collective-permute-start | bytes 392 | tf_op jit(solution)/shard_map/ppermute | solution.py:248
  78.7 7.6 %collective-permute-done.5.refs_6_ = bf16[130,16,128]{2,1,0:T(8,128)(2,1)} collective-permute-done((bf16[130,16,128]{2,1,0:T(8,128)(2,1)}, bf16[130,16,128]{2,1,0:T(8,128)(2,1)}, u32[]{:S(2)}, u32[]{:S(2)}) %collective-permute-start.5) | collective-permute-done | bytes 532512 | tf_op jit(solution)/shard_map/ppermute | solution.py:218
  86.9 3.1 %collective-permute-done.2.refs_2_ = bf16[130,16,128]{2,1,0:T(8,128)(2,1)} collective-permute-done((bf16[130,16,128]{2,1,0:T(8,128)(2,1)}, bf16[130,16,128]{2,1,0:T(8,128)(2,1)}, u32[]{:S(2)}, u32[]{:S(2)}) %collective-permute-start.2) | collective-permute-done | bytes 532512 | tf_op jit(solution)/shard_map/ppermute | solution.py:221
  90.9 3.4 %collective-permute-start.6 = (bf16[130,16,128]{2,1,0:T(8,128)(2,1)S(1)}, bf16[130,16,128]{2,1,0:T(8,128)(2,1)}, u32[]{:S(2)}, u32[]{:S(2)}) collective-permute-start(bf16[130,16,128]{2,1,0:T(8,128)(2,1)S(1)} %collective-permute-done.1.refs_1_), channel_id=1, source_target_pairs={{0,120},{8,0},{16,8},{24,16},{32,24},{40,32},{48,40},{56,48},{64,5... | collective-permute-start | bytes 1597448 | tf_op jit(solution)/shard_map/ppermute | solution.py:221
  94.3 1.9 collective-permute-start.7
  97.0 4.3 %all-to-all-start.2 = ((s32[4,1,128]{2,1,0:T(1,128)}), s32[4,1,128]{2,1,0:T(1,128)S(1)}, u32[]{:S(2)}, u32[]{:S(2)}) async-start(s32[4,1,128]{2,1,0:T(1,128)} %broadcast_in_dim.59), calls=%async_computation.2 | async-start | bytes 4096 | tf_op jit(solution)/shard_map/all_to_all | solution.py:252
  101.5 3.2 %all-to-all-done.2 = s32[4,1,128]{2,1,0:T(1,128)S(1)} async-done(((s32[4,1,128]{2,1,0:T(1,128)}), s32[4,1,128]{2,1,0:T(1,128)S(1)}, u32[]{:S(2)}, u32[]{:S(2)}) %all-to-all-start.2) | async-done | bytes 2080 | tf_op jit(solution)/shard_map/all_to_all | solution.py:252
  104.9 3.3 %collective-permute-done.7.refs_4_ = bf16[130,16,128]{2,1,0:T(8,128)(2,1)} collective-permute-done((bf16[130,16,128]{2,1,0:T(8,128)(2,1)}, bf16[130,16,128]{2,1,0:T(8,128)(2,1)}, u32[]{:S(2)}, u32[]{:S(2)}) %collective-permute-start.7) | collective-permute-done | bytes 532512 | tf_op jit(solution)/shard_map/ppermute | solution.py:218
  108.2 11.7 %shard_map.128 = (bf16[128,16,128]{2,1,0:T(8,128)(2,1)S(1)}, bf16[128,16,128]{2,1,0:T(8,128)(2,1)S(1)}, bf16[128,16,128]{2,1,0:T(8,128)(2,1)S(1)}, bf16[128,16,1...) custom-call(s32[256]{0:T(256)S(1)} %fusion.15.where_ref, ...), custom_call_target="tpu_custom_call" | custom-call | flops 713031680 | bytes 12582912 | tf_op jit(solution)/shard_map/pallas_call | solution.py:139
  120.0 1.9 collective-permute-start.12
  121.9 4.6 %collective-permute-start.15 = (bf16[128,16,128]{2,1,0:T(8,128)(2,1)S(1)}, bf16[128,16,128]{2,1,0:T(8,128)(2,1)S(1)}, u32[]{:S(2)}, u32[]{:S(2)}) collective-permute-start(bf16[128,16,128]{2,1,0:T(8,128)(2,1)S(1)} %get-tuple-element.28), channel_id=1, source_target_pairs={{0,120},{8,0},{16,8},{24,16},{32,24},{40,32},{48,40},{56,48},{64,5... | collective-permute-start | bytes 1572872 | tf_op jit(solution)/shard_map/ppermute | solution.py:221
  126.5 1.9 collective-permute-start.11
  128.4 4.0 %collective-permute-done.12 = bf16[128,16,128]{2,1,0:T(8,128)(2,1)S(1)} collective-permute-done((bf16[128,16,128]{2,1,0:T(8,128)(2,1)S(1)}, bf16[128,16,128]{2,1,0:T(8,128)(2,1)S(1)}, u32[]{:S(2)}, u32[]{:S(2)}) %collective-permute-start.12) | collective-permute-done | bytes 524320 | tf_op jit(solution)/shard_map/ppermute | solution.py:218
  132.6 1.9 collective-permute-start.13
  134.5 1.9 collective-permute-start.14
  136.6 4.6 %collective-permute-start.16 = (bf16[128,16,128]{2,1,0:T(8,128)(2,1)S(1)}, bf16[128,16,128]{2,1,0:T(8,128)(2,1)S(1)}, u32[]{:S(2)}, u32[]{:S(2)}) collective-permute-start(bf16[128,16,128]{2,1,0:T(8,128)(2,1)S(1)} %add_convert_fusion.1), channel_id=1, source_target_pairs={{0,120},{8,0},{16,8},{24,16},{32,24},{40,32},{48,40},{56,48},{64,5... | collective-permute-start | bytes 1572872 | tf_op jit(solution)/shard_map/ppermute | solution.py:221
  141.2 3.4 %collective-permute-done.11 = bf16[128,16,128]{2,1,0:T(8,128)(2,1)S(1)} collective-permute-done((bf16[128,16,128]{2,1,0:T(8,128)(2,1)S(1)}, bf16[128,16,128]{2,1,0:T(8,128)(2,1)S(1)}, u32[]{:S(2)}, u32[]{:S(2)}) %collective-permute-start.11) | collective-permute-done | bytes 524320 | tf_op jit(solution)/shard_map/ppermute | solution.py:221
  144.8 10.6 %collective-permute-done.14 = bf16[128,16,128]{2,1,0:T(8,128)(2,1)S(1)} collective-permute-done((bf16[128,16,128]{2,1,0:T(8,128)(2,1)S(1)}, bf16[128,16,128]{2,1,0:T(8,128)(2,1)S(1)}, u32[]{:S(2)}, u32[]{:S(2)}) %collective-permute-start.14) | collective-permute-done | bytes 524320 | tf_op jit(solution)/shard_map/ppermute | solution.py:218
  157.1 3.6 %all-to-all-start.3 = ((bf16[4,8,8,16,128]{4,3,2,1,0:T(8,128)(2,1)}), bf16[4,8,8,16,128]{4,3,2,1,0:T(8,128)(2,1)S(1)}, u32[]{:S(2)}, u32[]{:S(2)}) async-start(bf16[4,8,8,16,128]{4,3,2,1,0:T(8,128)(2,1)} %bitcast.29), calls=%async_computation.3 | async-start | bytes 2097152 | tf_op jit(solution)/shard_map/all_to_all | solution.py:282
  160.8 7.4 %collective-permute-start.10 = (bf16[8,16,256]{2,1,0:T(8,128)(2,1)S(1)}, bf16[8,16,256]{2,1,0:T(8,128)(2,1)S(1)}, u32[]{:S(2)}, u32[]{:S(2)}) collective-permute-start(bf16[8,16,256]{2,1,0:T(8,128)(2,1)S(1)} %get-tuple-element.20), channel_id=1, source_target_pairs={{0,4},{4,0},{1,5},{5,1},{2,6},{6,2},{3,7},{7,3},{8,12},{12,8},{9,1... | collective-permute-start | bytes 196616 | tf_op jit(solution)/shard_map/ppermute | solution.py:291
  168.2 2.1 %collective-permute-start.9 = (bf16[8,16,1024]{2,1,0:T(8,128)(2,1)S(1)}, bf16[8,16,1024]{2,1,0:T(8,128)(2,1)S(1)}, u32[]{:S(2)}, u32[]{:S(2)}) collective-permute-start(bf16[8,16,1024]{2,1,0:T(8,128)(2,1)S(1)} %copy-done.3), channel_id=1, source_target_pairs={{0,4},{4,0},{1,5},{5,1},{2,6},{6,2},{3,7},{7,3},{8,12},{12,8},{9,1... | collective-permute-start | bytes 786440 | tf_op jit(solution)/shard_map/ppermute | solution.py:290
  171.3 9.9 %all-to-all-start.4 = ((bf16[8,8,16,128]{3,2,1,0:T(8,128)(2,1)}), bf16[8,8,16,128]{3,2,1,0:T(8,128)(2,1)S(1)}, u32[]{:S(2)}, u32[]{:S(2)}) async-start(bf16[8,8,16,128]{3,2,1,0:T(8,128)(2,1)} %fusion), calls=%async_computation.4 | async-start | bytes 524288 | tf_op jit(solution)/shard_map/all_to_all | solution.py:284
  183.4 19.1 %all-to-all-done.4 = bf16[8,8,16,128]{3,2,1,0:T(8,128)(2,1)S(1)} async-done(((bf16[8,8,16,128]{3,2,1,0:T(8,128)(2,1)}), bf16[8,8,16,128]{3,2,1,0:T(8,128)(2,1)S(1)}, u32[]{:S(2)}, u32[]{:S(2)}) %all-to-all-start.4) | async-done | bytes 262176 | tf_op jit(solution)/shard_map/all_to_all | solution.py:284
  (90 shorter events, 19.3 us)
Async XLA Ops:
  0.6 18.9 %copy-start.8 = (s32[8,16]{1,0:T(8,128)S(1)}, s32[8,16]{1,0:T(8,128)}, u32[]{:S(2)}) copy-start(s32[8,16]{1,0:T(8,128)} %param.15) | copy-start | bytes 1540
  0.6 18.9 %copy-start.9 = (s32[8,16]{1,0:T(8,128)S(1)}, s32[8,16]{1,0:T(8,128)}, u32[]{:S(2)}) copy-start(s32[8,16]{1,0:T(8,128)} %param.16) | copy-start | bytes 1540
  0.7 20.8 %copy-start.4 = (bf16[8,16,2048]{2,1,0:T(8,128)(2,1)S(1)}, bf16[8,16,2048]{2,1,0:T(8,128)(2,1)}, u32[]{:S(2)}) copy-start(bf16[8,16,2048]{2,1,0:T(8,128)(2,1)} %param.14) | copy-start | bytes 1572868
  0.7 20.8 %copy-start.5 = (bf16[8,16,2048]{2,1,0:T(8,128)(2,1)S(1)}, bf16[8,16,2048]{2,1,0:T(8,128)(2,1)}, u32[]{:S(2)}) copy-start(bf16[8,16,2048]{2,1,0:T(8,128)(2,1)} %param.9) | copy-start | bytes 1572868
  3.8 32.8 %all-to-all-start = ((bf16[8,9,16,128]{3,2,1,0:T(8,128)(2,1)}), bf16[8,9,16,128]{3,2,1,0:T(8,128)(2,1)S(1)}, u32[]{:S(2)}, u32[]{:S(2)}) async-start(bf16[8,9,16,128]{3,2,1,0:T(8,128)(2,1)} %bitcast.13), calls=%async_computation | async-start | bytes 589824 | tf_op jit(solution)/shard_map/all_to_all | solution.py:200
  19.5 50.8 %collective-permute-start = (s32[2,8,16]{2,1,0:T(8,128)S(1)}, s32[2,8,16]{2,1,0:T(8,128)S(1)}, u32[]{:S(2)}, u32[]{:S(2)}) collective-permute-start(s32[2,8,16]{2,1,0:T(8,128)S(1)} %pad_add_fusion), channel_id=1, source_target_pairs={{0,4},{4,0},{1,5},{5,1},{2,6},{6,2},{3,7},{7,3},{8,12},{12,8},{9,1... | collective-permute-start | bytes 3080 | tf_op jit(solution)/shard_map/ppermute | solution.py:242
  37.8 4.2 %copy-start.6 = (bf16[8,16,256]{2,1,0:T(8,128)(2,1)S(1)}, bf16[8,16,256]{2,1,0:T(8,128)(2,1)}, u32[]{:S(2)}) copy-start(bf16[8,16,256]{2,1,0:T(8,128)(2,1)} %param.11) | copy-start | bytes 196612
  37.8 4.2 %copy-start.7 = (bf16[8,16,256]{2,1,0:T(8,128)(2,1)S(1)}, bf16[8,16,256]{2,1,0:T(8,128)(2,1)}, u32[]{:S(2)}) copy-start(bf16[8,16,256]{2,1,0:T(8,128)(2,1)} %param.10) | copy-start | bytes 196612
  37.8 16.4 %all-to-all-start.1 = ((bf16[4,65,16,128]{3,2,1,0:T(8,128)(2,1)}), bf16[4,65,16,128]{3,2,1,0:T(8,128)(2,1)S(1)}, u32[]{:S(2)}, u32[]{:S(2)}) async-start(bf16[4,65,16,128]{3,2,1,0:T(8,128)(2,1)} %broadcast_in_dim.58), calls=%async_computation.1 | async-start | bytes 2129920 | tf_op jit(solution)/shard_map/all_to_all | solution.py:209
  42.8 62.1 %collective-permute-start.8 = (bf16[8,16,2304]{2,1,0:T(8,128)(2,1)}, bf16[8,16,2304]{2,1,0:T(8,128)(2,1)S(1)}, u32[]{:S(2)}, u32[]{:S(2)}) collective-permute-start(bf16[8,16,2304]{2,1,0:T(8,128)(2,1)} %pad_maximum_fusion.2), channel_id=1, source_target_pairs={{0,4},{4,0},{1,5},{5,1},{2,6},{6,2},{3,7},{7,3},{8,12},{12,8},{9,1... | collective-permute-start | bytes 1769480 | tf_op jit(solution)/shard_map/ppermute | solution.py:240
  55.3 19.5 %collective-permute-start.4 = (bf16[130,16,128]{2,1,0:T(8,128)(2,1)}, bf16[130,16,128]{2,1,0:T(8,128)(2,1)S(1)}, u32[]{:S(2)}, u32[]{:S(2)}) collective-permute-start(bf16[130,16,128]{2,1,0:T(8,128)(2,1)} %bitcast.16), channel_id=1, source_target_pairs={{0,8},{8,16},{16,24},{24,32},{32,40},{40,48},{48,56},{56,64},{64,7... | collective-permute-start | bytes 1597448 | tf_op jit(solution)/shard_map/ppermute | solution.py:218
  65.1 13.6 %collective-permute-start.1 = (bf16[130,16,128]{2,1,0:T(8,128)(2,1)}, bf16[130,16,128]{2,1,0:T(8,128)(2,1)S(1)}, u32[]{:S(2)}, u32[]{:S(2)}) collective-permute-start(bf16[130,16,128]{2,1,0:T(8,128)(2,1)} %bitcast.16), channel_id=1, source_target_pairs={{0,120},{8,0},{16,8},{24,16},{32,24},{40,32},{48,40},{56,48},{64,5... | collective-permute-start | bytes 1597448 | tf_op jit(solution)/shard_map/ppermute | solution.py:221
  67.0 19.3 %collective-permute-start.5 = (bf16[130,16,128]{2,1,0:T(8,128)(2,1)}, bf16[130,16,128]{2,1,0:T(8,128)(2,1)}, u32[]{:S(2)}, u32[]{:S(2)}) collective-permute-start(bf16[130,16,128]{2,1,0:T(8,128)(2,1)} %bitcast.19), channel_id=1, source_target_pairs={{0,8},{8,16},{16,24},{24,32},{32,40},{40,48},{48,56},{56,64},{64,7... | collective-permute-start | bytes 1597448 | tf_op jit(solution)/shard_map/ppermute | solution.py:218
  70.4 19.7 %collective-permute-start.2 = (bf16[130,16,128]{2,1,0:T(8,128)(2,1)}, bf16[130,16,128]{2,1,0:T(8,128)(2,1)}, u32[]{:S(2)}, u32[]{:S(2)}) collective-permute-start(bf16[130,16,128]{2,1,0:T(8,128)(2,1)} %bitcast.19), channel_id=1, source_target_pairs={{0,120},{8,0},{16,8},{24,16},{32,24},{40,32},{48,40},{56,48},{64,5... | collective-permute-start | bytes 1597448 | tf_op jit(solution)/shard_map/ppermute | solution.py:221
  74.8 15.9 %collective-permute-start.3 = (bf16[4,16]{1,0:T(4,128)(2,1)S(1)}, bf16[4,16]{1,0:T(4,128)(2,1)S(1)}, u32[]{:S(2)}, u32[]{:S(2)}) collective-permute-start(bf16[4,16]{1,0:T(4,128)(2,1)S(1)} %bitcast.75), channel_id=1, source_target_pairs={{0,16},{8,24},{16,32},{24,40},{32,48},{40,56},{48,64},{56,72},{64,... | collective-permute-start | bytes 392 | tf_op jit(solution)/shard_map/ppermute | solution.py:248
  90.9 14.0 %collective-permute-start.6 = (bf16[130,16,128]{2,1,0:T(8,128)(2,1)S(1)}, bf16[130,16,128]{2,1,0:T(8,128)(2,1)}, u32[]{:S(2)}, u32[]{:S(2)}) collective-permute-start(bf16[130,16,128]{2,1,0:T(8,128)(2,1)S(1)} %collective-permute-done.1.refs_1_), channel_id=1, source_target_pairs={{0,120},{8,0},{16,8},{24,16},{32,24},{40,32},{48,40},{56,48},{64,5... | collective-permute-start | bytes 1597448 | tf_op jit(solution)/shard_map/ppermute | solution.py:221
  94.3 13.9 %collective-permute-start.7 = (bf16[130,16,128]{2,1,0:T(8,128)(2,1)}, bf16[130,16,128]{2,1,0:T(8,128)(2,1)}, u32[]{:S(2)}, u32[]{:S(2)}) collective-permute-start(bf16[130,16,128]{2,1,0:T(8,128)(2,1)} %collective-permute-done.5.refs_6_), channel_id=1, source_target_pairs={{0,8},{8,16},{16,24},{24,32},{32,40},{40,48},{48,56},{56,64},{64,7... | collective-permute-start | bytes 1597448 | tf_op jit(solution)/shard_map/ppermute | solution.py:218
  97.0 7.6 %all-to-all-start.2 = ((s32[4,1,128]{2,1,0:T(1,128)}), s32[4,1,128]{2,1,0:T(1,128)S(1)}, u32[]{:S(2)}, u32[]{:S(2)}) async-start(s32[4,1,128]{2,1,0:T(1,128)} %broadcast_in_dim.59), calls=%async_computation.2 | async-start | bytes 4096 | tf_op jit(solution)/shard_map/all_to_all | solution.py:252
  120.0 16.7 %copy-start = (bf16[8,16,1024]{2,1,0:T(8,128)(2,1)}, bf16[8,16,1024]{2,1,0:T(8,128)(2,1)S(1)}, u32[]{:S(2)}) copy-start(bf16[8,16,1024]{2,1,0:T(8,128)(2,1)S(1)} %get-tuple-element.17) | copy-start | bytes 786436
  120.0 16.7 %copy-start.2 = (bf16[8,16,1024]{2,1,0:T(8,128)(2,1)}, bf16[8,16,1024]{2,1,0:T(8,128)(2,1)S(1)}, u32[]{:S(2)}) copy-start(bf16[8,16,1024]{2,1,0:T(8,128)(2,1)S(1)} %get-tuple-element.18) | copy-start | bytes 786436
  120.0 12.5 %collective-permute-start.12 = (bf16[128,16,128]{2,1,0:T(8,128)(2,1)S(1)}, bf16[128,16,128]{2,1,0:T(8,128)(2,1)S(1)}, u32[]{:S(2)}, u32[]{:S(2)}) collective-permute-start(bf16[128,16,128]{2,1,0:T(8,128)(2,1)S(1)} %get-tuple-element.24), channel_id=1, source_target_pairs={{0,8},{8,16},{16,24},{24,32},{32,40},{40,48},{48,56},{56,64},{64,7... | collective-permute-start | bytes 1572872 | tf_op jit(solution)/shard_map/ppermute | solution.py:218
  121.9 14.6 %collective-permute-start.15 = (bf16[128,16,128]{2,1,0:T(8,128)(2,1)S(1)}, bf16[128,16,128]{2,1,0:T(8,128)(2,1)S(1)}, u32[]{:S(2)}, u32[]{:S(2)}) collective-permute-start(bf16[128,16,128]{2,1,0:T(8,128)(2,1)S(1)} %get-tuple-element.28), channel_id=1, source_target_pairs={{0,120},{8,0},{16,8},{24,16},{32,24},{40,32},{48,40},{56,48},{64,5... | collective-permute-start | bytes 1572872 | tf_op jit(solution)/shard_map/ppermute | solution.py:221
  126.5 18.1 %collective-permute-start.11 = (bf16[128,16,128]{2,1,0:T(8,128)(2,1)S(1)}, bf16[128,16,128]{2,1,0:T(8,128)(2,1)S(1)}, u32[]{:S(2)}, u32[]{:S(2)}) collective-permute-start(bf16[128,16,128]{2,1,0:T(8,128)(2,1)S(1)} %get-tuple-element.22), channel_id=1, source_target_pairs={{0,120},{8,0},{16,8},{24,16},{32,24},{40,32},{48,40},{56,48},{64,5... | collective-permute-start | bytes 1572872 | tf_op jit(solution)/shard_map/ppermute | solution.py:221
  132.6 12.0 %collective-permute-start.13 = (bf16[128,16,128]{2,1,0:T(8,128)(2,1)S(1)}, bf16[128,16,128]{2,1,0:T(8,128)(2,1)S(1)}, u32[]{:S(2)}, u32[]{:S(2)}) collective-permute-start(bf16[128,16,128]{2,1,0:T(8,128)(2,1)S(1)} %add_convert_fusion.3), channel_id=1, source_target_pairs={{0,8},{8,16},{16,24},{24,32},{32,40},{40,48},{48,56},{56,64},{64,7... | collective-permute-start | bytes 1572872 | tf_op jit(solution)/shard_map/ppermute | solution.py:218
  134.5 20.9 %collective-permute-start.14 = (bf16[128,16,128]{2,1,0:T(8,128)(2,1)S(1)}, bf16[128,16,128]{2,1,0:T(8,128)(2,1)S(1)}, u32[]{:S(2)}, u32[]{:S(2)}) collective-permute-start(bf16[128,16,128]{2,1,0:T(8,128)(2,1)S(1)} %get-tuple-element.26), channel_id=1, source_target_pairs={{0,8},{8,16},{16,24},{24,32},{32,40},{40,48},{48,56},{56,64},{64,7... | collective-permute-start | bytes 1572872 | tf_op jit(solution)/shard_map/ppermute | solution.py:218
  136.6 19.2 %collective-permute-start.16 = (bf16[128,16,128]{2,1,0:T(8,128)(2,1)S(1)}, bf16[128,16,128]{2,1,0:T(8,128)(2,1)S(1)}, u32[]{:S(2)}, u32[]{:S(2)}) collective-permute-start(bf16[128,16,128]{2,1,0:T(8,128)(2,1)S(1)} %add_convert_fusion.1), channel_id=1, source_target_pairs={{0,120},{8,0},{16,8},{24,16},{32,24},{40,32},{48,40},{56,48},{64,5... | collective-permute-start | bytes 1572872 | tf_op jit(solution)/shard_map/ppermute | solution.py:221
  157.1 11.0 %copy-start.3 = (bf16[8,16,1024]{2,1,0:T(8,128)(2,1)S(1)}, bf16[8,16,1024]{2,1,0:T(8,128)(2,1)}, u32[]{:S(2)}) copy-start(bf16[8,16,1024]{2,1,0:T(8,128)(2,1)} %copy-done.2) | copy-start | bytes 786436
  157.1 13.4 %all-to-all-start.3 = ((bf16[4,8,8,16,128]{4,3,2,1,0:T(8,128)(2,1)}), bf16[4,8,8,16,128]{4,3,2,1,0:T(8,128)(2,1)S(1)}, u32[]{:S(2)}, u32[]{:S(2)}) async-start(bf16[4,8,8,16,128]{4,3,2,1,0:T(8,128)(2,1)} %bitcast.29), calls=%async_computation.3 | async-start | bytes 2097152 | tf_op jit(solution)/shard_map/all_to_all | solution.py:282
  160.8 20.5 %collective-permute-start.10 = (bf16[8,16,256]{2,1,0:T(8,128)(2,1)S(1)}, bf16[8,16,256]{2,1,0:T(8,128)(2,1)S(1)}, u32[]{:S(2)}, u32[]{:S(2)}) collective-permute-start(bf16[8,16,256]{2,1,0:T(8,128)(2,1)S(1)} %get-tuple-element.20), channel_id=1, source_target_pairs={{0,4},{4,0},{1,5},{5,1},{2,6},{6,2},{3,7},{7,3},{8,12},{12,8},{9,1... | collective-permute-start | bytes 196616 | tf_op jit(solution)/shard_map/ppermute | solution.py:291
  168.2 14.4 %copy-start.1 = (bf16[8,16,1024]{2,1,0:T(8,128)(2,1)S(1)}, bf16[8,16,1024]{2,1,0:T(8,128)(2,1)}, u32[]{:S(2)}) copy-start(bf16[8,16,1024]{2,1,0:T(8,128)(2,1)} %copy-done) | copy-start | bytes 786436
  168.2 14.4 %collective-permute-start.9 = (bf16[8,16,1024]{2,1,0:T(8,128)(2,1)S(1)}, bf16[8,16,1024]{2,1,0:T(8,128)(2,1)S(1)}, u32[]{:S(2)}, u32[]{:S(2)}) collective-permute-start(bf16[8,16,1024]{2,1,0:T(8,128)(2,1)S(1)} %copy-done.3), channel_id=1, source_target_pairs={{0,4},{4,0},{1,5},{5,1},{2,6},{6,2},{3,7},{7,3},{8,12},{12,8},{9,1... | collective-permute-start | bytes 786440 | tf_op jit(solution)/shard_map/ppermute | solution.py:290
  171.3 31.2 %all-to-all-start.4 = ((bf16[8,8,16,128]{3,2,1,0:T(8,128)(2,1)}), bf16[8,8,16,128]{3,2,1,0:T(8,128)(2,1)S(1)}, u32[]{:S(2)}, u32[]{:S(2)}) async-start(bf16[8,8,16,128]{3,2,1,0:T(8,128)(2,1)} %fusion), calls=%async_computation.4 | async-start | bytes 524288 | tf_op jit(solution)/shard_map/all_to_all | solution.py:284

commit v8 on v7

--- a/solution.py
+++ b/solution.py
@@ -44,15 +44,19 @@
     outs = refs[LOADS + 2 : LOADS + 2 + PARTS]
     dq_mine, dq_other, self_mine, self_other = refs[LOADS + 2 + PARTS : LOADS + 6 + PARTS]
     store, grads, sem_in, sem_out = refs[LOADS + 6 + PARTS :]
-    loads, to = [], 0
-    for src in stored:
-        for i in range(src.shape[0] // (BLOCK + 1)):
+    half = BLOCK // 2
+    loads = []
+    for i, src in enumerate(stored):
+        size = BLOCK if i == 0 else half
+        first = 0 if i == 0 else (i + 1) // 2 * XS * BLOCK + (i + 1) % 2 * half
+        for x in range(XS):
             loads.append(
                 pltpu.make_async_copy(
-                    src.at[pl.ds(i * (BLOCK + 1), BLOCK)], store.at[pl.ds(to, BLOCK)], sem_in.at[to // BLOCK]
+                    src.at[pl.ds(x * (size + 1), size)],
+                    store.at[pl.ds(first + x * BLOCK, size)],
+                    sem_in.at[i * XS + x],
                 )
             )
-            to += BLOCK
     for copy in loads:
         copy.start()
 
@@ -144,7 +148,7 @@
         scratch_shapes=[
             pltpu.VMEM((PARTS * HALF, LP, HD), BF),
             pltpu.VMEM((PARTS * HALF, LP, HD), BF),
-            pltpu.SemaphoreType.DMA((ZL * XS,)),
+            pltpu.SemaphoreType.DMA((LOADS * XS,)),
             pltpu.SemaphoreType.DMA((PARTS,)),
         ],
         compiler_params=pltpu.CompilerParams(vmem_limit_bytes=40 * 2**20),
@@ -220,10 +224,13 @@
     def down(part):
         return lax.ppermute(part, around, ring(ZS, -1))
 
-    half = s0.shape[0] // 2
-    s1a, s3b = down(s0[:half]), up(s0[half:])
+    by_x = s0.reshape(XS, BLOCK + 1, LP, HD)
+    half = BLOCK // 2
+    s0a = jnp.concatenate([by_x[:, :half], by_x[:, BLOCK:]], axis=1).reshape(-1, LP, HD)
+    s0b = by_x[:, half:].reshape(-1, LP, HD)
+    s1a, s3b = down(s0a), up(s0b)
     s2a, s2b = down(s1a), up(s3b)
-    s1b, s3a = down(s0[half:]), up(s0[:half])
+    s1b, s3a = down(s0b), up(s0a)
 
     def pack(c):
         return jnp.concatenate(
@@ -242,11 +249,11 @@
     lists_other = lax.ppermute(lists, "core", swap)
 
     def codes_of(part):
-        return part.reshape(-1, BLOCK + 1, LP, HD)[:, BLOCK, 0, :CODES]
+        return part.reshape(XS, -1, LP, HD)[:, -1, 0, :CODES]
 
     c0 = codes_of(s0)
     c2 = lax.ppermute(c0, around, ring(ZS, 2))
-    seen = jnp.concatenate([c0, codes_of(s1a), codes_of(s1b), c2, codes_of(s3a), codes_of(s3b)])
+    seen = jnp.concatenate([c0, codes_of(s1a), c2, codes_of(s3b)])
     seen = seen.astype(jnp.int32).reshape(-1, 2)
     known = seen[:, 0] * 16 + seen[:, 1]
     slot_of = lax.all_to_all(

time: 205 us -> 204 us (level)
  the two profiles are of different devices: /device:TPU:9 before, /device:TPU:1 now
where the time goes in v8:
time: 204 us; the launch traced here: 201 us
  starting transfers between devices  102 us (50%)
  waiting for transfers between devices  70.4 us (35%)
  Pallas kernels  12.7 us (6%)
  other arithmetic  8.4 us (4%)
  local copies, waits for them, and re-layouts  5.33 us (3%)
    ppermute x6, starting transfers between devices, up(): return lax.ppermute(part, around, ring(ZS, 1))  22.5 us
    ppermute x6, starting transfers between devices, down(): return lax.ppermute(part, around, ring(ZS, -1))  19.4 us
    all_to_all x1, starting transfers between devices, per_device(): lax.all_to_all(jnp.broadcast_to(heads[None], (ZH, 2, TILES + 1, LP, HD))....  16.6 us
    all_to_all x1, waiting for transfers between devices, per_device(): lax.all_to_all(jnp.broadcast_to(heads[None], (ZH, 2, TILES + 1, LP, HD))....  14.9 us
    all_to_all x1, waiting for transfers between devices, per_device(): lax.all_to_all(x_sum, ('zh', 'core'), split_axis=0, concat_axis=0, tiled=...  14.8 us
    ppermute x6, waiting for transfers between devices, up(): return lax.ppermute(part, around, ring(ZS, 1))  13.8 us
    all_to_all x1, starting transfers between devices, per_device(): lax.all_to_all(x_sum, ('zh', 'core'), split_axis=0, concat_axis=0, tiled=...  13.4 us
    pallas_call x1, Pallas kernels, attention(): pl.pallas_call(attention_kernel, out_shape=(tiles,) * PARTS + (query, que...  12.7 us
  transfers between devices with their start and end apart: 22, of which 12 were waited for; matrix products, arithmetic and copies ran while one was open for 4% of the time, Pallas kernels for 0%

profile of v8, /device:TPU:1, one launch (start us, length us, event | category | flops | bytes accessed | tf_op | source)
XLA Modules:
  0.0 200.9 jit_solution(12362620153402896562)
XLA Ops:
  3.8 16.6 %all-to-all-start = ((bf16[8,9,16,128]{3,2,1,0:T(8,128)(2,1)}), bf16[8,9,16,128]{3,2,1,0:T(8,128)(2,1)S(1)}, u32[]{:S(2)}, u32[]{:S(2)}) async-start(bf16[8,9,16,128]{3,2,1,0:T(8,128)(2,1)} %bitcast.13), calls=%async_computation | async-start | bytes 589824 | tf_op jit(solution)/shard_map/all_to_all | solution.py:204
  20.4 1.9 collective-permute-start
  22.4 14.9 %all-to-all-done = bf16[8,9,16,128]{3,2,1,0:T(8,128)(2,1)S(1)} async-done(((bf16[8,9,16,128]{3,2,1,0:T(8,128)(2,1)}), bf16[8,9,16,128]{3,2,1,0:T(8,128)(2,1)S(1)}, u32[]{:S(2)}, u32[]{:S(2)}) %all-to-all-start) | async-done | bytes 294944 | tf_op jit(solution)/shard_map/all_to_all | solution.py:204
  38.6 4.1 %all-to-all-start.1 = ((bf16[4,65,16,128]{3,2,1,0:T(8,128)(2,1)}), bf16[4,65,16,128]{3,2,1,0:T(8,128)(2,1)S(1)}, u32[]{:S(2)}, u32[]{:S(2)}) async-start(bf16[4,65,16,128]{3,2,1,0:T(8,128)(2,1)} %broadcast_in_dim.58), calls=%async_computation.1 | async-start | bytes 2129920 | tf_op jit(solution)/shard_map/all_to_all | solution.py:213
  43.6 4.6 %collective-permute-start.8 = (bf16[8,16,2304]{2,1,0:T(8,128)(2,1)}, bf16[8,16,2304]{2,1,0:T(8,128)(2,1)S(1)}, u32[]{:S(2)}, u32[]{:S(2)}) collective-permute-start(bf16[8,16,2304]{2,1,0:T(8,128)(2,1)} %pad_maximum_fusion.2), channel_id=1, source_target_pairs={{0,4},{4,0},{1,5},{5,1},{2,6},{6,2},{3,7},{7,3},{8,12},{12,8},{9,1... | collective-permute-start | bytes 1769480 | tf_op jit(solution)/shard_map/ppermute | solution.py:247
  48.3 6.7 %all-to-all-done.1 = bf16[4,65,16,128]{3,2,1,0:T(8,128)(2,1)S(1)} async-done(((bf16[4,65,16,128]{3,2,1,0:T(8,128)(2,1)}), bf16[4,65,16,128]{3,2,1,0:T(8,128)(2,1)S(1)}, u32[]{:S(2)}, u32[]{:S(2)}) %all-to-all-start.1) | async-done | bytes 1064992 | tf_op jit(solution)/shard_map/all_to_all | solution.py:213
  55.9 9.7 %collective-permute-start.3 = (bf16[132,16,128]{2,1,0:T(8,128)(2,1)}, bf16[132,16,128]{2,1,0:T(8,128)(2,1)S(1)}, u32[]{:S(2)}, u32[]{:S(2)}) collective-permute-start(bf16[132,16,128]{2,1,0:T(8,128)(2,1)} %bitcast.19), channel_id=1, source_target_pairs={{0,8},{8,16},{16,24},{24,32},{32,40},{40,48},{48,56},{56,64},{64,7... | collective-permute-start | bytes 1622024 | tf_op jit(solution)/shard_map/ppermute | solution.py:222
  66.5 1.9 collective-permute-start.1
  68.6 2.2 %collective-permute-start.4 = (bf16[132,16,128]{2,1,0:T(8,128)(2,1)}, bf16[132,16,128]{2,1,0:T(8,128)(2,1)}, u32[]{:S(2)}, u32[]{:S(2)}) collective-permute-start(bf16[132,16,128]{2,1,0:T(8,128)(2,1)} %bitcast.19), channel_id=1, source_target_pairs={{0,120},{8,0},{16,8},{24,16},{32,24},{40,32},{48,40},{56,48},{64,5... | collective-permute-start | bytes 1622024 | tf_op jit(solution)/shard_map/ppermute | solution.py:225
  70.8 3.1 %collective-permute-start.7 = (bf16[132,16,128]{2,1,0:T(8,128)(2,1)}, bf16[132,16,128]{2,1,0:T(8,128)(2,1)}, u32[]{:S(2)}, u32[]{:S(2)}) collective-permute-start(bf16[132,16,128]{2,1,0:T(8,128)(2,1)} %bitcast.16), channel_id=1, source_target_pairs={{0,8},{8,16},{16,24},{24,32},{32,40},{40,48},{48,56},{56,64},{64,7... | collective-permute-start | bytes 1622024 | tf_op jit(solution)/shard_map/ppermute | solution.py:222
  75.5 2.9 %collective-permute-start.2 = (bf16[4,16]{1,0:T(4,128)(2,1)S(1)}, bf16[4,16]{1,0:T(4,128)(2,1)S(1)}, u32[]{:S(2)}, u32[]{:S(2)}) collective-permute-start(bf16[4,16]{1,0:T(4,128)(2,1)S(1)} %bitcast.67), channel_id=1, source_target_pairs={{0,16},{8,24},{16,32},{24,40},{32,48},{40,56},{48,64},{56,72},{64,... | collective-permute-start | bytes 392 | tf_op jit(solution)/shard_map/ppermute | solution.py:255
  78.4 1.8 collective-permute-done.1.refs_1_
  80.3 7.9 %collective-permute-done.2 = bf16[4,16]{1,0:T(4,128)(2,1)S(1)} collective-permute-done((bf16[4,16]{1,0:T(4,128)(2,1)S(1)}, bf16[4,16]{1,0:T(4,128)(2,1)S(1)}, u32[]{:S(2)}, u32[]{:S(2)}) %collective-permute-start.2) | collective-permute-done | bytes 160 | tf_op jit(solution)/shard_map/ppermute | solution.py:255
  88.3 1.9 collective-permute-start.6
  90.2 4.6 %collective-permute-start.5 = (bf16[132,16,128]{2,1,0:T(8,128)(2,1)S(1)}, bf16[132,16,128]{2,1,0:T(8,128)(2,1)}, u32[]{:S(2)}, u32[]{:S(2)}) collective-permute-start(bf16[132,16,128]{2,1,0:T(8,128)(2,1)S(1)} %collective-permute-done.1.refs_1_), channel_id=1, source_target_pairs={{0,120},{8,0},{16,8},{24,16},{32,24},{40,32},{48,40},{56,48},{64,5... | collective-permute-start | bytes 1622024 | tf_op jit(solution)/shard_map/ppermute | solution.py:225
  95.6 4.2 %all-to-all-start.2 = ((s32[4,1,128]{2,1,0:T(1,128)}), s32[4,1,128]{2,1,0:T(1,128)S(1)}, u32[]{:S(2)}, u32[]{:S(2)}) async-start(s32[4,1,128]{2,1,0:T(1,128)} %broadcast_in_dim.59), calls=%async_computation.2 | async-start | bytes 4096 | tf_op jit(solution)/shard_map/all_to_all | solution.py:259
  99.8 4.0 %all-to-all-done.2 = s32[4,1,128]{2,1,0:T(1,128)S(1)} async-done(((s32[4,1,128]{2,1,0:T(1,128)}), s32[4,1,128]{2,1,0:T(1,128)S(1)}, u32[]{:S(2)}, u32[]{:S(2)}) %all-to-all-start.2) | async-done | bytes 2080 | tf_op jit(solution)/shard_map/all_to_all | solution.py:259
  104.2 12.7 %shard_map.128 = (bf16[128,16,128]{2,1,0:T(8,128)(2,1)S(1)}, bf16[128,16,128]{2,1,0:T(8,128)(2,1)S(1)}, bf16[128,16,128]{2,1,0:T(8,128)(2,1)S(1)}, bf16[128,16,1...) custom-call(s32[256]{0:T(256)S(1)} %fusion.15.where_ref, ...), custom_call_target="tpu_custom_call" | custom-call | flops 713031680 | bytes 12582912 | tf_op jit(solution)/shard_map/pallas_call | solution.py:143
  116.9 2.2 %collective-permute-start.12 = (bf16[128,16,128]{2,1,0:T(8,128)(2,1)S(1)}, bf16[128,16,128]{2,1,0:T(8,128)(2,1)S(1)}, u32[]{:S(2)}, u32[]{:S(2)}) collective-permute-start(bf16[128,16,128]{2,1,0:T(8,128)(2,1)S(1)} %get-tuple-element.24), channel_id=1, source_target_pairs={{0,8},{8,16},{16,24},{24,32},{32,40},{40,48},{48,56},{56,64},{64,7... | collective-permute-start | bytes 1572872 | tf_op jit(solution)/shard_map/ppermute | solution.py:222
  119.1 4.5 %collective-permute-start.15 = (bf16[128,16,128]{2,1,0:T(8,128)(2,1)S(1)}, bf16[128,16,128]{2,1,0:T(8,128)(2,1)S(1)}, u32[]{:S(2)}, u32[]{:S(2)}) collective-permute-start(bf16[128,16,128]{2,1,0:T(8,128)(2,1)S(1)} %get-tuple-element.28), channel_id=1, source_target_pairs={{0,120},{8,0},{16,8},{24,16},{32,24},{40,32},{48,40},{56,48},{64,5... | collective-permute-start | bytes 1572872 | tf_op jit(solution)/shard_map/ppermute | solution.py:225
  123.7 3.4 %collective-permute-start.11 = (bf16[128,16,128]{2,1,0:T(8,128)(2,1)S(1)}, bf16[128,16,128]{2,1,0:T(8,128)(2,1)S(1)}, u32[]{:S(2)}, u32[]{:S(2)}) collective-permute-start(bf16[128,16,128]{2,1,0:T(8,128)(2,1)S(1)} %get-tuple-element.22), channel_id=1, source_target_pairs={{0,120},{8,0},{16,8},{24,16},{32,24},{40,32},{48,40},{56,48},{64,5... | collective-permute-start | bytes 1572872 | tf_op jit(solution)/shard_map/ppermute | solution.py:225
  127.0 2.5 %collective-permute-done.12 = bf16[128,16,128]{2,1,0:T(8,128)(2,1)S(1)} collective-permute-done((bf16[128,16,128]{2,1,0:T(8,128)(2,1)S(1)}, bf16[128,16,128]{2,1,0:T(8,128)(2,1)S(1)}, u32[]{:S(2)}, u32[]{:S(2)}) %collective-permute-start.12) | collective-permute-done | bytes 524320 | tf_op jit(solution)/shard_map/ppermute | solution.py:222
  129.7 1.9 collective-permute-start.13
  131.6 3.7 %collective-permute-start.14 = (bf16[128,16,128]{2,1,0:T(8,128)(2,1)S(1)}, bf16[128,16,128]{2,1,0:T(8,128)(2,1)S(1)}, u32[]{:S(2)}, u32[]{:S(2)}) collective-permute-start(bf16[128,16,128]{2,1,0:T(8,128)(2,1)S(1)} %get-tuple-element.26), channel_id=1, source_target_pairs={{0,8},{8,16},{16,24},{24,32},{32,40},{40,48},{48,56},{56,64},{64,7... | collective-permute-start | bytes 1572872 | tf_op jit(solution)/shard_map/ppermute | solution.py:222
  135.4 2.8 %collective-permute-start.16 = (bf16[128,16,128]{2,1,0:T(8,128)(2,1)S(1)}, bf16[128,16,128]{2,1,0:T(8,128)(2,1)S(1)}, u32[]{:S(2)}, u32[]{:S(2)}) collective-permute-start(bf16[128,16,128]{2,1,0:T(8,128)(2,1)S(1)} %add_convert_fusion.1), channel_id=1, source_target_pairs={{0,120},{8,0},{16,8},{24,16},{32,24},{40,32},{48,40},{56,48},{64,5... | collective-permute-start | bytes 1572872 | tf_op jit(solution)/shard_map/ppermute | solution.py:225
  138.3 4.1 %collective-permute-done.11 = bf16[128,16,128]{2,1,0:T(8,128)(2,1)S(1)} collective-permute-done((bf16[128,16,128]{2,1,0:T(8,128)(2,1)S(1)}, bf16[128,16,128]{2,1,0:T(8,128)(2,1)S(1)}, u32[]{:S(2)}, u32[]{:S(2)}) %collective-permute-start.11) | collective-permute-done | bytes 524320 | tf_op jit(solution)/shard_map/ppermute | solution.py:225
  142.6 9.8 %collective-permute-done.14 = bf16[128,16,128]{2,1,0:T(8,128)(2,1)S(1)} collective-permute-done((bf16[128,16,128]{2,1,0:T(8,128)(2,1)S(1)}, bf16[128,16,128]{2,1,0:T(8,128)(2,1)S(1)}, u32[]{:S(2)}, u32[]{:S(2)}) %collective-permute-start.14) | collective-permute-done | bytes 524320 | tf_op jit(solution)/shard_map/ppermute | solution.py:222
  154.9 3.6 %all-to-all-start.3 = ((bf16[4,8,8,16,128]{4,3,2,1,0:T(8,128)(2,1)}), bf16[4,8,8,16,128]{4,3,2,1,0:T(8,128)(2,1)S(1)}, u32[]{:S(2)}, u32[]{:S(2)}) async-start(bf16[4,8,8,16,128]{4,3,2,1,0:T(8,128)(2,1)} %bitcast.25), calls=%async_computation.3 | async-start | bytes 2097152 | tf_op jit(solution)/shard_map/all_to_all | solution.py:289
  158.6 6.8 %collective-permute-start.10 = (bf16[8,16,256]{2,1,0:T(8,128)(2,1)S(1)}, bf16[8,16,256]{2,1,0:T(8,128)(2,1)S(1)}, u32[]{:S(2)}, u32[]{:S(2)}) collective-permute-start(bf16[8,16,256]{2,1,0:T(8,128)(2,1)S(1)} %get-tuple-element.20), channel_id=1, source_target_pairs={{0,4},{4,0},{1,5},{5,1},{2,6},{6,2},{3,7},{7,3},{8,12},{12,8},{9,1... | collective-permute-start | bytes 196616 | tf_op jit(solution)/shard_map/ppermute | solution.py:298
  165.4 2.1 %collective-permute-start.9 = (bf16[8,16,1024]{2,1,0:T(8,128)(2,1)S(1)}, bf16[8,16,1024]{2,1,0:T(8,128)(2,1)S(1)}, u32[]{:S(2)}, u32[]{:S(2)}) collective-permute-start(bf16[8,16,1024]{2,1,0:T(8,128)(2,1)S(1)} %copy-done.3), channel_id=1, source_target_pairs={{0,4},{4,0},{1,5},{5,1},{2,6},{6,2},{3,7},{7,3},{8,12},{12,8},{9,1... | collective-permute-start | bytes 786440 | tf_op jit(solution)/shard_map/ppermute | solution.py:297
  169.3 13.4 %all-to-all-start.4 = ((bf16[8,8,16,128]{3,2,1,0:T(8,128)(2,1)}), bf16[8,8,16,128]{3,2,1,0:T(8,128)(2,1)S(1)}, u32[]{:S(2)}, u32[]{:S(2)}) async-start(bf16[8,8,16,128]{3,2,1,0:T(8,128)(2,1)} %fusion), calls=%async_computation.4 | async-start | bytes 524288 | tf_op jit(solution)/shard_map/all_to_all | solution.py:291
  184.8 14.8 %all-to-all-done.4 = bf16[8,8,16,128]{3,2,1,0:T(8,128)(2,1)S(1)} async-done(((bf16[8,8,16,128]{3,2,1,0:T(8,128)(2,1)}), bf16[8,8,16,128]{3,2,1,0:T(8,128)(2,1)S(1)}, u32[]{:S(2)}, u32[]{:S(2)}) %all-to-all-start.4) | async-done | bytes 262176 | tf_op jit(solution)/shard_map/all_to_all | solution.py:291
  (88 shorter events, 17.6 us)
Async XLA Ops:
  0.6 19.7 %copy-start.8 = (s32[8,16]{1,0:T(8,128)S(1)}, s32[8,16]{1,0:T(8,128)}, u32[]{:S(2)}) copy-start(s32[8,16]{1,0:T(8,128)} %param.15) | copy-start | bytes 1540
  0.6 19.7 %copy-start.9 = (s32[8,16]{1,0:T(8,128)S(1)}, s32[8,16]{1,0:T(8,128)}, u32[]{:S(2)}) copy-start(s32[8,16]{1,0:T(8,128)} %param.16) | copy-start | bytes 1540
  0.7 21.7 %copy-start.4 = (bf16[8,16,2048]{2,1,0:T(8,128)(2,1)S(1)}, bf16[8,16,2048]{2,1,0:T(8,128)(2,1)}, u32[]{:S(2)}) copy-start(bf16[8,16,2048]{2,1,0:T(8,128)(2,1)} %param.14) | copy-start | bytes 1572868
  0.7 21.7 %copy-start.5 = (bf16[8,16,2048]{2,1,0:T(8,128)(2,1)S(1)}, bf16[8,16,2048]{2,1,0:T(8,128)(2,1)}, u32[]{:S(2)}) copy-start(bf16[8,16,2048]{2,1,0:T(8,128)(2,1)} %param.9) | copy-start | bytes 1572868
  3.8 33.6 %all-to-all-start = ((bf16[8,9,16,128]{3,2,1,0:T(8,128)(2,1)}), bf16[8,9,16,128]{3,2,1,0:T(8,128)(2,1)S(1)}, u32[]{:S(2)}, u32[]{:S(2)}) async-start(bf16[8,9,16,128]{3,2,1,0:T(8,128)(2,1)} %bitcast.13), calls=%async_computation | async-start | bytes 589824 | tf_op jit(solution)/shard_map/all_to_all | solution.py:204
  20.4 48.0 %collective-permute-start = (s32[2,8,16]{2,1,0:T(8,128)S(1)}, s32[2,8,16]{2,1,0:T(8,128)S(1)}, u32[]{:S(2)}, u32[]{:S(2)}) collective-permute-start(s32[2,8,16]{2,1,0:T(8,128)S(1)} %pad_add_fusion), channel_id=1, source_target_pairs={{0,4},{4,0},{1,5},{5,1},{2,6},{6,2},{3,7},{7,3},{8,12},{12,8},{9,1... | collective-permute-start | bytes 3080 | tf_op jit(solution)/shard_map/ppermute | solution.py:249
  38.6 4.2 %copy-start.6 = (bf16[8,16,256]{2,1,0:T(8,128)(2,1)S(1)}, bf16[8,16,256]{2,1,0:T(8,128)(2,1)}, u32[]{:S(2)}) copy-start(bf16[8,16,256]{2,1,0:T(8,128)(2,1)} %param.11) | copy-start | bytes 196612
  38.6 4.2 %copy-start.7 = (bf16[8,16,256]{2,1,0:T(8,128)(2,1)S(1)}, bf16[8,16,256]{2,1,0:T(8,128)(2,1)}, u32[]{:S(2)}) copy-start(bf16[8,16,256]{2,1,0:T(8,128)(2,1)} %param.10) | copy-start | bytes 196612
  38.6 16.4 %all-to-all-start.1 = ((bf16[4,65,16,128]{3,2,1,0:T(8,128)(2,1)}), bf16[4,65,16,128]{3,2,1,0:T(8,128)(2,1)S(1)}, u32[]{:S(2)}, u32[]{:S(2)}) async-start(bf16[4,65,16,128]{3,2,1,0:T(8,128)(2,1)} %broadcast_in_dim.58), calls=%async_computation.1 | async-start | bytes 2129920 | tf_op jit(solution)/shard_map/all_to_all | solution.py:213
  43.6 60.5 %collective-permute-start.8 = (bf16[8,16,2304]{2,1,0:T(8,128)(2,1)}, bf16[8,16,2304]{2,1,0:T(8,128)(2,1)S(1)}, u32[]{:S(2)}, u32[]{:S(2)}) collective-permute-start(bf16[8,16,2304]{2,1,0:T(8,128)(2,1)} %pad_maximum_fusion.2), channel_id=1, source_target_pairs={{0,4},{4,0},{1,5},{5,1},{2,6},{6,2},{3,7},{7,3},{8,12},{12,8},{9,1... | collective-permute-start | bytes 1769480 | tf_op jit(solution)/shard_map/ppermute | solution.py:247
  55.9 19.7 %collective-permute-start.3 = (bf16[132,16,128]{2,1,0:T(8,128)(2,1)}, bf16[132,16,128]{2,1,0:T(8,128)(2,1)S(1)}, u32[]{:S(2)}, u32[]{:S(2)}) collective-permute-start(bf16[132,16,128]{2,1,0:T(8,128)(2,1)} %bitcast.19), channel_id=1, source_target_pairs={{0,8},{8,16},{16,24},{24,32},{32,40},{40,48},{48,56},{56,64},{64,7... | collective-permute-start | bytes 1622024 | tf_op jit(solution)/shard_map/ppermute | solution.py:222
  66.5 13.8 %collective-permute-start.1 = (bf16[132,16,128]{2,1,0:T(8,128)(2,1)}, bf16[132,16,128]{2,1,0:T(8,128)(2,1)S(1)}, u32[]{:S(2)}, u32[]{:S(2)}) collective-permute-start(bf16[132,16,128]{2,1,0:T(8,128)(2,1)} %bitcast.16), channel_id=1, source_target_pairs={{0,120},{8,0},{16,8},{24,16},{32,24},{40,32},{48,40},{56,48},{64,5... | collective-permute-start | bytes 1622024 | tf_op jit(solution)/shard_map/ppermute | solution.py:225
  68.6 35.6 %collective-permute-start.4 = (bf16[132,16,128]{2,1,0:T(8,128)(2,1)}, bf16[132,16,128]{2,1,0:T(8,128)(2,1)}, u32[]{:S(2)}, u32[]{:S(2)}) collective-permute-start(bf16[132,16,128]{2,1,0:T(8,128)(2,1)} %bitcast.19), channel_id=1, source_target_pairs={{0,120},{8,0},{16,8},{24,16},{32,24},{40,32},{48,40},{56,48},{64,5... | collective-permute-start | bytes 1622024 | tf_op jit(solution)/shard_map/ppermute | solution.py:225
  70.8 33.3 %collective-permute-start.7 = (bf16[132,16,128]{2,1,0:T(8,128)(2,1)}, bf16[132,16,128]{2,1,0:T(8,128)(2,1)}, u32[]{:S(2)}, u32[]{:S(2)}) collective-permute-start(bf16[132,16,128]{2,1,0:T(8,128)(2,1)} %bitcast.16), channel_id=1, source_target_pairs={{0,8},{8,16},{16,24},{24,32},{32,40},{40,48},{48,56},{56,64},{64,7... | collective-permute-start | bytes 1622024 | tf_op jit(solution)/shard_map/ppermute | solution.py:222
  75.5 12.7 %collective-permute-start.2 = (bf16[4,16]{1,0:T(4,128)(2,1)S(1)}, bf16[4,16]{1,0:T(4,128)(2,1)S(1)}, u32[]{:S(2)}, u32[]{:S(2)}) collective-permute-start(bf16[4,16]{1,0:T(4,128)(2,1)S(1)} %bitcast.67), channel_id=1, source_target_pairs={{0,16},{8,24},{16,32},{24,40},{32,48},{40,56},{48,64},{56,72},{64,... | collective-permute-start | bytes 392 | tf_op jit(solution)/shard_map/ppermute | solution.py:255
  88.3 15.9 %collective-permute-start.6 = (bf16[132,16,128]{2,1,0:T(8,128)(2,1)S(1)}, bf16[132,16,128]{2,1,0:T(8,128)(2,1)}, u32[]{:S(2)}, u32[]{:S(2)}) collective-permute-start(bf16[132,16,128]{2,1,0:T(8,128)(2,1)S(1)} %collective-permute-done.3.refs_6_), channel_id=1, source_target_pairs={{0,8},{8,16},{16,24},{24,32},{32,40},{40,48},{48,56},{56,64},{64,7... | collective-permute-start | bytes 1622024 | tf_op jit(solution)/shard_map/ppermute | solution.py:222
  90.2 14.0 %collective-permute-start.5 = (bf16[132,16,128]{2,1,0:T(8,128)(2,1)S(1)}, bf16[132,16,128]{2,1,0:T(8,128)(2,1)}, u32[]{:S(2)}, u32[]{:S(2)}) collective-permute-start(bf16[132,16,128]{2,1,0:T(8,128)(2,1)S(1)} %collective-permute-done.1.refs_1_), channel_id=1, source_target_pairs={{0,120},{8,0},{16,8},{24,16},{32,24},{40,32},{48,40},{56,48},{64,5... | collective-permute-start | bytes 1622024 | tf_op jit(solution)/shard_map/ppermute | solution.py:225
  95.6 8.3 %all-to-all-start.2 = ((s32[4,1,128]{2,1,0:T(1,128)}), s32[4,1,128]{2,1,0:T(1,128)S(1)}, u32[]{:S(2)}, u32[]{:S(2)}) async-start(s32[4,1,128]{2,1,0:T(1,128)} %broadcast_in_dim.59), calls=%async_computation.2 | async-start | bytes 4096 | tf_op jit(solution)/shard_map/all_to_all | solution.py:259
  116.9 18.5 %copy-start = (bf16[8,16,1024]{2,1,0:T(8,128)(2,1)}, bf16[8,16,1024]{2,1,0:T(8,128)(2,1)S(1)}, u32[]{:S(2)}) copy-start(bf16[8,16,1024]{2,1,0:T(8,128)(2,1)S(1)} %get-tuple-element.17) | copy-start | bytes 786436
  116.9 18.5 %copy-start.2 = (bf16[8,16,1024]{2,1,0:T(8,128)(2,1)}, bf16[8,16,1024]{2,1,0:T(8,128)(2,1)S(1)}, u32[]{:S(2)}) copy-start(bf16[8,16,1024]{2,1,0:T(8,128)(2,1)S(1)} %get-tuple-element.18) | copy-start | bytes 786436
  116.9 12.6 %collective-permute-start.12 = (bf16[128,16,128]{2,1,0:T(8,128)(2,1)S(1)}, bf16[128,16,128]{2,1,0:T(8,128)(2,1)S(1)}, u32[]{:S(2)}, u32[]{:S(2)}) collective-permute-start(bf16[128,16,128]{2,1,0:T(8,128)(2,1)S(1)} %get-tuple-element.24), channel_id=1, source_target_pairs={{0,8},{8,16},{16,24},{24,32},{32,40},{40,48},{48,56},{56,64},{64,7... | collective-permute-start | bytes 1572872 | tf_op jit(solution)/shard_map/ppermute | solution.py:222
  119.1 16.1 %collective-permute-start.15 = (bf16[128,16,128]{2,1,0:T(8,128)(2,1)S(1)}, bf16[128,16,128]{2,1,0:T(8,128)(2,1)S(1)}, u32[]{:S(2)}, u32[]{:S(2)}) collective-permute-start(bf16[128,16,128]{2,1,0:T(8,128)(2,1)S(1)} %get-tuple-element.28), channel_id=1, source_target_pairs={{0,120},{8,0},{16,8},{24,16},{32,24},{40,32},{48,40},{56,48},{64,5... | collective-permute-start | bytes 1572872 | tf_op jit(solution)/shard_map/ppermute | solution.py:225
  123.7 18.7 %collective-permute-start.11 = (bf16[128,16,128]{2,1,0:T(8,128)(2,1)S(1)}, bf16[128,16,128]{2,1,0:T(8,128)(2,1)S(1)}, u32[]{:S(2)}, u32[]{:S(2)}) collective-permute-start(bf16[128,16,128]{2,1,0:T(8,128)(2,1)S(1)} %get-tuple-element.22), channel_id=1, source_target_pairs={{0,120},{8,0},{16,8},{24,16},{32,24},{40,32},{48,40},{56,48},{64,5... | collective-permute-start | bytes 1572872 | tf_op jit(solution)/shard_map/ppermute | solution.py:225
  129.7 12.7 %collective-permute-start.13 = (bf16[128,16,128]{2,1,0:T(8,128)(2,1)S(1)}, bf16[128,16,128]{2,1,0:T(8,128)(2,1)S(1)}, u32[]{:S(2)}, u32[]{:S(2)}) collective-permute-start(bf16[128,16,128]{2,1,0:T(8,128)(2,1)S(1)} %add_convert_fusion.3), channel_id=1, source_target_pairs={{0,8},{8,16},{16,24},{24,32},{32,40},{40,48},{48,56},{56,64},{64,7... | collective-permute-start | bytes 1572872 | tf_op jit(solution)/shard_map/ppermute | solution.py:222
  131.6 20.7 %collective-permute-start.14 = (bf16[128,16,128]{2,1,0:T(8,128)(2,1)S(1)}, bf16[128,16,128]{2,1,0:T(8,128)(2,1)S(1)}, u32[]{:S(2)}, u32[]{:S(2)}) collective-permute-start(bf16[128,16,128]{2,1,0:T(8,128)(2,1)S(1)} %get-tuple-element.26), channel_id=1, source_target_pairs={{0,8},{8,16},{16,24},{24,32},{32,40},{40,48},{48,56},{56,64},{64,7... | collective-permute-start | bytes 1572872 | tf_op jit(solution)/shard_map/ppermute | solution.py:222
  135.4 18.2 %collective-permute-start.16 = (bf16[128,16,128]{2,1,0:T(8,128)(2,1)S(1)}, bf16[128,16,128]{2,1,0:T(8,128)(2,1)S(1)}, u32[]{:S(2)}, u32[]{:S(2)}) collective-permute-start(bf16[128,16,128]{2,1,0:T(8,128)(2,1)S(1)} %add_convert_fusion.1), channel_id=1, source_target_pairs={{0,120},{8,0},{16,8},{24,16},{32,24},{40,32},{48,40},{56,48},{64,5... | collective-permute-start | bytes 1572872 | tf_op jit(solution)/shard_map/ppermute | solution.py:225
  154.9 10.5 %copy-start.3 = (bf16[8,16,1024]{2,1,0:T(8,128)(2,1)S(1)}, bf16[8,16,1024]{2,1,0:T(8,128)(2,1)}, u32[]{:S(2)}) copy-start(bf16[8,16,1024]{2,1,0:T(8,128)(2,1)} %copy-done.2) | copy-start | bytes 786436
  154.9 13.6 %all-to-all-start.3 = ((bf16[4,8,8,16,128]{4,3,2,1,0:T(8,128)(2,1)}), bf16[4,8,8,16,128]{4,3,2,1,0:T(8,128)(2,1)S(1)}, u32[]{:S(2)}, u32[]{:S(2)}) async-start(bf16[4,8,8,16,128]{4,3,2,1,0:T(8,128)(2,1)} %bitcast.25), calls=%async_computation.3 | async-start | bytes 2097152 | tf_op jit(solution)/shard_map/all_to_all | solution.py:289
  158.6 24.1 %collective-permute-start.10 = (bf16[8,16,256]{2,1,0:T(8,128)(2,1)S(1)}, bf16[8,16,256]{2,1,0:T(8,128)(2,1)S(1)}, u32[]{:S(2)}, u32[]{:S(2)}) collective-permute-start(bf16[8,16,256]{2,1,0:T(8,128)(2,1)S(1)} %get-tuple-element.20), channel_id=1, source_target_pairs={{0,4},{4,0},{1,5},{5,1},{2,6},{6,2},{3,7},{7,3},{8,12},{12,8},{9,1... | collective-permute-start | bytes 196616 | tf_op jit(solution)/shard_map/ppermute | solution.py:298
  165.4 18.6 %copy-start.1 = (bf16[8,16,1024]{2,1,0:T(8,128)(2,1)S(1)}, bf16[8,16,1024]{2,1,0:T(8,128)(2,1)}, u32[]{:S(2)}) copy-start(bf16[8,16,1024]{2,1,0:T(8,128)(2,1)} %copy-done) | copy-start | bytes 786436
  165.4 18.6 %collective-permute-start.9 = (bf16[8,16,1024]{2,1,0:T(8,128)(2,1)S(1)}, bf16[8,16,1024]{2,1,0:T(8,128)(2,1)S(1)}, u32[]{:S(2)}, u32[]{:S(2)}) collective-permute-start(bf16[8,16,1024]{2,1,0:T(8,128)(2,1)S(1)} %copy-done.3), channel_id=1, source_target_pairs={{0,4},{4,0},{1,5},{5,1},{2,6},{6,2},{3,7},{7,3},{8,12},{12,8},{9,1... | collective-permute-start | bytes 786440 | tf_op jit(solution)/shard_map/ppermute | solution.py:297
  169.3 30.3 %all-to-all-start.4 = ((bf16[8,8,16,128]{3,2,1,0:T(8,128)(2,1)}), bf16[8,8,16,128]{3,2,1,0:T(8,128)(2,1)S(1)}, u32[]{:S(2)}, u32[]{:S(2)}) async-start(bf16[8,8,16,128]{3,2,1,0:T(8,128)(2,1)} %fusion), calls=%async_computation.4 | async-start | bytes 524288 | tf_op jit(solution)/shard_map/all_to_all | solution.py:291

commit v9 on v8

--- a/solution.py
+++ b/solution.py
@@ -158,6 +158,30 @@
     )(where, valid, *stored, mine, other)
 
 
+def heads_kernel(slot_ref, at_ref, key_ref, value_ref, out_ref):
+    lane = lax.broadcasted_iota(jnp.int32, (LP, HD), 1)
+    slot, at = slot_ref[0], at_ref[0]
+    code = jnp.where(lane == at, slot >> 4, jnp.where(lane == at + 1, slot & 15, 0))
+    code = code.astype(F32).astype(BF)
+    for to in range(2 * ZH):
+        lanes = slice(to % 2 * HD, (to % 2 + 1) * HD)
+        for i in range(P_DEV):
+            out_ref[to, 2 * i] = key_ref[i, :, lanes]
+            out_ref[to, 2 * i + 1] = value_ref[i, :, lanes]
+        out_ref[to, TILES] = code
+
+
+def heads_of(slot, at, key, value):
+    smem = pl.BlockSpec(memory_space=pltpu.SMEM)
+    vmem = pl.BlockSpec(memory_space=pltpu.VMEM)
+    return pl.pallas_call(
+        heads_kernel,
+        out_shape=jax.ShapeDtypeStruct((2 * ZH, TILES + 1, LP, HD), BF),
+        in_specs=[smem, smem, vmem, vmem],
+        out_specs=vmem,
+    )(slot, at, key, value)
+
+
 def total(*parts):
     out = parts[0].astype(F32)
     for part in parts[1:]:
@@ -190,19 +214,9 @@
         second = jnp.where(core == 0, other_part, mine_part)
         return jnp.concatenate([first, second], axis=axis)
 
-    lane = lax.broadcasted_iota(jnp.int32, (1, LP, HD), 2)
-    at = 4 * lax.axis_index("zh") + 2 * core
-    code_tile = jnp.where(lane == at, passage_slot // 16, jnp.where(lane == at + 1, passage_slot % 16, 0))
-    code_tile = code_tile.astype(BF)
-
-    def passages(c):
-        lanes = slice(c * HD, (c + 1) * HD)
-        both = jnp.stack([passage_key[:, :, lanes], passage_value[:, :, lanes]], axis=1)
-        return jnp.concatenate([both.reshape(TILES, LP, HD), code_tile], axis=0)
-
-    heads = jnp.stack([passages(0), passages(1)])
+    at = (4 * lax.axis_index("zh") + 2 * core).astype(jnp.int32).reshape(1)
     far = lax.all_to_all(
-        jnp.broadcast_to(heads[None], (ZH, 2, TILES + 1, LP, HD)).reshape(2 * ZH, TILES + 1, LP, HD),
+        heads_of(passage_slot, at, passage_key, passage_value),
         ("zh", "core"),
         split_axis=0,
         concat_axis=0,

time: 204 us -> 204 us (level)
  transfers between devices with their start and end apart: 22 -> 22, of which waited for: 12 -> 12; matrix products, arithmetic and copies ran while one was open for 4% -> 5% of each run, Pallas kernels for 0% -> 0%
where the time goes in v9:
time: 204 us; the launch traced here: 200 us
  starting transfers between devices  102 us (50%)
  waiting for transfers between devices  69 us (34%)
  Pallas kernels  14.2 us (7%)
  other arithmetic  9.02 us (4%)
  local copies, waits for them, and re-layouts  4.15 us (2%)
    ppermute x6, starting transfers between devices, up(): return lax.ppermute(part, around, ring(ZS, 1))  22.4 us
    ppermute x6, starting transfers between devices, down(): return lax.ppermute(part, around, ring(ZS, -1))  19.5 us
    all_to_all x1, starting transfers between devices, per_device(): lax.all_to_all(heads_of(passage_slot, at, passage_key, passage_value), ('...  16.6 us
    all_to_all x1, waiting for transfers between devices, per_device(): lax.all_to_all(x_sum, ('zh', 'core'), split_axis=0, concat_axis=0, tiled=...  14.9 us
    ppermute x6, waiting for transfers between devices, up(): return lax.ppermute(part, around, ring(ZS, 1))  13.9 us
    all_to_all x1, starting transfers between devices, per_device(): lax.all_to_all(x_sum, ('zh', 'core'), split_axis=0, concat_axis=0, tiled=...  13.4 us
    all_to_all x1, waiting for transfers between devices, per_device(): lax.all_to_all(heads_of(passage_slot, at, passage_key, passage_value), ('...  13.2 us
    pallas_call x1, Pallas kernels, attention(): pl.pallas_call(attention_kernel, out_shape=(tiles,) * PARTS + (query, que...  12.7 us
  transfers between devices with their start and end apart: 22, of which 12 were waited for; matrix products, arithmetic and copies ran while one was open for 5% of the time, Pallas kernels for 0%

profile of v9, /device:TPU:1, one launch (start us, length us, event | category | flops | bytes accessed | tf_op | source)
XLA Modules:
  0.0 200.3 jit_solution(2631879294391559721)
XLA Ops:
  2.9 16.6 %all-to-all-start = ((bf16[8,9,16,128]{3,2,1,0:T(8,128)(2,1)}), bf16[8,9,16,128]{3,2,1,0:T(8,128)(2,1)S(1)}, u32[]{:S(2)}, u32[]{:S(2)}) async-start(bf16[8,9,16,128]{3,2,1,0:T(8,128)(2,1)} %shard_map.128), calls=%async_computation | async-start | bytes 589824 | tf_op jit(solution)/shard_map/all_to_all | solution.py:218
  20.2 1.9 collective-permute-start
  23.2 13.2 %all-to-all-done = bf16[8,9,16,128]{3,2,1,0:T(8,128)(2,1)S(1)} async-done(((bf16[8,9,16,128]{3,2,1,0:T(8,128)(2,1)}), bf16[8,9,16,128]{3,2,1,0:T(8,128)(2,1)S(1)}, u32[]{:S(2)}, u32[]{:S(2)}) %all-to-all-start) | async-done | bytes 294944 | tf_op jit(solution)/shard_map/all_to_all | solution.py:218
  37.7 4.1 %all-to-all-start.1 = ((bf16[4,65,16,128]{3,2,1,0:T(8,128)(2,1)}), bf16[4,65,16,128]{3,2,1,0:T(8,128)(2,1)S(1)}, u32[]{:S(2)}, u32[]{:S(2)}) async-start(bf16[4,65,16,128]{3,2,1,0:T(8,128)(2,1)} %broadcast_in_dim.28), calls=%async_computation.1 | async-start | bytes 2129920 | tf_op jit(solution)/shard_map/all_to_all | solution.py:227
  42.8 4.6 %collective-permute-start.8 = (bf16[8,16,2304]{2,1,0:T(8,128)(2,1)}, bf16[8,16,2304]{2,1,0:T(8,128)(2,1)S(1)}, u32[]{:S(2)}, u32[]{:S(2)}) collective-permute-start(bf16[8,16,2304]{2,1,0:T(8,128)(2,1)} %pad_maximum_fusion.2), channel_id=1, source_target_pairs={{0,4},{4,0},{1,5},{5,1},{2,6},{6,2},{3,7},{7,3},{8,12},{12,8},{9,1... | collective-permute-start | bytes 1769480 | tf_op jit(solution)/shard_map/ppermute | solution.py:261
  47.5 6.7 %all-to-all-done.1 = bf16[4,65,16,128]{3,2,1,0:T(8,128)(2,1)S(1)} async-done(((bf16[4,65,16,128]{3,2,1,0:T(8,128)(2,1)}), bf16[4,65,16,128]{3,2,1,0:T(8,128)(2,1)S(1)}, u32[]{:S(2)}, u32[]{:S(2)}) %all-to-all-start.1) | async-done | bytes 1064992 | tf_op jit(solution)/shard_map/all_to_all | solution.py:227
  55.0 9.7 %collective-permute-start.3 = (bf16[132,16,128]{2,1,0:T(8,128)(2,1)}, bf16[132,16,128]{2,1,0:T(8,128)(2,1)S(1)}, u32[]{:S(2)}, u32[]{:S(2)}) collective-permute-start(bf16[132,16,128]{2,1,0:T(8,128)(2,1)} %bitcast.9), channel_id=1, source_target_pairs={{0,8},{8,16},{16,24},{24,32},{32,40},{40,48},{48,56},{56,64},{64,7... | collective-permute-start | bytes 1622024 | tf_op jit(solution)/shard_map/ppermute | solution.py:236
  65.7 1.9 collective-permute-start.1
  67.7 2.2 %collective-permute-start.4 = (bf16[132,16,128]{2,1,0:T(8,128)(2,1)}, bf16[132,16,128]{2,1,0:T(8,128)(2,1)}, u32[]{:S(2)}, u32[]{:S(2)}) collective-permute-start(bf16[132,16,128]{2,1,0:T(8,128)(2,1)} %bitcast.9), channel_id=1, source_target_pairs={{0,120},{8,0},{16,8},{24,16},{32,24},{40,32},{48,40},{56,48},{64,5... | collective-permute-start | bytes 1622024 | tf_op jit(solution)/shard_map/ppermute | solution.py:239
  70.0 3.1 %collective-permute-start.7 = (bf16[132,16,128]{2,1,0:T(8,128)(2,1)}, bf16[132,16,128]{2,1,0:T(8,128)(2,1)}, u32[]{:S(2)}, u32[]{:S(2)}) collective-permute-start(bf16[132,16,128]{2,1,0:T(8,128)(2,1)} %bitcast.6), channel_id=1, source_target_pairs={{0,8},{8,16},{16,24},{24,32},{32,40},{40,48},{48,56},{56,64},{64,7... | collective-permute-start | bytes 1622024 | tf_op jit(solution)/shard_map/ppermute | solution.py:236
  74.7 2.9 %collective-permute-start.2 = (bf16[4,16]{1,0:T(4,128)(2,1)S(1)}, bf16[4,16]{1,0:T(4,128)(2,1)S(1)}, u32[]{:S(2)}, u32[]{:S(2)}) collective-permute-start(bf16[4,16]{1,0:T(4,128)(2,1)S(1)} %bitcast.47), channel_id=1, source_target_pairs={{0,16},{8,24},{16,32},{24,40},{32,48},{40,56},{48,64},{56,72},{64,... | collective-permute-start | bytes 392 | tf_op jit(solution)/shard_map/ppermute | solution.py:269
  77.5 1.9 collective-permute-done.1.refs_1_
  79.4 7.9 %collective-permute-done.2 = bf16[4,16]{1,0:T(4,128)(2,1)S(1)} collective-permute-done((bf16[4,16]{1,0:T(4,128)(2,1)S(1)}, bf16[4,16]{1,0:T(4,128)(2,1)S(1)}, u32[]{:S(2)}, u32[]{:S(2)}) %collective-permute-start.2) | collective-permute-done | bytes 160 | tf_op jit(solution)/shard_map/ppermute | solution.py:269
  87.4 1.9 collective-permute-start.6
  89.4 4.6 %collective-permute-start.5 = (bf16[132,16,128]{2,1,0:T(8,128)(2,1)S(1)}, bf16[132,16,128]{2,1,0:T(8,128)(2,1)}, u32[]{:S(2)}, u32[]{:S(2)}) collective-permute-start(bf16[132,16,128]{2,1,0:T(8,128)(2,1)S(1)} %collective-permute-done.1.refs_1_), channel_id=1, source_target_pairs={{0,120},{8,0},{16,8},{24,16},{32,24},{40,32},{48,40},{56,48},{64,5... | collective-permute-start | bytes 1622024 | tf_op jit(solution)/shard_map/ppermute | solution.py:239
  94.7 4.2 %all-to-all-start.2 = ((s32[4,1,128]{2,1,0:T(1,128)}), s32[4,1,128]{2,1,0:T(1,128)S(1)}, u32[]{:S(2)}, u32[]{:S(2)}) async-start(s32[4,1,128]{2,1,0:T(1,128)} %broadcast_in_dim.29), calls=%async_computation.2 | async-start | bytes 4096 | tf_op jit(solution)/shard_map/all_to_all | solution.py:273
  99.0 4.0 %all-to-all-done.2 = s32[4,1,128]{2,1,0:T(1,128)S(1)} async-done(((s32[4,1,128]{2,1,0:T(1,128)}), s32[4,1,128]{2,1,0:T(1,128)S(1)}, u32[]{:S(2)}, u32[]{:S(2)}) %all-to-all-start.2) | async-done | bytes 2080 | tf_op jit(solution)/shard_map/all_to_all | solution.py:273
  103.3 12.7 %shard_map.129 = (bf16[128,16,128]{2,1,0:T(8,128)(2,1)S(1)}, bf16[128,16,128]{2,1,0:T(8,128)(2,1)S(1)}, bf16[128,16,128]{2,1,0:T(8,128)(2,1)S(1)}, bf16[128,16,1...) custom-call(s32[256]{0:T(256)S(1)} %fusion.13.where_ref, ...), custom_call_target="tpu_custom_call" | custom-call | flops 713031680 | bytes 12582912 | tf_op jit(solution)/shard_map/pallas_call | solution.py:143
  116.1 2.2 %collective-permute-start.12 = (bf16[128,16,128]{2,1,0:T(8,128)(2,1)S(1)}, bf16[128,16,128]{2,1,0:T(8,128)(2,1)S(1)}, u32[]{:S(2)}, u32[]{:S(2)}) collective-permute-start(bf16[128,16,128]{2,1,0:T(8,128)(2,1)S(1)} %get-tuple-element.24), channel_id=1, source_target_pairs={{0,8},{8,16},{16,24},{24,32},{32,40},{40,48},{48,56},{56,64},{64,7... | collective-permute-start | bytes 1572872 | tf_op jit(solution)/shard_map/ppermute | solution.py:236
  118.3 4.6 %collective-permute-start.15 = (bf16[128,16,128]{2,1,0:T(8,128)(2,1)S(1)}, bf16[128,16,128]{2,1,0:T(8,128)(2,1)S(1)}, u32[]{:S(2)}, u32[]{:S(2)}) collective-permute-start(bf16[128,16,128]{2,1,0:T(8,128)(2,1)S(1)} %get-tuple-element.28), channel_id=1, source_target_pairs={{0,120},{8,0},{16,8},{24,16},{32,24},{40,32},{48,40},{56,48},{64,5... | collective-permute-start | bytes 1572872 | tf_op jit(solution)/shard_map/ppermute | solution.py:239
  122.8 3.4 %collective-permute-start.11 = (bf16[128,16,128]{2,1,0:T(8,128)(2,1)S(1)}, bf16[128,16,128]{2,1,0:T(8,128)(2,1)S(1)}, u32[]{:S(2)}, u32[]{:S(2)}) collective-permute-start(bf16[128,16,128]{2,1,0:T(8,128)(2,1)S(1)} %get-tuple-element.22), channel_id=1, source_target_pairs={{0,120},{8,0},{16,8},{24,16},{32,24},{40,32},{48,40},{56,48},{64,5... | collective-permute-start | bytes 1572872 | tf_op jit(solution)/shard_map/ppermute | solution.py:239
  126.2 2.5 %collective-permute-done.12 = bf16[128,16,128]{2,1,0:T(8,128)(2,1)S(1)} collective-permute-done((bf16[128,16,128]{2,1,0:T(8,128)(2,1)S(1)}, bf16[128,16,128]{2,1,0:T(8,128)(2,1)S(1)}, u32[]{:S(2)}, u32[]{:S(2)}) %collective-permute-start.12) | collective-permute-done | bytes 524320 | tf_op jit(solution)/shard_map/ppermute | solution.py:236
  128.9 1.9 collective-permute-start.13
  130.8 3.7 %collective-permute-start.14 = (bf16[128,16,128]{2,1,0:T(8,128)(2,1)S(1)}, bf16[128,16,128]{2,1,0:T(8,128)(2,1)S(1)}, u32[]{:S(2)}, u32[]{:S(2)}) collective-permute-start(bf16[128,16,128]{2,1,0:T(8,128)(2,1)S(1)} %get-tuple-element.26), channel_id=1, source_target_pairs={{0,8},{8,16},{16,24},{24,32},{32,40},{40,48},{48,56},{56,64},{64,7... | collective-permute-start | bytes 1572872 | tf_op jit(solution)/shard_map/ppermute | solution.py:236
  134.6 2.8 %collective-permute-start.16 = (bf16[128,16,128]{2,1,0:T(8,128)(2,1)S(1)}, bf16[128,16,128]{2,1,0:T(8,128)(2,1)S(1)}, u32[]{:S(2)}, u32[]{:S(2)}) collective-permute-start(bf16[128,16,128]{2,1,0:T(8,128)(2,1)S(1)} %add_convert_fusion.1), channel_id=1, source_target_pairs={{0,120},{8,0},{16,8},{24,16},{32,24},{40,32},{48,40},{56,48},{64,5... | collective-permute-start | bytes 1572872 | tf_op jit(solution)/shard_map/ppermute | solution.py:239
  137.5 4.1 %collective-permute-done.11 = bf16[128,16,128]{2,1,0:T(8,128)(2,1)S(1)} collective-permute-done((bf16[128,16,128]{2,1,0:T(8,128)(2,1)S(1)}, bf16[128,16,128]{2,1,0:T(8,128)(2,1)S(1)}, u32[]{:S(2)}, u32[]{:S(2)}) %collective-permute-start.11) | collective-permute-done | bytes 524320 | tf_op jit(solution)/shard_map/ppermute | solution.py:239
  141.8 9.8 %collective-permute-done.14 = bf16[128,16,128]{2,1,0:T(8,128)(2,1)S(1)} collective-permute-done((bf16[128,16,128]{2,1,0:T(8,128)(2,1)S(1)}, bf16[128,16,128]{2,1,0:T(8,128)(2,1)S(1)}, u32[]{:S(2)}, u32[]{:S(2)}) %collective-permute-start.14) | collective-permute-done | bytes 524320 | tf_op jit(solution)/shard_map/ppermute | solution.py:236
  154.1 3.6 %all-to-all-start.3 = ((bf16[4,8,8,16,128]{4,3,2,1,0:T(8,128)(2,1)}), bf16[4,8,8,16,128]{4,3,2,1,0:T(8,128)(2,1)S(1)}, u32[]{:S(2)}, u32[]{:S(2)}) async-start(bf16[4,8,8,16,128]{4,3,2,1,0:T(8,128)(2,1)} %bitcast.15), calls=%async_computation.3 | async-start | bytes 2097152 | tf_op jit(solution)/shard_map/all_to_all | solution.py:303
  157.8 6.8 %collective-permute-start.10 = (bf16[8,16,256]{2,1,0:T(8,128)(2,1)S(1)}, bf16[8,16,256]{2,1,0:T(8,128)(2,1)S(1)}, u32[]{:S(2)}, u32[]{:S(2)}) collective-permute-start(bf16[8,16,256]{2,1,0:T(8,128)(2,1)S(1)} %get-tuple-element.20), channel_id=1, source_target_pairs={{0,4},{4,0},{1,5},{5,1},{2,6},{6,2},{3,7},{7,3},{8,12},{12,8},{9,1... | collective-permute-start | bytes 196616 | tf_op jit(solution)/shard_map/ppermute | solution.py:312
  164.6 2.1 %collective-permute-start.9 = (bf16[8,16,1024]{2,1,0:T(8,128)(2,1)S(1)}, bf16[8,16,1024]{2,1,0:T(8,128)(2,1)S(1)}, u32[]{:S(2)}, u32[]{:S(2)}) collective-permute-start(bf16[8,16,1024]{2,1,0:T(8,128)(2,1)S(1)} %copy-done.3), channel_id=1, source_target_pairs={{0,4},{4,0},{1,5},{5,1},{2,6},{6,2},{3,7},{7,3},{8,12},{12,8},{9,1... | collective-permute-start | bytes 786440 | tf_op jit(solution)/shard_map/ppermute | solution.py:311
  168.6 13.4 %all-to-all-start.4 = ((bf16[8,8,16,128]{3,2,1,0:T(8,128)(2,1)}), bf16[8,8,16,128]{3,2,1,0:T(8,128)(2,1)S(1)}, u32[]{:S(2)}, u32[]{:S(2)}) async-start(bf16[8,8,16,128]{3,2,1,0:T(8,128)(2,1)} %fusion), calls=%async_computation.4 | async-start | bytes 524288 | tf_op jit(solution)/shard_map/all_to_all | solution.py:305
  184.1 14.9 %all-to-all-done.4 = bf16[8,8,16,128]{3,2,1,0:T(8,128)(2,1)S(1)} async-done(((bf16[8,8,16,128]{3,2,1,0:T(8,128)(2,1)}), bf16[8,8,16,128]{3,2,1,0:T(8,128)(2,1)S(1)}, u32[]{:S(2)}, u32[]{:S(2)}) %all-to-all-start.4) | async-done | bytes 262176 | tf_op jit(solution)/shard_map/all_to_all | solution.py:305
  (77 shorter events, 18.6 us)
Async XLA Ops:
  0.6 21.5 %copy-start.4 = (bf16[8,16,2048]{2,1,0:T(8,128)(2,1)S(1)}, bf16[8,16,2048]{2,1,0:T(8,128)(2,1)}, u32[]{:S(2)}) copy-start(bf16[8,16,2048]{2,1,0:T(8,128)(2,1)} %param.14) | copy-start | bytes 1572868
  2.9 33.6 %all-to-all-start = ((bf16[8,9,16,128]{3,2,1,0:T(8,128)(2,1)}), bf16[8,9,16,128]{3,2,1,0:T(8,128)(2,1)S(1)}, u32[]{:S(2)}, u32[]{:S(2)}) async-start(bf16[8,9,16,128]{3,2,1,0:T(8,128)(2,1)} %shard_map.128), calls=%async_computation | async-start | bytes 589824 | tf_op jit(solution)/shard_map/all_to_all | solution.py:218
  20.2 47.4 %collective-permute-start = (s32[2,8,16]{2,1,0:T(8,128)S(1)}, s32[2,8,16]{2,1,0:T(8,128)S(1)}, u32[]{:S(2)}, u32[]{:S(2)}) collective-permute-start(s32[2,8,16]{2,1,0:T(8,128)S(1)} %pad_add_fusion), channel_id=1, source_target_pairs={{0,4},{4,0},{1,5},{5,1},{2,6},{6,2},{3,7},{7,3},{8,12},{12,8},{9,1... | collective-permute-start | bytes 3080 | tf_op jit(solution)/shard_map/ppermute | solution.py:263
  37.7 4.2 %copy-start.5 = (bf16[8,16,256]{2,1,0:T(8,128)(2,1)S(1)}, bf16[8,16,256]{2,1,0:T(8,128)(2,1)}, u32[]{:S(2)}) copy-start(bf16[8,16,256]{2,1,0:T(8,128)(2,1)} %param.11) | copy-start | bytes 196612
  37.7 4.2 %copy-start.6 = (bf16[8,16,256]{2,1,0:T(8,128)(2,1)S(1)}, bf16[8,16,256]{2,1,0:T(8,128)(2,1)}, u32[]{:S(2)}) copy-start(bf16[8,16,256]{2,1,0:T(8,128)(2,1)} %param.10) | copy-start | bytes 196612
  37.7 16.4 %all-to-all-start.1 = ((bf16[4,65,16,128]{3,2,1,0:T(8,128)(2,1)}), bf16[4,65,16,128]{3,2,1,0:T(8,128)(2,1)S(1)}, u32[]{:S(2)}, u32[]{:S(2)}) async-start(bf16[4,65,16,128]{3,2,1,0:T(8,128)(2,1)} %broadcast_in_dim.28), calls=%async_computation.1 | async-start | bytes 2129920 | tf_op jit(solution)/shard_map/all_to_all | solution.py:227
  42.8 60.5 %collective-permute-start.8 = (bf16[8,16,2304]{2,1,0:T(8,128)(2,1)}, bf16[8,16,2304]{2,1,0:T(8,128)(2,1)S(1)}, u32[]{:S(2)}, u32[]{:S(2)}) collective-permute-start(bf16[8,16,2304]{2,1,0:T(8,128)(2,1)} %pad_maximum_fusion.2), channel_id=1, source_target_pairs={{0,4},{4,0},{1,5},{5,1},{2,6},{6,2},{3,7},{7,3},{8,12},{12,8},{9,1... | collective-permute-start | bytes 1769480 | tf_op jit(solution)/shard_map/ppermute | solution.py:261
  55.0 19.7 %collective-permute-start.3 = (bf16[132,16,128]{2,1,0:T(8,128)(2,1)}, bf16[132,16,128]{2,1,0:T(8,128)(2,1)S(1)}, u32[]{:S(2)}, u32[]{:S(2)}) collective-permute-start(bf16[132,16,128]{2,1,0:T(8,128)(2,1)} %bitcast.9), channel_id=1, source_target_pairs={{0,8},{8,16},{16,24},{24,32},{32,40},{40,48},{48,56},{56,64},{64,7... | collective-permute-start | bytes 1622024 | tf_op jit(solution)/shard_map/ppermute | solution.py:236
  64.7 2.9 %copy-start.7 = (s32[8,16]{1,0:T(8,128)S(1)}, s32[8,16]{1,0:T(8,128)}, u32[]{:S(2)}) copy-start(s32[8,16]{1,0:T(8,128)} %param.15) | copy-start | bytes 1540
  64.7 34.2 %copy-start.8 = (s32[8,16]{1,0:T(8,128)S(1)}, s32[8,16]{1,0:T(8,128)}, u32[]{:S(2)}) copy-start(s32[8,16]{1,0:T(8,128)} %param.16) | copy-start | bytes 1540
  65.7 13.8 %collective-permute-start.1 = (bf16[132,16,128]{2,1,0:T(8,128)(2,1)}, bf16[132,16,128]{2,1,0:T(8,128)(2,1)S(1)}, u32[]{:S(2)}, u32[]{:S(2)}) collective-permute-start(bf16[132,16,128]{2,1,0:T(8,128)(2,1)} %bitcast.6), channel_id=1, source_target_pairs={{0,120},{8,0},{16,8},{24,16},{32,24},{40,32},{48,40},{56,48},{64,5... | collective-permute-start | bytes 1622024 | tf_op jit(solution)/shard_map/ppermute | solution.py:239
  67.7 35.6 %collective-permute-start.4 = (bf16[132,16,128]{2,1,0:T(8,128)(2,1)}, bf16[132,16,128]{2,1,0:T(8,128)(2,1)}, u32[]{:S(2)}, u32[]{:S(2)}) collective-permute-start(bf16[132,16,128]{2,1,0:T(8,128)(2,1)} %bitcast.9), channel_id=1, source_target_pairs={{0,120},{8,0},{16,8},{24,16},{32,24},{40,32},{48,40},{56,48},{64,5... | collective-permute-start | bytes 1622024 | tf_op jit(solution)/shard_map/ppermute | solution.py:239
  70.0 33.3 %collective-permute-start.7 = (bf16[132,16,128]{2,1,0:T(8,128)(2,1)}, bf16[132,16,128]{2,1,0:T(8,128)(2,1)}, u32[]{:S(2)}, u32[]{:S(2)}) collective-permute-start(bf16[132,16,128]{2,1,0:T(8,128)(2,1)} %bitcast.6), channel_id=1, source_target_pairs={{0,8},{8,16},{16,24},{24,32},{32,40},{40,48},{48,56},{56,64},{64,7... | collective-permute-start | bytes 1622024 | tf_op jit(solution)/shard_map/ppermute | solution.py:236
  74.7 12.7 %collective-permute-start.2 = (bf16[4,16]{1,0:T(4,128)(2,1)S(1)}, bf16[4,16]{1,0:T(4,128)(2,1)S(1)}, u32[]{:S(2)}, u32[]{:S(2)}) collective-permute-start(bf16[4,16]{1,0:T(4,128)(2,1)S(1)} %bitcast.47), channel_id=1, source_target_pairs={{0,16},{8,24},{16,32},{24,40},{32,48},{40,56},{48,64},{56,72},{64,... | collective-permute-start | bytes 392 | tf_op jit(solution)/shard_map/ppermute | solution.py:269
  87.4 15.9 %collective-permute-start.6 = (bf16[132,16,128]{2,1,0:T(8,128)(2,1)S(1)}, bf16[132,16,128]{2,1,0:T(8,128)(2,1)}, u32[]{:S(2)}, u32[]{:S(2)}) collective-permute-start(bf16[132,16,128]{2,1,0:T(8,128)(2,1)S(1)} %collective-permute-done.3.refs_6_), channel_id=1, source_target_pairs={{0,8},{8,16},{16,24},{24,32},{32,40},{40,48},{48,56},{56,64},{64,7... | collective-permute-start | bytes 1622024 | tf_op jit(solution)/shard_map/ppermute | solution.py:236
  89.4 14.0 %collective-permute-start.5 = (bf16[132,16,128]{2,1,0:T(8,128)(2,1)S(1)}, bf16[132,16,128]{2,1,0:T(8,128)(2,1)}, u32[]{:S(2)}, u32[]{:S(2)}) collective-permute-start(bf16[132,16,128]{2,1,0:T(8,128)(2,1)S(1)} %collective-permute-done.1.refs_1_), channel_id=1, source_target_pairs={{0,120},{8,0},{16,8},{24,16},{32,24},{40,32},{48,40},{56,48},{64,5... | collective-permute-start | bytes 1622024 | tf_op jit(solution)/shard_map/ppermute | solution.py:239
  94.7 8.3 %all-to-all-start.2 = ((s32[4,1,128]{2,1,0:T(1,128)}), s32[4,1,128]{2,1,0:T(1,128)S(1)}, u32[]{:S(2)}, u32[]{:S(2)}) async-start(s32[4,1,128]{2,1,0:T(1,128)} %broadcast_in_dim.29), calls=%async_computation.2 | async-start | bytes 4096 | tf_op jit(solution)/shard_map/all_to_all | solution.py:273
  116.1 18.6 %copy-start = (bf16[8,16,1024]{2,1,0:T(8,128)(2,1)}, bf16[8,16,1024]{2,1,0:T(8,128)(2,1)S(1)}, u32[]{:S(2)}) copy-start(bf16[8,16,1024]{2,1,0:T(8,128)(2,1)S(1)} %get-tuple-element.17) | copy-start | bytes 786436
  116.1 18.6 %copy-start.2 = (bf16[8,16,1024]{2,1,0:T(8,128)(2,1)}, bf16[8,16,1024]{2,1,0:T(8,128)(2,1)S(1)}, u32[]{:S(2)}) copy-start(bf16[8,16,1024]{2,1,0:T(8,128)(2,1)S(1)} %get-tuple-element.18) | copy-start | bytes 786436
  116.1 12.6 %collective-permute-start.12 = (bf16[128,16,128]{2,1,0:T(8,128)(2,1)S(1)}, bf16[128,16,128]{2,1,0:T(8,128)(2,1)S(1)}, u32[]{:S(2)}, u32[]{:S(2)}) collective-permute-start(bf16[128,16,128]{2,1,0:T(8,128)(2,1)S(1)} %get-tuple-element.24), channel_id=1, source_target_pairs={{0,8},{8,16},{16,24},{24,32},{32,40},{40,48},{48,56},{56,64},{64,7... | collective-permute-start | bytes 1572872 | tf_op jit(solution)/shard_map/ppermute | solution.py:236
  118.3 16.2 %collective-permute-start.15 = (bf16[128,16,128]{2,1,0:T(8,128)(2,1)S(1)}, bf16[128,16,128]{2,1,0:T(8,128)(2,1)S(1)}, u32[]{:S(2)}, u32[]{:S(2)}) collective-permute-start(bf16[128,16,128]{2,1,0:T(8,128)(2,1)S(1)} %get-tuple-element.28), channel_id=1, source_target_pairs={{0,120},{8,0},{16,8},{24,16},{32,24},{40,32},{48,40},{56,48},{64,5... | collective-permute-start | bytes 1572872 | tf_op jit(solution)/shard_map/ppermute | solution.py:239
  122.8 18.8 %collective-permute-start.11 = (bf16[128,16,128]{2,1,0:T(8,128)(2,1)S(1)}, bf16[128,16,128]{2,1,0:T(8,128)(2,1)S(1)}, u32[]{:S(2)}, u32[]{:S(2)}) collective-permute-start(bf16[128,16,128]{2,1,0:T(8,128)(2,1)S(1)} %get-tuple-element.22), channel_id=1, source_target_pairs={{0,120},{8,0},{16,8},{24,16},{32,24},{40,32},{48,40},{56,48},{64,5... | collective-permute-start | bytes 1572872 | tf_op jit(solution)/shard_map/ppermute | solution.py:239
  128.9 12.7 %collective-permute-start.13 = (bf16[128,16,128]{2,1,0:T(8,128)(2,1)S(1)}, bf16[128,16,128]{2,1,0:T(8,128)(2,1)S(1)}, u32[]{:S(2)}, u32[]{:S(2)}) collective-permute-start(bf16[128,16,128]{2,1,0:T(8,128)(2,1)S(1)} %add_convert_fusion.3), channel_id=1, source_target_pairs={{0,8},{8,16},{16,24},{24,32},{32,40},{40,48},{48,56},{56,64},{64,7... | collective-permute-start | bytes 1572872 | tf_op jit(solution)/shard_map/ppermute | solution.py:236
  130.8 20.8 %collective-permute-start.14 = (bf16[128,16,128]{2,1,0:T(8,128)(2,1)S(1)}, bf16[128,16,128]{2,1,0:T(8,128)(2,1)S(1)}, u32[]{:S(2)}, u32[]{:S(2)}) collective-permute-start(bf16[128,16,128]{2,1,0:T(8,128)(2,1)S(1)} %get-tuple-element.26), channel_id=1, source_target_pairs={{0,8},{8,16},{16,24},{24,32},{32,40},{40,48},{48,56},{56,64},{64,7... | collective-permute-start | bytes 1572872 | tf_op jit(solution)/shard_map/ppermute | solution.py:236
  134.6 18.2 %collective-permute-start.16 = (bf16[128,16,128]{2,1,0:T(8,128)(2,1)S(1)}, bf16[128,16,128]{2,1,0:T(8,128)(2,1)S(1)}, u32[]{:S(2)}, u32[]{:S(2)}) collective-permute-start(bf16[128,16,128]{2,1,0:T(8,128)(2,1)S(1)} %add_convert_fusion.1), channel_id=1, source_target_pairs={{0,120},{8,0},{16,8},{24,16},{32,24},{40,32},{48,40},{56,48},{64,5... | collective-permute-start | bytes 1572872 | tf_op jit(solution)/shard_map/ppermute | solution.py:239
  154.1 10.4 %copy-start.3 = (bf16[8,16,1024]{2,1,0:T(8,128)(2,1)S(1)}, bf16[8,16,1024]{2,1,0:T(8,128)(2,1)}, u32[]{:S(2)}) copy-start(bf16[8,16,1024]{2,1,0:T(8,128)(2,1)} %copy-done.2) | copy-start | bytes 786436
  154.1 13.6 %all-to-all-start.3 = ((bf16[4,8,8,16,128]{4,3,2,1,0:T(8,128)(2,1)}), bf16[4,8,8,16,128]{4,3,2,1,0:T(8,128)(2,1)S(1)}, u32[]{:S(2)}, u32[]{:S(2)}) async-start(bf16[4,8,8,16,128]{4,3,2,1,0:T(8,128)(2,1)} %bitcast.15), calls=%async_computation.3 | async-start | bytes 2097152 | tf_op jit(solution)/shard_map/all_to_all | solution.py:303
  157.8 24.1 %collective-permute-start.10 = (bf16[8,16,256]{2,1,0:T(8,128)(2,1)S(1)}, bf16[8,16,256]{2,1,0:T(8,128)(2,1)S(1)}, u32[]{:S(2)}, u32[]{:S(2)}) collective-permute-start(bf16[8,16,256]{2,1,0:T(8,128)(2,1)S(1)} %get-tuple-element.20), channel_id=1, source_target_pairs={{0,4},{4,0},{1,5},{5,1},{2,6},{6,2},{3,7},{7,3},{8,12},{12,8},{9,1... | collective-permute-start | bytes 196616 | tf_op jit(solution)/shard_map/ppermute | solution.py:312
  164.6 18.7 %copy-start.1 = (bf16[8,16,1024]{2,1,0:T(8,128)(2,1)S(1)}, bf16[8,16,1024]{2,1,0:T(8,128)(2,1)}, u32[]{:S(2)}) copy-start(bf16[8,16,1024]{2,1,0:T(8,128)(2,1)} %copy-done) | copy-start | bytes 786436
  164.6 18.6 %collective-permute-start.9 = (bf16[8,16,1024]{2,1,0:T(8,128)(2,1)S(1)}, bf16[8,16,1024]{2,1,0:T(8,128)(2,1)S(1)}, u32[]{:S(2)}, u32[]{:S(2)}) collective-permute-start(bf16[8,16,1024]{2,1,0:T(8,128)(2,1)S(1)} %copy-done.3), channel_id=1, source_target_pairs={{0,4},{4,0},{1,5},{5,1},{2,6},{6,2},{3,7},{7,3},{8,12},{12,8},{9,1... | collective-permute-start | bytes 786440 | tf_op jit(solution)/shard_map/ppermute | solution.py:311
  168.6 30.4 %all-to-all-start.4 = ((bf16[8,8,16,128]{3,2,1,0:T(8,128)(2,1)}), bf16[8,8,16,128]{3,2,1,0:T(8,128)(2,1)S(1)}, u32[]{:S(2)}, u32[]{:S(2)}) async-start(bf16[8,8,16,128]{3,2,1,0:T(8,128)(2,1)} %fusion), calls=%async_computation.4 | async-start | bytes 524288 | tf_op jit(solution)/shard_map/all_to_all | solution.py:305
